TPU v7x, 256 devices: a whole 4x4x8 slice. The times are simulated.
256 devices in a mesh: dp: 16 (over y_hi, z), tensor: 16 (over x, y_lo, core).
Axes of the slice: x: 4, y: 4 (y_hi: 2, y_lo: 2; y = y_hi * 2 + y_lo), z: 8, core: 2. Of those that a mesh axis runs over, the one named last changes fastest.
Arguments:
- out_grad: bfloat16 [8192, 2048], P('dp'), may hold values from -6 to 6
- down_weight: bfloat16 [11008, 2048], P('tensor'), may hold values from -0.125 to 0.125
- gate_pre: bfloat16 [8192, 11008], P('dp', 'tensor'), may hold values from -8 to 8
Outputs:
- factor: float32 [11008, 11008], P('dp', 'tensor')
All inputs are finite; a program needn't handle non-finite values.
Results may differ from a plain program's by a relative error of at most 0.014.
Values may be sent and summed in bfloat16 or wider, within the bound.
No kernel may reach another device: no remote copies, remote signals or barrier semaphores. Data moves between devices by JAX's collectives and lax.ppermute only.
A program may use at most 128 MiB of HBM per device.

v0:
```python
import jax
import jax.numpy as jnp
from jax import lax
from jax.sharding import PartitionSpec as P


def shards(out_grad, down_weight, gate_pre):
    hidden_grad = lax.dot_general(
        out_grad, down_weight, (((1,), (1,)), ((), ())), preferred_element_type=jnp.float32
    ).astype(jnp.bfloat16)
    up_grad = (hidden_grad.astype(jnp.float32) * jax.nn.silu(gate_pre.astype(jnp.float32))).astype(
        jnp.bfloat16
    )
    total = jnp.float32(up_grad.shape[0] * lax.axis_size("dp"))
    whole = lax.all_gather(up_grad, "tensor", axis=1, tiled=True)
    summed = lax.psum_scatter(
        lax.dot_general(
            whole, up_grad, (((0,), (0,)), ((), ())), preferred_element_type=jnp.float32
        ),
        "dp",
        scatter_dimension=0,
        tiled=True,
    )
    return summed / total


def solution(mesh):
    placed = (P("dp", None), P("tensor", None), P("dp", "tensor"))
    return jax.shard_map(
        shards, mesh=mesh, in_specs=placed, out_specs=P("dp", "tensor"), check_vma=False
    )
```

profile of v0, /device:TPU:1, one launch (start us, length us, event | category | flops | bytes accessed | tf_op | source)
XLA Modules:
  0.0 653.2 jit_solution(1773169513543820149)
XLA Ops:
  6.5 0.0 copy-start
  6.5 0.0 all-gather.2.cloned.1.call-start
  6.5 1.8 copy-done
  8.3 4.4 fusion.4
  12.7 0.0 all-gather.2.cloned.1.call-update
  12.8 0.0 reduce-scatter.2.cloned.1.call-start
  12.8 72.6 %all-gather.2.cloned.1.call-done = bf16[512,11008]{0,1:T(8,128)(2,1)} async-done(((bf16[512,688]{0,1:T(8,128)(2,1)}), bf16[512,11008]{0,1:T(8,128)(2,1)}) %all-gather.2.cloned.1.call-update) | async-done | bytes 11272208 | tf_op jit(solution)/shard_map/all_gather | solution.py:15
  85.4 18.2 %fusion.5 = f32[11008,688]{1,0:T(8,128)} fusion(bf16[512,11008]{0,1:T(8,128)(2,1)} %all-gather.2.cloned.1.call-done, bf16[512,688]{0,1:T(8,128)(2,1)} %fusion.4), kind=kOutput, calls=%fused_computation.9 | convolution fusion | flops 7755268096 | bytes 42270720 | tf_op jit(solution)/shard_map/dot_general | solution.py:17
  103.5 0.0 reduce-scatter.2.cloned.1.call-update
  103.6 539.8 %reduce-scatter.2.cloned.1.call-done = f32[688,688]{1,0:T(8,128)} async-done(((f32[11008,688]{1,0:T(8,128)}), f32[688,688]{1,0:T(8,128)}) %reduce-scatter.2.cloned.1.call-update) | async-done | bytes 1893392 | tf_op jit(solution)/shard_map/reduce_scatter | solution.py:16
  643.3 3.1 broadcast_multiply_fusion
Async XLA Ops:
  6.5 1.8 copy-start
  6.5 78.8 %all-gather.2.cloned.1.call-start = ((), (), s32[]{:S(2)}) async-start(), calls=%async_computation.1 | async-start | bytes 11976704 | tf_op jit(solution)/shard_map/all_gather | solution.py:15
  12.8 630.6 %reduce-scatter.2.cloned.1.call-start = ((), (), s32[]{:S(2)}) async-start(), calls=%async_computation.2 | async-start | bytes 35930112 | tf_op jit(solution)/shard_map/reduce_scatter | solution.py:16
Sparse Core Ops, SparseCore 0:
  12.9 72.4 all-gather.1
  103.7 539.5 reduce-scatter.1
where the time goes:
time: 655 us; the launch traced here: 653 us
  waiting for transfers between devices  612 us (93%)
  matrix products  22.6 us (3%)
  between operations  13.4 us (2%)
    reduce_scatter x1, waiting for transfers between devices, shards(): lax.psum_scatter(lax.dot_general(whole, up_grad, (((0,), (0,)), ((), ()))...  540 us
    all_gather x1, waiting for transfers between devices, shards(): whole = lax.all_gather(up_grad, 'tensor', axis=1, tiled=True)  72.6 us
    dot_general x1, matrix products, shards(): lax.dot_general(whole, up_grad, (((0,), (0,)), ((), ())), preferred_eleme...  18.2 us
  transfers between devices with their start and end apart: 2, of which 2 were waited for; matrix products, arithmetic and copies ran while one was open for 0% of the time, Pallas kernels for 0%

commit v1 on v0

v1 whole, which is shorter than its diff:
```python
import jax
import jax.numpy as jnp
from jax import lax
from jax.experimental import pallas as pl
from jax.experimental.pallas import tpu as pltpu
from jax.sharding import PartitionSpec as P

BOTH = ("dp", "tensor")
RING = 8
PLACES = (0, 4, 1, 7, 2, 6, 3, 5)


def place(offset, half):
    k = PLACES.index(offset)
    return (k // 2) * 4 + half * 2 + k % 2


def spread(turn):
    pairs = []
    for h in range(2):
        for source in range(RING):
            for b in range(2):
                for z in range(RING):
                    target = (h * RING + z) * 16 + place((source - z) % RING, b ^ turn)
                    pairs.append(((h * RING + source) * 16 + b * RING + z, target))
    return pairs


def along_z(step):
    return [(h * RING + z, h * RING + (z + step) % RING) for h in range(2) for z in range(RING)]


ACROSS = [(i, (i + RING) % 16) for i in range(16)]


def product_body(rows_ref, columns_ref, out_ref, total):
    k = pl.program_id(0)

    @pl.when(k == 0)
    def _():
        total[...] = jnp.zeros_like(total)

    for half in range(2):
        total[half] += lax.dot_general(
            rows_ref[0, half, 0], columns_ref[0], (((1,), (1,)), ((), ())),
            preferred_element_type=jnp.float32,
        )

    @pl.when(k == RING - 1)
    def _():
        out_ref[...] = total[...].astype(out_ref.dtype)


def finish_body(rows_ref, columns_ref, other_ref, out_ref, total, *, scale):
    k = pl.program_id(0)

    @pl.when(k == 0)
    def _():
        total[...] = other_ref[...].astype(jnp.float32)

    for half in range(2):
        total[half] += lax.dot_general(
            rows_ref[0, half, 0], columns_ref[0], (((1,), (1,)), ((), ())),
            preferred_element_type=jnp.float32,
        )

    @pl.when(k == RING - 1)
    def _():
        out_ref[...] = total[...] * scale


def product(rows, columns, other=None, scale=None):
    part, tokens = rows.shape[3:]
    n = columns.shape[1]
    in_specs = [
        pl.BlockSpec((1, 2, 1, part, tokens), lambda k: (k // 2, 0, k % 2, 0, 0)),
        pl.BlockSpec((1, n, tokens), lambda k: (k, 0, 0)),
    ]
    whole = pl.BlockSpec((2, part, n), lambda k: (0, 0, 0))
    args = [rows, columns]
    if other is None:
        body, kind = product_body, jnp.bfloat16
    else:
        def body(*refs):
            finish_body(*refs, scale=scale)
        kind = jnp.float32
        in_specs.append(whole)
        args.append(other)
    return pl.pallas_call(
        body,
        grid=(RING,),
        in_specs=in_specs,
        out_specs=whole,
        out_shape=jax.ShapeDtypeStruct((2, part, n), kind),
        scratch_shapes=[pltpu.VMEM((2, part, n), jnp.float32)],
        compiler_params=pltpu.CompilerParams(
            dimension_semantics=("arbitrary",), vmem_limit_bytes=32 * 1024 * 1024
        ),
        cost_estimate=pl.CostEstimate(
            flops=2 * 2 * part * n * tokens * RING, bytes_accessed=16 * 1024 * 1024, transcendentals=0
        ),
    )(*args)


def shards(out_grad, down_weight, gate_pre):
    n, tokens = down_weight.shape[0], out_grad.shape[0]
    part = n // 2
    hidden_grad = lax.dot_general(
        down_weight, out_grad, (((1,), (1,)), ((), ())), preferred_element_type=jnp.float32
    ).astype(jnp.bfloat16)
    up_grad = (hidden_grad.astype(jnp.float32) * jax.nn.silu(gate_pre.T.astype(jnp.float32))).astype(
        jnp.bfloat16
    )
    h = lax.axis_index("dp") // RING
    t = lax.axis_index("tensor")
    b, half = t // RING, (t // 2) % 2

    low, high = up_grad[:part], up_grad[part:]
    got = [
        lax.ppermute(jnp.where((b ^ turn) == 0, low, high), BOTH, spread(turn)) for turn in range(2)
    ]
    first_turn = half ^ (1 - h)
    theirs = jnp.where(first_turn == 0, got[0], got[1])
    ours = jnp.where(first_turn == 0, got[1], got[0])

    blocks = {0: up_grad}
    up, down = up_grad, up_grad
    for step in range(1, RING // 2):
        up = lax.ppermute(up, "dp", along_z(1))
        down = lax.ppermute(down, "dp", along_z(-1))
        blocks[RING - step], blocks[step] = up, down
    blocks[RING // 2] = jnp.concatenate(
        [lax.ppermute(up[:part], "dp", along_z(1)), lax.ppermute(down[part:], "dp", along_z(-1))], axis=0
    )
    columns = jnp.stack([blocks[offset] for offset in PLACES])

    rows_theirs = lax.all_gather(theirs, "tensor", axis=0).reshape(4, 2, 2, part, tokens)
    rows_ours = lax.all_gather(ours, "tensor", axis=0).reshape(4, 2, 2, part, tokens)
    sent = lax.ppermute(product(rows_theirs, columns), "dp", ACROSS)
    total = tokens * lax.axis_size("dp")
    return product(rows_ours, columns, sent, 1.0 / total).reshape(n, n)


def solution(mesh):
    placed = (P("dp", None), P("tensor", None), P("dp", "tensor"))
    return jax.shard_map(
        shards, mesh=mesh, in_specs=placed, out_specs=P("dp", "tensor"), check_vma=False
    )
```

time: 655 us -> 206 us (0.31)
  waiting for transfers between devices: 612 us -> 83.9 us
  starting transfers between devices: 0.04 us -> 61.8 us
  matrix products: 22.6 us -> 4.41 us
  Pallas kernels: 0 us -> 17.3 us
  local copies, waits for them, and re-layouts: 1.79 us -> 18 us
    reduce_scatter x1 -> x0, waiting for transfers between devices: 540 us -> none  [shards(): lax.psum_scatter(lax.dot_general(whole, up_grad, (((0,), (0,)), ((), ()))...]
    ppermute x0 -> x11, waiting for transfers between devices: none -> 76.4 us  [the longest x3 45.1 us: shards(): up = lax.ppermute(up, 'dp', along_z(1))]
    all_gather x1 -> x2, waiting for transfers between devices: 72.6 us -> 6.75 us  [the longest x1 6.75 us: shards(): lax.all_gather(ours, 'tensor', axis=0).reshape(4, 2, 2, part, tokens)]
    ppermute x0 -> x11, starting transfers between devices: none -> 61.8 us  [the longest x3 41.2 us: shards(): down = lax.ppermute(down, 'dp', along_z(-1))]
    dot_general x2 -> x1, matrix products: 22.6 us -> 4.41 us  [shards(): lax.dot_general(down_weight, out_grad, (((1,), (1,)), ((), ())), preferre...]
    pallas_call x0 -> x2, Pallas kernels: none -> 17.3 us  [product(): pl.pallas_call(body, grid=(RING,), in_specs=in_specs, out_specs=whole, ou...]
    unnamed x2 -> x15, local copies, waits for them, and re-layouts: 1.79 us -> 17 us
  transfers between devices with their start and end apart: 2 -> 13, of which waited for: 2 -> 8; matrix products, arithmetic and copies ran while one was open for 0% -> 3% of each run, Pallas kernels for 0% -> 4%
where the time goes in v1:
time: 206 us; the launch traced here: 203 us
  waiting for transfers between devices  83.9 us (41%)
  starting transfers between devices  61.8 us (30%)
  local copies, waits for them, and re-layouts  18 us (9%)
  Pallas kernels  17.3 us (8%)
  between operations  13.5 us (7%)
  matrix products  4.41 us (2%)
  other arithmetic  3.83 us (2%)
    ppermute x3, waiting for transfers between devices, shards(): up = lax.ppermute(up, 'dp', along_z(1))  45.1 us
    ppermute x3, starting transfers between devices, shards(): down = lax.ppermute(down, 'dp', along_z(-1))  41.2 us
    ppermute x1, waiting for transfers between devices, shards(): sent = lax.ppermute(product(rows_theirs, columns), 'dp', ACROSS)  19.8 us
    pallas_call x2, Pallas kernels, product(): pl.pallas_call(body, grid=(RING,), in_specs=in_specs, out_specs=whole, ou...  17.3 us
    unnamed x15, local copies, waits for them, and re-layouts  17 us
    ppermute x2, starting transfers between devices, shards(): lax.ppermute(jnp.where(b ^ turn == 0, low, high), BOTH, spread(turn))  14.2 us
    all_gather x1, waiting for transfers between devices, shards(): lax.all_gather(ours, 'tensor', axis=0).reshape(4, 2, 2, part, tokens)  6.75 us
    ppermute x1, waiting for transfers between devices, shards(): lax.ppermute(up[:part], 'dp', along_z(1))  6.14 us
  transfers between devices with their start and end apart: 13, of which 8 were waited for; matrix products, arithmetic and copies ran while one was open for 3% of the time, Pallas kernels for 4%

profile of v1, /device:TPU:1, one launch (start us, length us, event | category | flops | bytes accessed | tf_op | source)
XLA Modules:
  0.0 202.8 jit_solution(16658321597460396319)
XLA Ops:
  6.5 1.8 copy-done
  8.3 4.4 %bitcast_dynamic-update-slice_fusion.6 = (bf16[8,688,512]{2,1,0:T(8,128)(2,1)}, bf16[688,512]{1,0:T(8,128)(2,1)S(1)}) fusion(bf16[512,688]{0,1:T(8,128)(2,1)} %param.5, bf16[688,2048]{1,0:T(8,128)(2,1)S(1)} %copy-done, bf16[512,2048]{1,0:T(8,128)(2,1)} %param.3), kind=kOutput, calls=%fused_computation.16 | convolution fusion | flops 1446010880 | bytes 7028736 | tf_op jit(solution)/shard_map/dot_general | solution.py:108
  13.7 6.3 %collective-permute-start = (bf16[344,512]{1,0:T(8,128)(2,1)}, bf16[344,512]{1,0:T(8,128)(2,1)}, u32[]{:S(2)}, u32[]{:S(2)}) collective-permute-start(bf16[344,512]{1,0:T(8,128)(2,1)} %get-tuple-element.8), channel_id=1, source_target_pairs={{0,2},{1,23},{2,43},{3,63},{4,67},{5,94},{6,106},{7,118},{8,0},{9,... | collective-permute-start | bytes 1056776 | tf_op jit(solution)/shard_map/ppermute | solution.py:120
  20.0 7.9 %collective-permute-start.1 = (bf16[344,512]{1,0:T(8,128)(2,1)}, bf16[344,512]{1,0:T(8,128)(2,1)}, u32[]{:S(2)}, u32[]{:S(2)}) collective-permute-start(bf16[344,512]{1,0:T(8,128)(2,1)} %get-tuple-element.7), channel_id=1, source_target_pairs={{0,0},{1,21},{2,41},{3,61},{4,65},{5,92},{6,104},{7,116},{8,2},{9,... | collective-permute-start | bytes 1056776 | tf_op jit(solution)/shard_map/ppermute | solution.py:120
  27.9 4.4 %collective-permute-done = bf16[344,512]{1,0:T(8,128)(2,1)} collective-permute-done((bf16[344,512]{1,0:T(8,128)(2,1)}, bf16[344,512]{1,0:T(8,128)(2,1)}, u32[]{:S(2)}, u32[]{:S(2)}) %collective-permute-start) | collective-permute-done | bytes 352288 | tf_op jit(solution)/shard_map/ppermute | solution.py:120
  33.3 2.0 broadcast_select_fusion.2
  36.7 35.1 %collective-permute-start.6 = (bf16[688,512]{1,0:T(8,128)(2,1)S(1)}, bf16[688,512]{1,0:T(8,128)(2,1)S(1)}, u32[]{:S(2)}, u32[]{:S(2)}) collective-permute-start(bf16[688,512]{1,0:T(8,128)(2,1)S(1)} %get-tuple-element.10), channel_id=1, source_target_pairs={{0,112},{16,0},{32,16},{48,32},{64,48},{80,64},{96,80},{112,96},{1... | collective-permute-start | bytes 2113544 | tf_op jit(solution)/shard_map/ppermute | solution.py:130
  71.9 15.5 %collective-permute-done.2 = bf16[688,512]{1,0:T(8,128)(2,1)S(1)} collective-permute-done((bf16[688,512]{1,0:T(8,128)(2,1)S(1)}, bf16[688,512]{1,0:T(8,128)(2,1)S(1)}, u32[]{:S(2)}, u32[]{:S(2)}) %collective-permute-start.2) | collective-permute-done | bytes 704544 | tf_op jit(solution)/shard_map/ppermute | solution.py:129
  87.3 3.1 %collective-permute-start.7 = (bf16[688,512]{1,0:T(8,128)(2,1)S(1)}, bf16[688,512]{1,0:T(8,128)(2,1)S(1)}, u32[]{:S(2)}, u32[]{:S(2)}) collective-permute-start(bf16[688,512]{1,0:T(8,128)(2,1)S(1)} %collective-permute-done.6), channel_id=1, source_target_pairs={{0,112},{16,0},{32,16},{48,32},{64,48},{80,64},{96,80},{112,96},{1... | collective-permute-start | bytes 2113544 | tf_op jit(solution)/shard_map/ppermute | solution.py:130
  90.4 15.2 %collective-permute-done.3 = bf16[688,512]{1,0:T(8,128)(2,1)S(1)} collective-permute-done((bf16[688,512]{1,0:T(8,128)(2,1)S(1)}, bf16[688,512]{1,0:T(8,128)(2,1)S(1)}, u32[]{:S(2)}, u32[]{:S(2)}) %collective-permute-start.3) | collective-permute-done | bytes 704544 | tf_op jit(solution)/shard_map/ppermute | solution.py:129
  105.7 3.0 %collective-permute-start.8 = (bf16[688,512]{1,0:T(8,128)(2,1)S(1)}, bf16[688,512]{1,0:T(8,128)(2,1)S(1)}, u32[]{:S(2)}, u32[]{:S(2)}) collective-permute-start(bf16[688,512]{1,0:T(8,128)(2,1)S(1)} %collective-permute-done.7), channel_id=1, source_target_pairs={{0,112},{16,0},{32,16},{48,32},{64,48},{80,64},{96,80},{112,96},{1... | collective-permute-start | bytes 2113544 | tf_op jit(solution)/shard_map/ppermute | solution.py:130
  108.6 14.5 %collective-permute-done.4 = bf16[688,512]{1,0:T(8,128)(2,1)S(1)} collective-permute-done((bf16[688,512]{1,0:T(8,128)(2,1)S(1)}, bf16[688,512]{1,0:T(8,128)(2,1)S(1)}, u32[]{:S(2)}, u32[]{:S(2)}) %collective-permute-start.4) | collective-permute-done | bytes 704544 | tf_op jit(solution)/shard_map/ppermute | solution.py:129
  123.2 2.8 %collective-permute-start.9 = (bf16[344,512]{1,0:T(8,128)(2,1)S(1)}, bf16[344,512]{1,0:T(8,128)(2,1)S(1)}, u32[]{:S(2)}, u32[]{:S(2)}) collective-permute-start(bf16[344,512]{1,0:T(8,128)(2,1)S(1)} %slice.19), channel_id=1, source_target_pairs={{0,112},{16,0},{32,16},{48,32},{64,48},{80,64},{96,80},{112,96},{1... | collective-permute-start | bytes 1056776 | tf_op jit(solution)/shard_map/ppermute | solution.py:133
  126.0 6.1 %collective-permute-done.5 = bf16[344,512]{1,0:T(8,128)(2,1)S(1)} collective-permute-done((bf16[344,512]{1,0:T(8,128)(2,1)S(1)}, bf16[344,512]{1,0:T(8,128)(2,1)S(1)}, u32[]{:S(2)}, u32[]{:S(2)}) %collective-permute-start.5) | collective-permute-done | bytes 352288 | tf_op jit(solution)/shard_map/ppermute | solution.py:133
  133.1 1.0 bitcast_dynamic-update-slice_fusion.5
  138.6 2.7 %copy-done.1 = bf16[8,688,512]{2,1,0:T(8,128)(2,1)S(1)} copy-done((bf16[8,688,512]{2,1,0:T(8,128)(2,1)S(1)}, bf16[8,688,512]{2,1,0:T(8,128)(2,1)}, u32[]{:S(2)}) %copy-start.1) | copy-done | bytes 5636120
  141.3 2.7 %copy-done.4 = bf16[5504,512]{1,0:T(8,128)(2,1)S(1)} copy-done((bf16[5504,512]{1,0:T(8,128)(2,1)S(1)}, bf16[5504,512]{1,0:T(8,128)(2,1)}, u32[]{:S(2)}) %copy-start.4) | copy-done | bytes 5636120
  144.0 7.9 %shard_map.37 = bf16[2,344,688]{2,1,0:T(8,128)(2,1)} custom-call(bf16[4,2,2,344,512]{4,3,2,1,0:T(8,128)(2,1)S(1)} %bitcast.39, bf16[8,688,512]{2,1,0:T(8,128)(2,1)S(1)} %copy-done.1), custom_call_target="tpu_custom_call" | custom-call | flops 3877634048 | bytes 16777216 | tf_op jit(solution)/shard_map/pallas_call | solution.py:89
  151.9 2.9 %collective-permute-start.10 = (bf16[2,344,688]{2,1,0:T(8,128)(2,1)}, bf16[2,344,688]{2,1,0:T(8,128)(2,1)}, u32[]{:S(2)}, u32[]{:S(2)}) collective-permute-start(bf16[2,344,688]{2,1,0:T(8,128)(2,1)} %shard_map.37), channel_id=1, source_target_pairs={{0,128},{16,144},{32,160},{48,176},{64,192},{80,208},{96,224},{112... | collective-permute-start | bytes 2840072 | tf_op jit(solution)/shard_map/ppermute | solution.py:139
  154.8 6.7 %all-gather.5.cloned.1.call-done = bf16[5504,512]{1,0:T(8,128)(2,1)} async-done(((bf16[344,512]{1,0:T(8,128)(2,1)}), bf16[5504,512]{1,0:T(8,128)(2,1)}) %all-gather.5.cloned.1.call-update) | async-done | bytes 5636112 | tf_op jit(solution)/shard_map/all_gather | solution.py:138
  161.5 19.8 %collective-permute-done.10.refs_2_ = bf16[2,344,688]{2,1,0:T(8,128)(2,1)} collective-permute-done((bf16[2,344,688]{2,1,0:T(8,128)(2,1)}, bf16[2,344,688]{2,1,0:T(8,128)(2,1)}, u32[]{:S(2)}, u32[]{:S(2)}) %collective-permute-start.10) | collective-permute-done | bytes 946720 | tf_op jit(solution)/shard_map/ppermute | solution.py:139
  181.3 2.6 %copy-done.2 = bf16[8,688,512]{2,1,0:T(8,128)(2,1)S(1)} copy-done((bf16[8,688,512]{2,1,0:T(8,128)(2,1)S(1)}, bf16[8,688,512]{2,1,0:T(8,128)(2,1)}, u32[]{:S(2)}) %copy-start.2) | copy-done | bytes 5636120
  183.9 2.6 %copy-done.3 = bf16[5504,512]{1,0:T(8,128)(2,1)S(1)} copy-done((bf16[5504,512]{1,0:T(8,128)(2,1)S(1)}, bf16[5504,512]{1,0:T(8,128)(2,1)}, u32[]{:S(2)}) %copy-start.3) | copy-done | bytes 5636120
  186.5 9.4 %shard_map.38 = f32[2,344,688]{2,1,0:T(8,128)} custom-call(bf16[4,2,2,344,512]{4,3,2,1,0:T(8,128)(2,1)S(1)} %bitcast.38, bf16[8,688,512]{2,1,0:T(8,128)(2,1)S(1)} %copy-done.2, bf16[2,344,688]{2,1,0:T(8,128)(2,1)} %collective-permute-done.10.refs_2_), custom_call_target="tpu_custom_call" | custom-call | flops 3877634048 | bytes 16777216 | tf_op jit(solution)/shard_map/pallas_call | solution.py:89
  (28 shorter events, 9.0 us)
Async XLA Ops:
  6.5 1.8 copy-start
  6.5 132.1 %all-gather.7.cloned.1.call-start = ((), (), s32[]{:S(2)}) async-start(), calls=%async_computation.1 | async-start | bytes 5988352 | tf_op jit(solution)/shard_map/all_gather | solution.py:137
  13.7 18.7 %collective-permute-start = (bf16[344,512]{1,0:T(8,128)(2,1)}, bf16[344,512]{1,0:T(8,128)(2,1)}, u32[]{:S(2)}, u32[]{:S(2)}) collective-permute-start(bf16[344,512]{1,0:T(8,128)(2,1)} %get-tuple-element.8), channel_id=1, source_target_pairs={{0,2},{1,23},{2,43},{3,63},{4,67},{5,94},{6,106},{7,118},{8,0},{9,... | collective-permute-start | bytes 1056776 | tf_op jit(solution)/shard_map/ppermute | solution.py:120
  20.0 13.3 %collective-permute-start.1 = (bf16[344,512]{1,0:T(8,128)(2,1)}, bf16[344,512]{1,0:T(8,128)(2,1)}, u32[]{:S(2)}, u32[]{:S(2)}) collective-permute-start(bf16[344,512]{1,0:T(8,128)(2,1)} %get-tuple-element.7), channel_id=1, source_target_pairs={{0,0},{1,21},{2,41},{3,61},{4,65},{5,92},{6,104},{7,116},{8,2},{9,... | collective-permute-start | bytes 1056776 | tf_op jit(solution)/shard_map/ppermute | solution.py:120
  35.3 126.3 %all-gather.5.cloned.1.call-start = ((), (), s32[]{:S(2)}) async-start(), calls=%async_computation | async-start | bytes 5988352 | tf_op jit(solution)/shard_map/all_gather | solution.py:138
  36.0 51.3 %collective-permute-start.2 = (bf16[688,512]{1,0:T(8,128)(2,1)S(1)}, bf16[688,512]{1,0:T(8,128)(2,1)S(1)}, u32[]{:S(2)}, u32[]{:S(2)}) collective-permute-start(bf16[688,512]{1,0:T(8,128)(2,1)S(1)} %get-tuple-element.10), channel_id=1, source_target_pairs={{0,16},{16,32},{32,48},{48,64},{64,80},{80,96},{96,112},{112,0},{1... | collective-permute-start | bytes 2113544 | tf_op jit(solution)/shard_map/ppermute | solution.py:129
  36.7 50.6 %collective-permute-start.6 = (bf16[688,512]{1,0:T(8,128)(2,1)S(1)}, bf16[688,512]{1,0:T(8,128)(2,1)S(1)}, u32[]{:S(2)}, u32[]{:S(2)}) collective-permute-start(bf16[688,512]{1,0:T(8,128)(2,1)S(1)} %get-tuple-element.10), channel_id=1, source_target_pairs={{0,112},{16,0},{32,16},{48,32},{64,48},{80,64},{96,80},{112,96},{1... | collective-permute-start | bytes 2113544 | tf_op jit(solution)/shard_map/ppermute | solution.py:130
  87.3 18.3 %collective-permute-start.3 = (bf16[688,512]{1,0:T(8,128)(2,1)S(1)}, bf16[688,512]{1,0:T(8,128)(2,1)S(1)}, u32[]{:S(2)}, u32[]{:S(2)}) collective-permute-start(bf16[688,512]{1,0:T(8,128)(2,1)S(1)} %collective-permute-done.2), channel_id=1, source_target_pairs={{0,16},{16,32},{32,48},{48,64},{64,80},{80,96},{96,112},{112,0},{1... | collective-permute-start | bytes 2113544 | tf_op jit(solution)/shard_map/ppermute | solution.py:129
  87.3 18.3 %collective-permute-start.7 = (bf16[688,512]{1,0:T(8,128)(2,1)S(1)}, bf16[688,512]{1,0:T(8,128)(2,1)S(1)}, u32[]{:S(2)}, u32[]{:S(2)}) collective-permute-start(bf16[688,512]{1,0:T(8,128)(2,1)S(1)} %collective-permute-done.6), channel_id=1, source_target_pairs={{0,112},{16,0},{32,16},{48,32},{64,48},{80,64},{96,80},{112,96},{1... | collective-permute-start | bytes 2113544 | tf_op jit(solution)/shard_map/ppermute | solution.py:130
  105.7 17.4 %collective-permute-start.4 = (bf16[688,512]{1,0:T(8,128)(2,1)S(1)}, bf16[688,512]{1,0:T(8,128)(2,1)S(1)}, u32[]{:S(2)}, u32[]{:S(2)}) collective-permute-start(bf16[688,512]{1,0:T(8,128)(2,1)S(1)} %collective-permute-done.3), channel_id=1, source_target_pairs={{0,16},{16,32},{32,48},{48,64},{64,80},{80,96},{96,112},{112,0},{1... | collective-permute-start | bytes 2113544 | tf_op jit(solution)/shard_map/ppermute | solution.py:129
  105.7 17.5 %collective-permute-start.8 = (bf16[688,512]{1,0:T(8,128)(2,1)S(1)}, bf16[688,512]{1,0:T(8,128)(2,1)S(1)}, u32[]{:S(2)}, u32[]{:S(2)}) collective-permute-start(bf16[688,512]{1,0:T(8,128)(2,1)S(1)} %collective-permute-done.7), channel_id=1, source_target_pairs={{0,112},{16,0},{32,16},{48,32},{64,48},{80,64},{96,80},{112,96},{1... | collective-permute-start | bytes 2113544 | tf_op jit(solution)/shard_map/ppermute | solution.py:130
  123.1 9.0 %collective-permute-start.5 = (bf16[344,512]{1,0:T(8,128)(2,1)S(1)}, bf16[344,512]{1,0:T(8,128)(2,1)S(1)}, u32[]{:S(2)}, u32[]{:S(2)}) collective-permute-start(bf16[344,512]{1,0:T(8,128)(2,1)S(1)} %slice.18), channel_id=1, source_target_pairs={{0,16},{16,32},{32,48},{48,64},{64,80},{80,96},{96,112},{112,0},{1... | collective-permute-start | bytes 1056776 | tf_op jit(solution)/shard_map/ppermute | solution.py:133
  123.2 8.9 %collective-permute-start.9 = (bf16[344,512]{1,0:T(8,128)(2,1)S(1)}, bf16[344,512]{1,0:T(8,128)(2,1)S(1)}, u32[]{:S(2)}, u32[]{:S(2)}) collective-permute-start(bf16[344,512]{1,0:T(8,128)(2,1)S(1)} %slice.19), channel_id=1, source_target_pairs={{0,112},{16,0},{32,16},{48,32},{64,48},{80,64},{96,80},{112,96},{1... | collective-permute-start | bytes 1056776 | tf_op jit(solution)/shard_map/ppermute | solution.py:133
  138.6 2.7 %copy-start.1 = (bf16[8,688,512]{2,1,0:T(8,128)(2,1)S(1)}, bf16[8,688,512]{2,1,0:T(8,128)(2,1)}, u32[]{:S(2)}) copy-start(bf16[8,688,512]{2,1,0:T(8,128)(2,1)} %bitcast_dynamic-update-slice_fusion.columns_ref.refs_1_) | copy-start | bytes 16908292
  141.3 2.7 %copy-start.4 = (bf16[5504,512]{1,0:T(8,128)(2,1)S(1)}, bf16[5504,512]{1,0:T(8,128)(2,1)}, u32[]{:S(2)}) copy-start(bf16[5504,512]{1,0:T(8,128)(2,1)} %all-gather.7.cloned.1.call-done) | copy-start | bytes 16908292
  151.9 29.4 %collective-permute-start.10 = (bf16[2,344,688]{2,1,0:T(8,128)(2,1)}, bf16[2,344,688]{2,1,0:T(8,128)(2,1)}, u32[]{:S(2)}, u32[]{:S(2)}) collective-permute-start(bf16[2,344,688]{2,1,0:T(8,128)(2,1)} %shard_map.37), channel_id=1, source_target_pairs={{0,128},{16,144},{32,160},{48,176},{64,192},{80,208},{96,224},{112... | collective-permute-start | bytes 2840072 | tf_op jit(solution)/shard_map/ppermute | solution.py:139
  181.3 2.6 %copy-start.2 = (bf16[8,688,512]{2,1,0:T(8,128)(2,1)S(1)}, bf16[8,688,512]{2,1,0:T(8,128)(2,1)}, u32[]{:S(2)}) copy-start(bf16[8,688,512]{2,1,0:T(8,128)(2,1)} %bitcast_dynamic-update-slice_fusion.columns_ref.refs_1_) | copy-start | bytes 16908292
  183.9 2.6 %copy-start.3 = (bf16[5504,512]{1,0:T(8,128)(2,1)S(1)}, bf16[5504,512]{1,0:T(8,128)(2,1)}, u32[]{:S(2)}) copy-start(bf16[5504,512]{1,0:T(8,128)(2,1)} %all-gather.5.cloned.1.call-done) | copy-start | bytes 16908292
Sparse Core Ops, SparseCore 0:
  35.4 80.4 all-gather.6
  117.7 43.7 all-gather.4

commit v2 on v1

v2 whole, which is shorter than its diff:
```python
import functools

import jax
import jax.numpy as jnp
from jax import lax
from jax.experimental import pallas as pl
from jax.experimental.pallas import tpu as pltpu
from jax.sharding import PartitionSpec as P

BOTH = ("dp", "tensor")
RING = 8
PLACES = (0, 4, 1, 7, 2, 6, 3, 5)


def place(offset, half):
    k = PLACES.index(offset)
    return (k // 2) * 4 + half * 2 + k % 2


def in_plane(turn):
    pairs = []
    for h in range(2):
        for source in range(RING):
            for b in range(2):
                for z in range(RING):
                    plane = (h * RING + source) * 16
                    pairs.append((plane + b * RING + z, plane + place((source - z) % RING, b ^ turn)))
    return pairs


def shifted():
    pairs = []
    for h in range(2):
        for z in range(RING):
            for offset in range(RING):
                for half in range(2):
                    t = place(offset, half)
                    pairs.append(((h * RING + (z + offset) % RING) * 16 + t, (h * RING + z) * 16 + t))
    return pairs


def along_z(step):
    return [(h * RING + z, h * RING + (z + step) % RING) for h in range(2) for z in range(RING)]


ACROSS = [(i, (i + RING) % 16) for i in range(16)]


def product_body(rows_ref, columns_ref, *refs, steps, scale):
    out_ref, total = refs[-2:]
    k = pl.program_id(0)
    pair = columns_ref.shape[0]

    def partial(half):
        return sum(
            lax.dot_general(
                rows_ref[0, half, i], columns_ref[i], (((1,), (1,)), ((), ())),
                preferred_element_type=jnp.float32,
            )
            for i in range(pair)
        )

    @pl.when(k == 0)
    def _():
        for half in range(2):
            total[half] = partial(half)

    @pl.when((k > 0) & (k < steps - 1))
    def _():
        for half in range(2):
            total[half] += partial(half)

    @pl.when(k == steps - 1)
    def _():
        for half in range(2):
            whole = total[half] + partial(half)
            if scale is not None:
                whole = (whole + refs[0][half].astype(jnp.float32)) * scale
            out_ref[half] = whole.astype(out_ref.dtype)


def product(rows, columns, other=None, scale=None):
    steps, part, tokens = rows.shape[0], *rows.shape[3:]
    n = columns.shape[1]
    in_specs = [
        pl.BlockSpec((1, 2, 2, part, tokens), lambda k: (k, 0, 0, 0, 0)),
        pl.BlockSpec((2, n, tokens), lambda k: (k, 0, 0)),
    ]
    whole = pl.BlockSpec((2, part, n), lambda k: (0, 0, 0))
    args = [rows, columns]
    if other is not None:
        in_specs.append(whole)
        args.append(other)
    return pl.pallas_call(
        functools.partial(product_body, steps=steps, scale=scale),
        grid=(steps,),
        in_specs=in_specs,
        out_specs=whole,
        out_shape=jax.ShapeDtypeStruct((2, part, n), jnp.bfloat16 if other is None else jnp.float32),
        scratch_shapes=[pltpu.VMEM((2, part, n), jnp.float32)],
        compiler_params=pltpu.CompilerParams(
            dimension_semantics=("arbitrary",), vmem_limit_bytes=56 * 1024 * 1024
        ),
        cost_estimate=pl.CostEstimate(
            flops=2 * 2 * part * n * tokens * RING, bytes_accessed=16 * 1024 * 1024, transcendentals=0
        ),
    )(*args)


def put(columns, block, offset, start=0):
    return lax.dynamic_update_slice(columns, block[None], (PLACES.index(offset), start, 0))


def shards(out_grad, down_weight, gate_pre):
    n, tokens = down_weight.shape[0], out_grad.shape[0]
    part = n // 2
    hidden_grad = lax.dot_general(
        down_weight, out_grad, (((1,), (1,)), ((), ())), preferred_element_type=jnp.float32
    ).astype(jnp.bfloat16)
    up_grad = (hidden_grad.astype(jnp.float32) * jax.nn.silu(gate_pre.T.astype(jnp.float32))).astype(
        jnp.bfloat16
    )
    h = lax.axis_index("dp") // RING
    t = lax.axis_index("tensor")
    b, half = t // RING, (t // 2) % 2

    low, high = up_grad[:part], up_grad[part:]
    got = [
        lax.ppermute(jnp.where((b ^ turn) == 0, low, high), BOTH, in_plane(turn)) for turn in range(2)
    ]
    up, down = lax.ppermute(up_grad, "dp", along_z(1)), lax.ppermute(up_grad, "dp", along_z(-1))
    got[0], got[1], up, down, up_grad = lax.optimization_barrier((got[0], got[1], up, down, up_grad))

    first_turn = half ^ (1 - h)
    theirs = jnp.where(first_turn == 0, got[0], got[1])
    ours = jnp.where(first_turn == 0, got[1], got[0])
    theirs = lax.ppermute(theirs, BOTH, shifted())
    columns = jnp.broadcast_to(up_grad[None], (RING, n, tokens))
    columns = put(put(columns, up, RING - 1), down, 1)
    theirs, up, down, ours, columns = lax.optimization_barrier((theirs, up, down, ours, columns))
    rows_theirs = lax.all_gather(theirs, "tensor", axis=0).reshape(4, 2, 2, part, tokens)

    up, down = lax.ppermute(up, "dp", along_z(1)), lax.ppermute(down, "dp", along_z(-1))
    ours = lax.ppermute(ours, BOTH, shifted())
    up, down, ours, columns = lax.optimization_barrier((up, down, ours, columns))
    rows_ours = lax.all_gather(ours, "tensor", axis=0).reshape(4, 2, 2, part, tokens)

    columns = put(put(columns, up, RING - 2), down, 2)
    up, down = lax.ppermute(up, "dp", along_z(1)), lax.ppermute(down, "dp", along_z(-1))
    up, down, columns = lax.optimization_barrier((up, down, columns))

    columns = put(put(columns, up, RING - 3), down, 3)
    up = lax.ppermute(up[:part], "dp", along_z(1))
    down = lax.ppermute(down[part:], "dp", along_z(-1))
    up, down, columns = lax.optimization_barrier((up, down, columns))
    columns = put(put(columns, up, RING // 2), down, RING // 2, part)
    sent = lax.ppermute(product(rows_theirs, columns), "dp", ACROSS)
    total = tokens * lax.axis_size("dp")
    return product(rows_ours, columns, sent, 1.0 / total).reshape(n, n)


def solution(mesh):
    placed = (P("dp", None), P("tensor", None), P("dp", "tensor"))
    return jax.shard_map(
        shards, mesh=mesh, in_specs=placed, out_specs=P("dp", "tensor"), check_vma=False
    )
```

time: 206 us -> 184 us (0.89); the launches traced: 203 us -> 183 us
  starting transfers between devices: 61.8 us -> 35.9 us
  waiting for transfers between devices: 83.9 us -> 94.2 us
  local copies, waits for them, and re-layouts: 18 us -> 15.2 us
    all_gather x1, waiting for transfers between devices: 6.75 us -> 45.6 us  [shards(): lax.all_gather(ours, 'tensor', axis=0).reshape(4, 2, 2, part, tokens)]
    ppermute x10 -> x12, starting transfers between devices: 58.9 us -> 34.6 us  [the longest x1 7.82 us: shards(): ours = lax.ppermute(ours, BOTH, shifted())]
    ppermute x1, waiting for transfers between devices: 19.8 us -> 0.01 us  [shards(): sent = lax.ppermute(product(rows_theirs, columns), 'dp', ACROSS)]
    unnamed x15 -> x2, local copies, waits for them, and re-layouts: 17 us -> 1.79 us
    dynamic_update_slice x0 -> x8, local copies, waits for them, and re-layouts: none -> 10.4 us  [put(): lax.dynamic_update_slice(columns, block[None], (PLACES.index(offset), sta...]
    ppermute x10 -> x12, waiting for transfers between devices: 56.6 us -> 48.5 us  [the longest x2 15.5 us: shards(): lax.ppermute(jnp.where(b ^ turn == 0, low, high), BOTH, in_plane(turn))]
    broadcast_in_dim x0 -> x1, local copies, waits for them, and re-layouts: none -> 2.89 us  [shards(): columns = jnp.broadcast_to(up_grad[None], (RING, n, tokens))]
  transfers between devices with their start and end apart: 13 -> 15, of which waited for: 8 -> 9; matrix products, arithmetic and copies ran while one was open for 3% -> 8% of each run, Pallas kernels for 4% -> 5%
where the time goes in v2:
time: 184 us; the launch traced here: 183 us
  waiting for transfers between devices  94.2 us (51%)
  starting transfers between devices  35.9 us (20%)
  Pallas kernels  17.9 us (10%)
  local copies, waits for them, and re-layouts  15.2 us (8%)
  between operations  13.5 us (7%)
  matrix products  3.55 us (2%)
  other arithmetic  2.77 us (2%)
    all_gather x1, waiting for transfers between devices, shards(): lax.all_gather(ours, 'tensor', axis=0).reshape(4, 2, 2, part, tokens)  45.6 us
    pallas_call x2, Pallas kernels, product(): pl.pallas_call(functools.partial(product_body, steps=steps, scale=scale),...  17.9 us
    ppermute x2, waiting for transfers between devices, shards(): lax.ppermute(jnp.where(b ^ turn == 0, low, high), BOTH, in_plane(turn))  15.5 us
    ppermute x1, waiting for transfers between devices, shards(): ours = lax.ppermute(ours, BOTH, shifted())  15.3 us
    dynamic_update_slice x8, local copies, waits for them, and re-layouts, put(): lax.dynamic_update_slice(columns, block[None], (PLACES.index(offset), sta...  10.4 us
    ppermute x2, waiting for transfers between devices, shards(): lax.ppermute(up, 'dp', along_z(1))  8.88 us
    ppermute x1, starting transfers between devices, shards(): ours = lax.ppermute(ours, BOTH, shifted())  7.82 us
    ppermute x2, starting transfers between devices, shards(): lax.ppermute(jnp.where(b ^ turn == 0, low, high), BOTH, in_plane(turn))  7.04 us
  transfers between devices with their start and end apart: 15, of which 9 were waited for; matrix products, arithmetic and copies ran while one was open for 8% of the time, Pallas kernels for 5%

profile of v2, /device:TPU:1, one launch (start us, length us, event | category | flops | bytes accessed | tf_op | source)
XLA Modules:
  0.0 182.9 jit_solution(55190011170543801)
XLA Ops:
  8.3 3.6 %fusion.4 = bf16[688,512]{1,0:T(8,128)(2,1)S(1)} fusion(bf16[512,688]{0,1:T(8,128)(2,1)} %param.5, bf16[688,2048]{1,0:T(8,128)(2,1)S(1)} %copy-done, bf16[512,2048]{1,0:T(8,128)(2,1)} %param.3), kind=kOutput, calls=%fused_computation.6 | convolution fusion | flops 1446010880 | bytes 6324224 | tf_op jit(solution)/shard_map/dot_general | solution.py:117
  11.9 2.5 %collective-permute-start.2 = (bf16[688,512]{1,0:T(8,128)(2,1)S(1)}, bf16[688,512]{1,0:T(8,128)(2,1)}, u32[]{:S(2)}, u32[]{:S(2)}) collective-permute-start(bf16[688,512]{1,0:T(8,128)(2,1)S(1)} %fusion.4), channel_id=1, source_target_pairs={{0,16},{16,32},{32,48},{48,64},{64,80},{80,96},{96,112},{112,0},{1... | collective-permute-start | bytes 2113544 | tf_op jit(solution)/shard_map/ppermute | solution.py:131
  14.4 4.0 %collective-permute-start.3 = (bf16[688,512]{1,0:T(8,128)(2,1)S(1)}, bf16[688,512]{1,0:T(8,128)(2,1)}, u32[]{:S(2)}, u32[]{:S(2)}) collective-permute-start(bf16[688,512]{1,0:T(8,128)(2,1)S(1)} %fusion.4), channel_id=1, source_target_pairs={{0,112},{16,0},{32,16},{48,32},{64,48},{80,64},{96,80},{112,96},{1... | collective-permute-start | bytes 2113544 | tf_op jit(solution)/shard_map/ppermute | solution.py:131
  19.4 3.1 %collective-permute-start = (bf16[344,512]{1,0:T(8,128)(2,1)}, bf16[344,512]{1,0:T(8,128)(2,1)}, u32[]{:S(2)}, u32[]{:S(2)}) collective-permute-start(bf16[344,512]{1,0:T(8,128)(2,1)} %get-tuple-element.48), channel_id=1, source_target_pairs={{0,0},{1,5},{2,9},{3,13},{4,1},{5,12},{6,8},{7,4},{8,2},{9,7},{10,... | collective-permute-start | bytes 1056776 | tf_op jit(solution)/shard_map/ppermute | solution.py:129
  22.5 3.9 %collective-permute-start.1 = (bf16[344,512]{1,0:T(8,128)(2,1)}, bf16[344,512]{1,0:T(8,128)(2,1)}, u32[]{:S(2)}, u32[]{:S(2)}) collective-permute-start(bf16[344,512]{1,0:T(8,128)(2,1)} %get-tuple-element.47), channel_id=1, source_target_pairs={{0,2},{1,7},{2,11},{3,15},{4,3},{5,14},{6,10},{7,6},{8,0},{9,5},{1... | collective-permute-start | bytes 1056776 | tf_op jit(solution)/shard_map/ppermute | solution.py:129
  26.5 4.6 %collective-permute-done = bf16[344,512]{1,0:T(8,128)(2,1)} collective-permute-done((bf16[344,512]{1,0:T(8,128)(2,1)}, bf16[344,512]{1,0:T(8,128)(2,1)}, u32[]{:S(2)}, u32[]{:S(2)}) %collective-permute-start) | collective-permute-done | bytes 352288 | tf_op jit(solution)/shard_map/ppermute | solution.py:129
  31.1 10.9 %collective-permute-done.1 = bf16[344,512]{1,0:T(8,128)(2,1)} collective-permute-done((bf16[344,512]{1,0:T(8,128)(2,1)}, bf16[344,512]{1,0:T(8,128)(2,1)}, u32[]{:S(2)}, u32[]{:S(2)}) %collective-permute-start.1) | collective-permute-done | bytes 352288 | tf_op jit(solution)/shard_map/ppermute | solution.py:129
  42.0 1.9 %broadcast_select_fusion.2 = (bf16[344,512]{1,0:T(8,128)(2,1)}, bf16[344,512]{1,0:T(8,128)(2,1)S(1)}) fusion(bf16[344,512]{1,0:T(8,128)(2,1)} %collective-permute-done.1, bf16[344,512]{1,0:T(8,128)(2,1)} %collective-permute-done, pred[]{:T(512)S(6)} %eq.12), kind=kLoop, calls=%fused_computation.18 | loop fusion | flops 352256 | bytes 1409025 | tf_op jit(solution)/shard_map/jit(_where)/select_n | solution.py:136
  43.9 4.7 %collective-permute-start.4 = (bf16[344,512]{1,0:T(8,128)(2,1)S(1)}, bf16[344,512]{1,0:T(8,128)(2,1)}, u32[]{:S(2)}, u32[]{:S(2)}) collective-permute-start(bf16[344,512]{1,0:T(8,128)(2,1)S(1)} %get-tuple-element.46), channel_id=1, source_target_pairs={{0,0},{2,2},{20,4},{22,6},{40,8},{42,10},{60,12},{62,14},{65,1},{6... | collective-permute-start | bytes 1056776 | tf_op jit(solution)/shard_map/ppermute | solution.py:137
  48.6 2.9 %broadcast_in_dim.30 = bf16[8,688,512]{2,1,0:T(8,128)(2,1)} broadcast(bf16[688,512]{1,0:T(8,128)(2,1)S(1)} %fusion.4), dimensions={1,2} | broadcast | bytes 6340608 | tf_op jit(solution)/shard_map/broadcast_in_dim | solution.py:138
  51.5 2.0 %bitcast_dynamic-update-slice_fusion.5 = bf16[8,688,512]{2,1,0:T(8,128)(2,1)} fusion(bf16[8,688,512]{2,1,0:T(8,128)(2,1)} %broadcast_in_dim.30, bf16[688,512]{1,0:T(8,128)(2,1)} %collective-permute-done.2), kind=kLoop, calls=%fused_computation.13 | loop fusion | bytes 1409024 | tf_op jit(solution)/shard_map/dynamic_update_slice | solution.py:111
  53.5 2.1 %bitcast_dynamic-update-slice_fusion.4 = bf16[8,688,512]{2,1,0:T(8,128)(2,1)} fusion(bf16[8,688,512]{2,1,0:T(8,128)(2,1)} %bitcast_dynamic-update-slice_fusion.5, bf16[688,512]{1,0:T(8,128)(2,1)} %collective-permute-done.3), kind=kLoop, calls=%fused_computation.12 | loop fusion | bytes 1409024 | tf_op jit(solution)/shard_map/dynamic_update_slice | solution.py:111
  55.6 3.0 %collective-permute-done.4 = bf16[344,512]{1,0:T(8,128)(2,1)} collective-permute-done((bf16[344,512]{1,0:T(8,128)(2,1)S(1)}, bf16[344,512]{1,0:T(8,128)(2,1)}, u32[]{:S(2)}, u32[]{:S(2)}) %collective-permute-start.4) | collective-permute-done | bytes 352288 | tf_op jit(solution)/shard_map/ppermute | solution.py:137
  58.7 2.7 %collective-permute-start.6 = (bf16[688,512]{1,0:T(8,128)(2,1)}, bf16[688,512]{1,0:T(8,128)(2,1)}, u32[]{:S(2)}, u32[]{:S(2)}) collective-permute-start(bf16[688,512]{1,0:T(8,128)(2,1)} %collective-permute-done.3), channel_id=1, source_target_pairs={{0,112},{16,0},{32,16},{48,32},{64,48},{80,64},{96,80},{112,96},{1... | collective-permute-start | bytes 2113544 | tf_op jit(solution)/shard_map/ppermute | solution.py:143
  61.4 7.8 %collective-permute-start.7 = (bf16[344,512]{1,0:T(8,128)(2,1)}, bf16[344,512]{1,0:T(8,128)(2,1)}, u32[]{:S(2)}, u32[]{:S(2)}) collective-permute-start(bf16[344,512]{1,0:T(8,128)(2,1)} %get-tuple-element.32), channel_id=1, source_target_pairs={{0,0},{2,2},{20,4},{22,6},{40,8},{42,10},{60,12},{62,14},{65,1},{6... | collective-permute-start | bytes 1056776 | tf_op jit(solution)/shard_map/ppermute | solution.py:144
  69.2 15.3 %collective-permute-done.7 = bf16[344,512]{1,0:T(8,128)(2,1)} collective-permute-done((bf16[344,512]{1,0:T(8,128)(2,1)}, bf16[344,512]{1,0:T(8,128)(2,1)}, u32[]{:S(2)}, u32[]{:S(2)}) %collective-permute-start.7) | collective-permute-done | bytes 352288 | tf_op jit(solution)/shard_map/ppermute | solution.py:144
  84.6 2.7 %collective-permute-start.9 = (bf16[688,512]{1,0:T(8,128)(2,1)}, bf16[688,512]{1,0:T(8,128)(2,1)S(1)}, u32[]{:S(2)}, u32[]{:S(2)}) collective-permute-start(bf16[688,512]{1,0:T(8,128)(2,1)} %collective-permute-done.6), channel_id=1, source_target_pairs={{0,112},{16,0},{32,16},{48,32},{64,48},{80,64},{96,80},{112,96},{1... | collective-permute-start | bytes 2113544 | tf_op jit(solution)/shard_map/ppermute | solution.py:149
  88.2 2.0 %bitcast_dynamic-update-slice_fusion.2 = bf16[8,688,512]{2,1,0:T(8,128)(2,1)} fusion(bf16[8,688,512]{2,1,0:T(8,128)(2,1)} %bitcast_dynamic-update-slice_fusion.3, bf16[688,512]{1,0:T(8,128)(2,1)} %collective-permute-done.6), kind=kLoop, calls=%fused_computation.10 | loop fusion | bytes 1409024 | tf_op jit(solution)/shard_map/dynamic_update_slice | solution.py:111
  90.2 8.9 %collective-permute-done.8 = bf16[688,512]{1,0:T(8,128)(2,1)S(1)} collective-permute-done((bf16[688,512]{1,0:T(8,128)(2,1)S(1)}, bf16[688,512]{1,0:T(8,128)(2,1)S(1)}, u32[]{:S(2)}, u32[]{:S(2)}) %collective-permute-start.8) | collective-permute-done | bytes 704544 | tf_op jit(solution)/shard_map/ppermute | solution.py:149
  99.1 2.5 %collective-permute-done.9 = bf16[688,512]{1,0:T(8,128)(2,1)S(1)} collective-permute-done((bf16[688,512]{1,0:T(8,128)(2,1)}, bf16[688,512]{1,0:T(8,128)(2,1)S(1)}, u32[]{:S(2)}, u32[]{:S(2)}) %collective-permute-start.9) | collective-permute-done | bytes 704544 | tf_op jit(solution)/shard_map/ppermute | solution.py:149
  106.5 2.6 %collective-permute-done.10 = bf16[344,512]{1,0:T(8,128)(2,1)S(1)} collective-permute-done((bf16[344,512]{1,0:T(8,128)(2,1)S(1)}, bf16[344,512]{1,0:T(8,128)(2,1)S(1)}, u32[]{:S(2)}, u32[]{:S(2)}) %collective-permute-start.10) | collective-permute-done | bytes 352288 | tf_op jit(solution)/shard_map/ppermute | solution.py:153
  111.4 8.6 %shard_map.37 = bf16[2,344,688]{2,1,0:T(8,128)(2,1)} custom-call(bf16[4,2,2,344,512]{4,3,2,1,0:T(8,128)(2,1)} %bitcast.37, bf16[8,688,512]{2,1,0:T(8,128)(2,1)} %bitcast_dynamic-update-slice_fusion.6.columns_ref), custom_call_target="tpu_custom_call" | custom-call | flops 3877634048 | bytes 16777216 | tf_op jit(solution)/shard_map/pallas_call | solution.py:94
  121.2 45.6 %all-gather.5.cloned.1.call-done = bf16[5504,512]{1,0:T(8,128)(2,1)} async-done(((bf16[344,512]{1,0:T(8,128)(2,1)}), bf16[5504,512]{1,0:T(8,128)(2,1)}) %all-gather.5.cloned.1.call-update) | async-done | bytes 5636112 | tf_op jit(solution)/shard_map/all_gather | solution.py:146
  166.8 9.3 %shard_map.38 = f32[2,344,688]{2,1,0:T(8,128)} custom-call(bf16[4,2,2,344,512]{4,3,2,1,0:T(8,128)(2,1)} %bitcast.36, bf16[8,688,512]{2,1,0:T(8,128)(2,1)} %bitcast_dynamic-update-slice_fusion.6.columns_ref, bf16[2,344,688]{2,1,0:T(8,128)(2,1)} %collective-permute-done.12.refs_0_), custom_call_target="tpu_custom_call" | custom-call | flops 3877634048 | bytes 16777216 | tf_op jit(solution)/shard_map/pallas_call | solution.py:94
  (26 shorter events, 12.2 us)
Async XLA Ops:
  6.5 1.8 copy-start
  6.5 104.8 %all-gather.7.cloned.1.call-start = ((), (), s32[]{:S(2)}) async-start(), calls=%async_computation.1 | async-start | bytes 5988352 | tf_op jit(solution)/shard_map/all_gather | solution.py:141
  11.9 30.1 %collective-permute-start.2 = (bf16[688,512]{1,0:T(8,128)(2,1)S(1)}, bf16[688,512]{1,0:T(8,128)(2,1)}, u32[]{:S(2)}, u32[]{:S(2)}) collective-permute-start(bf16[688,512]{1,0:T(8,128)(2,1)S(1)} %fusion.4), channel_id=1, source_target_pairs={{0,16},{16,32},{32,48},{48,64},{64,80},{80,96},{96,112},{112,0},{1... | collective-permute-start | bytes 2113544 | tf_op jit(solution)/shard_map/ppermute | solution.py:131
  14.4 27.6 %collective-permute-start.3 = (bf16[688,512]{1,0:T(8,128)(2,1)S(1)}, bf16[688,512]{1,0:T(8,128)(2,1)}, u32[]{:S(2)}, u32[]{:S(2)}) collective-permute-start(bf16[688,512]{1,0:T(8,128)(2,1)S(1)} %fusion.4), channel_id=1, source_target_pairs={{0,112},{16,0},{32,16},{48,32},{64,48},{80,64},{96,80},{112,96},{1... | collective-permute-start | bytes 2113544 | tf_op jit(solution)/shard_map/ppermute | solution.py:131
  19.4 11.7 %collective-permute-start = (bf16[344,512]{1,0:T(8,128)(2,1)}, bf16[344,512]{1,0:T(8,128)(2,1)}, u32[]{:S(2)}, u32[]{:S(2)}) collective-permute-start(bf16[344,512]{1,0:T(8,128)(2,1)} %get-tuple-element.48), channel_id=1, source_target_pairs={{0,0},{1,5},{2,9},{3,13},{4,1},{5,12},{6,8},{7,4},{8,2},{9,7},{10,... | collective-permute-start | bytes 1056776 | tf_op jit(solution)/shard_map/ppermute | solution.py:129
  22.5 19.5 %collective-permute-start.1 = (bf16[344,512]{1,0:T(8,128)(2,1)}, bf16[344,512]{1,0:T(8,128)(2,1)}, u32[]{:S(2)}, u32[]{:S(2)}) collective-permute-start(bf16[344,512]{1,0:T(8,128)(2,1)} %get-tuple-element.47), channel_id=1, source_target_pairs={{0,2},{1,7},{2,11},{3,15},{4,3},{5,14},{6,10},{7,6},{8,0},{9,5},{1... | collective-permute-start | bytes 1056776 | tf_op jit(solution)/shard_map/ppermute | solution.py:129
  43.9 14.7 %collective-permute-start.4 = (bf16[344,512]{1,0:T(8,128)(2,1)S(1)}, bf16[344,512]{1,0:T(8,128)(2,1)}, u32[]{:S(2)}, u32[]{:S(2)}) collective-permute-start(bf16[344,512]{1,0:T(8,128)(2,1)S(1)} %get-tuple-element.46), channel_id=1, source_target_pairs={{0,0},{2,2},{20,4},{22,6},{40,8},{42,10},{60,12},{62,14},{65,1},{6... | collective-permute-start | bytes 1056776 | tf_op jit(solution)/shard_map/ppermute | solution.py:137
  58.6 108.2 %all-gather.5.cloned.1.call-start = ((), (), s32[]{:S(2)}) async-start(), calls=%async_computation | async-start | bytes 5988352 | tf_op jit(solution)/shard_map/all_gather | solution.py:146
  58.6 25.9 %collective-permute-start.5 = (bf16[688,512]{1,0:T(8,128)(2,1)}, bf16[688,512]{1,0:T(8,128)(2,1)S(1)}, u32[]{:S(2)}, u32[]{:S(2)}) collective-permute-start(bf16[688,512]{1,0:T(8,128)(2,1)} %collective-permute-done.2), channel_id=1, source_target_pairs={{0,16},{16,32},{32,48},{48,64},{64,80},{80,96},{96,112},{112,0},{1... | collective-permute-start | bytes 2113544 | tf_op jit(solution)/shard_map/ppermute | solution.py:143
  58.7 25.8 %collective-permute-start.6 = (bf16[688,512]{1,0:T(8,128)(2,1)}, bf16[688,512]{1,0:T(8,128)(2,1)}, u32[]{:S(2)}, u32[]{:S(2)}) collective-permute-start(bf16[688,512]{1,0:T(8,128)(2,1)} %collective-permute-done.3), channel_id=1, source_target_pairs={{0,112},{16,0},{32,16},{48,32},{64,48},{80,64},{96,80},{112,96},{1... | collective-permute-start | bytes 2113544 | tf_op jit(solution)/shard_map/ppermute | solution.py:143
  61.4 23.1 %collective-permute-start.7 = (bf16[344,512]{1,0:T(8,128)(2,1)}, bf16[344,512]{1,0:T(8,128)(2,1)}, u32[]{:S(2)}, u32[]{:S(2)}) collective-permute-start(bf16[344,512]{1,0:T(8,128)(2,1)} %get-tuple-element.32), channel_id=1, source_target_pairs={{0,0},{2,2},{20,4},{22,6},{40,8},{42,10},{60,12},{62,14},{65,1},{6... | collective-permute-start | bytes 1056776 | tf_op jit(solution)/shard_map/ppermute | solution.py:144
  84.5 14.6 %collective-permute-start.8 = (bf16[688,512]{1,0:T(8,128)(2,1)S(1)}, bf16[688,512]{1,0:T(8,128)(2,1)S(1)}, u32[]{:S(2)}, u32[]{:S(2)}) collective-permute-start(bf16[688,512]{1,0:T(8,128)(2,1)S(1)} %collective-permute-done.5), channel_id=1, source_target_pairs={{0,16},{16,32},{32,48},{48,64},{64,80},{80,96},{96,112},{112,0},{1... | collective-permute-start | bytes 2113544 | tf_op jit(solution)/shard_map/ppermute | solution.py:149
  84.6 17.0 %collective-permute-start.9 = (bf16[688,512]{1,0:T(8,128)(2,1)}, bf16[688,512]{1,0:T(8,128)(2,1)S(1)}, u32[]{:S(2)}, u32[]{:S(2)}) collective-permute-start(bf16[688,512]{1,0:T(8,128)(2,1)} %collective-permute-done.6), channel_id=1, source_target_pairs={{0,112},{16,0},{32,16},{48,32},{64,48},{80,64},{96,80},{112,96},{1... | collective-permute-start | bytes 2113544 | tf_op jit(solution)/shard_map/ppermute | solution.py:149
  101.6 7.5 %collective-permute-start.10 = (bf16[344,512]{1,0:T(8,128)(2,1)S(1)}, bf16[344,512]{1,0:T(8,128)(2,1)S(1)}, u32[]{:S(2)}, u32[]{:S(2)}) collective-permute-start(bf16[344,512]{1,0:T(8,128)(2,1)S(1)} %slice.14), channel_id=1, source_target_pairs={{0,16},{16,32},{32,48},{48,64},{64,80},{80,96},{96,112},{112,0},{1... | collective-permute-start | bytes 1056776 | tf_op jit(solution)/shard_map/ppermute | solution.py:153
  103.4 6.4 %collective-permute-start.11 = (bf16[344,512]{1,0:T(8,128)(2,1)S(1)}, bf16[344,512]{1,0:T(8,128)(2,1)S(1)}, u32[]{:S(2)}, u32[]{:S(2)}) collective-permute-start(bf16[344,512]{1,0:T(8,128)(2,1)S(1)} %slice.15), channel_id=1, source_target_pairs={{0,112},{16,0},{32,16},{48,32},{64,48},{80,64},{96,80},{112,96},{1... | collective-permute-start | bytes 1056776 | tf_op jit(solution)/shard_map/ppermute | solution.py:154
  120.0 46.8 %collective-permute-start.12 = (bf16[2,344,688]{2,1,0:T(8,128)(2,1)}, bf16[2,344,688]{2,1,0:T(8,128)(2,1)}, u32[]{:S(2)}, u32[]{:S(2)}) collective-permute-start(bf16[2,344,688]{2,1,0:T(8,128)(2,1)} %shard_map.37), channel_id=1, source_target_pairs={{0,128},{16,144},{32,160},{48,176},{64,192},{80,208},{96,224},{112... | collective-permute-start | bytes 2840072 | tf_op jit(solution)/shard_map/ppermute | solution.py:157
Sparse Core Ops, SparseCore 0:
  58.7 43.6 all-gather.6
  104.3 62.4 all-gather.4

commit v3 on v2

--- a/solution.py
+++ b/solution.py
@@ -46,8 +46,7 @@
 ACROSS = [(i, (i + RING) % 16) for i in range(16)]
 
 
-def product_body(rows_ref, columns_ref, *refs, steps, scale):
-    out_ref, total = refs[-2:]
+def product_body(rows_ref, columns_ref, out_ref, total, *, steps):
     k = pl.program_id(0)
     pair = columns_ref.shape[0]
 
@@ -73,13 +72,10 @@
     @pl.when(k == steps - 1)
     def _():
         for half in range(2):
-            whole = total[half] + partial(half)
-            if scale is not None:
-                whole = (whole + refs[0][half].astype(jnp.float32)) * scale
-            out_ref[half] = whole.astype(out_ref.dtype)
-
-
-def product(rows, columns, other=None, scale=None):
+            out_ref[half] = (total[half] + partial(half)).astype(out_ref.dtype)
+
+
+def product(rows, columns):
     steps, part, tokens = rows.shape[0], *rows.shape[3:]
     n = columns.shape[1]
     in_specs = [
@@ -87,16 +83,12 @@
         pl.BlockSpec((2, n, tokens), lambda k: (k, 0, 0)),
     ]
     whole = pl.BlockSpec((2, part, n), lambda k: (0, 0, 0))
-    args = [rows, columns]
-    if other is not None:
-        in_specs.append(whole)
-        args.append(other)
     return pl.pallas_call(
-        functools.partial(product_body, steps=steps, scale=scale),
+        functools.partial(product_body, steps=steps),
         grid=(steps,),
         in_specs=in_specs,
         out_specs=whole,
-        out_shape=jax.ShapeDtypeStruct((2, part, n), jnp.bfloat16 if other is None else jnp.float32),
+        out_shape=jax.ShapeDtypeStruct((2, part, n), jnp.bfloat16),
         scratch_shapes=[pltpu.VMEM((2, part, n), jnp.float32)],
         compiler_params=pltpu.CompilerParams(
             dimension_semantics=("arbitrary",), vmem_limit_bytes=56 * 1024 * 1024
@@ -104,7 +96,75 @@
         cost_estimate=pl.CostEstimate(
             flops=2 * 2 * part * n * tokens * RING, bytes_accessed=16 * 1024 * 1024, transcendentals=0
         ),
-    )(*args)
+    )(rows, columns)
+
+
+def along_x(step):
+    return [
+        ((x * 2 + y) * 2 + c, ((x + step) % 4 * 2 + y) * 2 + c)
+        for x in range(4) for y in range(2) for c in range(2)
+    ]
+
+
+ACROSS_Y = [(t, t ^ 2) for t in range(16)]
+ACROSS_CORE = [(t, t ^ 1) for t in range(16)]
+ARRIVALS = ((0, 0), (3, 0), (1, 0), (0, 1), (3, 1), (2, 0), (1, 1), (2, 1))
+
+
+def own_body(where_ref, own0, own1, twin0, twin1, columns_ref, out_ref, total):
+    k = pl.program_id(0)
+    y, c = where_ref[8], where_ref[9]
+
+    def partial(own, twin):
+        return sum(
+            lax.dot_general(
+                rows_ref[0], columns_ref[i], (((1,), (1,)), ((), ())), preferred_element_type=jnp.float32
+            )
+            for rows_ref, i in ((own, c), (twin, 1 - c))
+        )
+
+    for half, (own, twin) in enumerate(((own0, twin0), (own1, twin1))):
+        @pl.when(k == 0)
+        def _():
+            total[half] = partial(own, twin)
+
+        @pl.when((k > 0) & (k < 3))
+        def _():
+            total[half] += partial(own, twin)
+
+        @pl.when(k == 3)
+        def _():
+            out_ref[half ^ y] = total[half] + partial(own, twin)
+
+
+def own_product(own, twin, columns, t):
+    part, tokens = own.shape[1:]
+    n = columns.shape[1]
+    table = [
+        [ARRIVALS.index(((k - x) % 4, y)) for y in range(2) for k in range(4)] for x in range(4)
+    ]
+    row = lax.dynamic_index_in_dim(jnp.array(table, jnp.int32), t // 4, keepdims=False)
+    where = jnp.concatenate([row, jnp.stack([(t // 2) % 2, t % 2]).astype(jnp.int32)])
+    block = (1, part, tokens)
+    first = pl.BlockSpec(block, lambda k, s: (s[k], 0, 0))
+    second = pl.BlockSpec(block, lambda k, s: (s[4 + k], 0, 0))
+    return pl.pallas_call(
+        own_body,
+        grid_spec=pltpu.PrefetchScalarGridSpec(
+            num_scalar_prefetch=1,
+            grid=(4,),
+            in_specs=[first, second, first, second, pl.BlockSpec((2, n, tokens), lambda k, s: (k, 0, 0))],
+            out_specs=pl.BlockSpec((2, part, n), lambda k, s: (0, 0, 0)),
+            scratch_shapes=[pltpu.VMEM((2, part, n), jnp.float32)],
+        ),
+        out_shape=jax.ShapeDtypeStruct((2, part, n), jnp.float32),
+        compiler_params=pltpu.CompilerParams(
+            dimension_semantics=("arbitrary",), vmem_limit_bytes=56 * 1024 * 1024
+        ),
+        cost_estimate=pl.CostEstimate(
+            flops=2 * 2 * part * n * tokens * RING, bytes_accessed=16 * 1024 * 1024, transcendentals=0
+        ),
+    )(where, own, own, twin, twin, columns)
 
 
 def put(columns, block, offset, start=0):
@@ -143,20 +203,45 @@
     up, down = lax.ppermute(up, "dp", along_z(1)), lax.ppermute(down, "dp", along_z(-1))
     ours = lax.ppermute(ours, BOTH, shifted())
     up, down, ours, columns = lax.optimization_barrier((up, down, ours, columns))
-    rows_ours = lax.all_gather(ours, "tensor", axis=0).reshape(4, 2, 2, part, tokens)
-
     columns = put(put(columns, up, RING - 2), down, 2)
     up, down = lax.ppermute(up, "dp", along_z(1)), lax.ppermute(down, "dp", along_z(-1))
-    up, down, columns = lax.optimization_barrier((up, down, columns))
+    before, after = lax.ppermute(ours, "tensor", along_x(1)), lax.ppermute(ours, "tensor", along_x(-1))
+    beside = lax.ppermute(ours, "tensor", ACROSS_Y)
+    up, down, columns, before, after, beside = lax.optimization_barrier(
+        (up, down, columns, before, after, beside)
+    )
 
     columns = put(put(columns, up, RING - 3), down, 3)
     up = lax.ppermute(up[:part], "dp", along_z(1))
     down = lax.ppermute(down[part:], "dp", along_z(-1))
-    up, down, columns = lax.optimization_barrier((up, down, columns))
+    near = jnp.stack([ours, before, after, beside])
+    before_beside = lax.ppermute(beside, "tensor", along_x(1))
+    far = lax.ppermute(after, "tensor", along_x(-1))
+    after_beside = lax.ppermute(after, "tensor", ACROSS_Y)
+    near_twin = lax.ppermute(near, "tensor", ACROSS_CORE)
+    up, down, columns, before_beside, far, after_beside, near_twin = lax.optimization_barrier(
+        (up, down, columns, before_beside, far, after_beside, near_twin)
+    )
     columns = put(put(columns, up, RING // 2), down, RING // 2, part)
+
+    cut = part // 32 * 16 + 16
+    last = jnp.concatenate(
+        [
+            lax.ppermute(before_beside[:cut], "tensor", along_x(1)),
+            lax.ppermute(after_beside[cut:], "tensor", along_x(-1)),
+        ],
+        axis=0,
+    )
+    middle = jnp.stack([before_beside, far, after_beside])
+    middle_twin = lax.ppermute(middle, "tensor", ACROSS_CORE)
+    last_twin = lax.ppermute(last, "tensor", ACROSS_CORE)
+    own = jnp.concatenate([near, middle, last[None]])
+    twin = jnp.concatenate([near_twin, middle_twin, last_twin[None]])
+
     sent = lax.ppermute(product(rows_theirs, columns), "dp", ACROSS)
+    kept = own_product(own, twin, columns, t)
     total = tokens * lax.axis_size("dp")
-    return product(rows_ours, columns, sent, 1.0 / total).reshape(n, n)
+    return ((kept + sent.astype(jnp.float32)) * (1.0 / total)).reshape(n, n)
 
 
 def solution(mesh):

time: 184 us -> 193 us (1.049)
  waiting for transfers between devices: 94.2 us -> 66.6 us
  starting transfers between devices: 35.9 us -> 53.7 us
  local copies, waits for them, and re-layouts: 15.2 us -> 24.3 us
  other arithmetic: 2.77 us -> 11.1 us
    all_gather x1 -> x0, waiting for transfers between devices: 45.6 us -> none  [shards(): lax.all_gather(ours, 'tensor', axis=0).reshape(4, 2, 2, part, tokens)]
    ppermute x0 -> x11, starting transfers between devices: none -> 17.3 us  [the longest x1 7.64 us: shards(): lax.ppermute(ours, 'tensor', along_x(-1))]
    ppermute x0 -> x11, waiting for transfers between devices: none -> 12.3 us  [the longest x1 5.07 us: shards(): beside = lax.ppermute(ours, 'tensor', ACROSS_Y)]
    ppermute x1, waiting for transfers between devices: 0.01 us -> 9.09 us  [shards(): sent = lax.ppermute(product(rows_theirs, columns), 'dp', ACROSS)]
    ppermute x2, waiting for transfers between devices: 8.88 us -> 0.01 us  [shards(): lax.ppermute(up, 'dp', along_z(1))]
    unnamed x2 -> x16, local copies, waits for them, and re-layouts: 1.79 us -> 8.25 us
    ppermute x1, waiting for transfers between devices: 2.59 us -> 6.91 us  [shards(): up = lax.ppermute(up[:part], 'dp', along_z(1))]
    ppermute x1, waiting for transfers between devices: 0.72 us -> 4.81 us  [shards(): down = lax.ppermute(down[part:], 'dp', along_z(-1))]
  transfers between devices with their start and end apart: 15 -> 25, of which waited for: 9 -> 11; matrix products, arithmetic and copies ran while one was open for 8% -> 14% of each run, Pallas kernels for 5% -> 10%
where the time goes in v3:
time: 193 us; the launch traced here: 192 us
  waiting for transfers between devices  66.6 us (35%)
  starting transfers between devices  53.7 us (28%)
  local copies, waits for them, and re-layouts  24.3 us (13%)
  Pallas kernels  19 us (10%)
  between operations  13.6 us (7%)
  other arithmetic  11.1 us (6%)
  matrix products  3.55 us (2%)
    ppermute x2, waiting for transfers between devices, shards(): lax.ppermute(jnp.where(b ^ turn == 0, low, high), BOTH, in_plane(turn))  15.5 us
    ppermute x1, waiting for transfers between devices, shards(): ours = lax.ppermute(ours, BOTH, shifted())  15.1 us
    dynamic_update_slice x8, local copies, waits for them, and re-layouts, put(): lax.dynamic_update_slice(columns, block[None], (PLACES.index(offset), sta...  11.6 us
    pallas_call x1, Pallas kernels, own_product(): pl.pallas_call(own_body, grid_spec=pltpu.PrefetchScalarGridSpec(num_scala...  10.2 us
    ppermute x1, waiting for transfers between devices, shards(): sent = lax.ppermute(product(rows_theirs, columns), 'dp', ACROSS)  9.09 us
    pallas_call x1, Pallas kernels, product(): pl.pallas_call(functools.partial(product_body, steps=steps), grid=(steps,...  8.76 us
    unnamed x16, local copies, waits for them, and re-layouts  8.25 us
    ppermute x1, starting transfers between devices, shards(): ours = lax.ppermute(ours, BOTH, shifted())  7.82 us
  transfers between devices with their start and end apart: 25, of which 11 were waited for; matrix products, arithmetic and copies ran while one was open for 14% of the time, Pallas kernels for 10%

profile of v3, /device:TPU:1, one launch (start us, length us, event | category | flops | bytes accessed | tf_op | source)
XLA Modules:
  0.0 191.8 jit_solution(768902806740262064)
XLA Ops:
  8.3 3.6 %fusion.4 = bf16[688,512]{1,0:T(8,128)(2,1)S(1)} fusion(bf16[512,688]{0,1:T(8,128)(2,1)} %param.6, bf16[688,2048]{1,0:T(8,128)(2,1)S(1)} %copy-done, bf16[512,2048]{1,0:T(8,128)(2,1)} %param.4), kind=kOutput, calls=%fused_computation.9 | convolution fusion | flops 1446010880 | bytes 6324224 | tf_op jit(solution)/shard_map/dot_general | solution.py:177
  14.4 4.0 %collective-permute-start.3 = (bf16[688,512]{1,0:T(8,128)(2,1)S(1)}, bf16[688,512]{1,0:T(8,128)(2,1)}, u32[]{:S(2)}, u32[]{:S(2)}) collective-permute-start(bf16[688,512]{1,0:T(8,128)(2,1)S(1)} %fusion.4), channel_id=1, source_target_pairs={{0,112},{16,0},{32,16},{48,32},{64,48},{80,64},{96,80},{112,96},{1... | collective-permute-start | bytes 2113544 | tf_op jit(solution)/shard_map/ppermute | solution.py:191
  19.4 3.1 %collective-permute-start = (bf16[344,512]{1,0:T(8,128)(2,1)}, bf16[344,512]{1,0:T(8,128)(2,1)}, u32[]{:S(2)}, u32[]{:S(2)}) collective-permute-start(bf16[344,512]{1,0:T(8,128)(2,1)} %get-tuple-element.62), channel_id=1, source_target_pairs={{0,0},{1,5},{2,9},{3,13},{4,1},{5,12},{6,8},{7,4},{8,2},{9,7},{10,... | collective-permute-start | bytes 1056776 | tf_op jit(solution)/shard_map/ppermute | solution.py:189
  22.5 3.9 %collective-permute-start.1 = (bf16[344,512]{1,0:T(8,128)(2,1)}, bf16[344,512]{1,0:T(8,128)(2,1)}, u32[]{:S(2)}, u32[]{:S(2)}) collective-permute-start(bf16[344,512]{1,0:T(8,128)(2,1)} %get-tuple-element.61), channel_id=1, source_target_pairs={{0,2},{1,7},{2,11},{3,15},{4,3},{5,14},{6,10},{7,6},{8,0},{9,5},{1... | collective-permute-start | bytes 1056776 | tf_op jit(solution)/shard_map/ppermute | solution.py:189
  26.5 4.6 %collective-permute-done = bf16[344,512]{1,0:T(8,128)(2,1)} collective-permute-done((bf16[344,512]{1,0:T(8,128)(2,1)}, bf16[344,512]{1,0:T(8,128)(2,1)}, u32[]{:S(2)}, u32[]{:S(2)}) %collective-permute-start) | collective-permute-done | bytes 352288 | tf_op jit(solution)/shard_map/ppermute | solution.py:189
  31.1 10.9 %collective-permute-done.1 = bf16[344,512]{1,0:T(8,128)(2,1)} collective-permute-done((bf16[344,512]{1,0:T(8,128)(2,1)}, bf16[344,512]{1,0:T(8,128)(2,1)}, u32[]{:S(2)}, u32[]{:S(2)}) %collective-permute-start.1) | collective-permute-done | bytes 352288 | tf_op jit(solution)/shard_map/ppermute | solution.py:189
  43.9 4.7 %collective-permute-start.4 = (bf16[344,512]{1,0:T(8,128)(2,1)S(1)}, bf16[344,512]{1,0:T(8,128)(2,1)}, u32[]{:S(2)}, u32[]{:S(2)}) collective-permute-start(bf16[344,512]{1,0:T(8,128)(2,1)S(1)} %get-tuple-element.60), channel_id=1, source_target_pairs={{0,0},{2,2},{20,4},{22,6},{40,8},{42,10},{60,12},{62,14},{65,1},{6... | collective-permute-start | bytes 1056776 | tf_op jit(solution)/shard_map/ppermute | solution.py:197
  48.6 3.0 %broadcast_in_dim.36 = bf16[8,688,512]{2,1,0:T(8,128)(2,1)} broadcast(bf16[688,512]{1,0:T(8,128)(2,1)S(1)} %fusion.4), dimensions={1,2} | broadcast | bytes 6340608 | tf_op jit(solution)/shard_map/broadcast_in_dim | solution.py:198
  55.7 2.8 %collective-permute-done.4 = bf16[344,512]{1,0:T(8,128)(2,1)} collective-permute-done((bf16[344,512]{1,0:T(8,128)(2,1)S(1)}, bf16[344,512]{1,0:T(8,128)(2,1)}, u32[]{:S(2)}, u32[]{:S(2)}) %collective-permute-start.4) | collective-permute-done | bytes 352288 | tf_op jit(solution)/shard_map/ppermute | solution.py:197
  61.3 7.8 %collective-permute-start.7 = (bf16[344,512]{1,0:T(8,128)(2,1)S(1)}, bf16[344,512]{1,0:T(8,128)(2,1)S(1)}, u32[]{:S(2)}, u32[]{:S(2)}) collective-permute-start(bf16[344,512]{1,0:T(8,128)(2,1)S(1)} %copy-done.3), channel_id=1, source_target_pairs={{0,0},{2,2},{20,4},{22,6},{40,8},{42,10},{60,12},{62,14},{65,1},{6... | collective-permute-start | bytes 1056776 | tf_op jit(solution)/shard_map/ppermute | solution.py:204
  69.1 15.1 %collective-permute-done.7 = bf16[344,512]{1,0:T(8,128)(2,1)S(1)} collective-permute-done((bf16[344,512]{1,0:T(8,128)(2,1)S(1)}, bf16[344,512]{1,0:T(8,128)(2,1)S(1)}, u32[]{:S(2)}, u32[]{:S(2)}) %collective-permute-start.7) | collective-permute-done | bytes 352288 | tf_op jit(solution)/shard_map/ppermute | solution.py:204
  88.3 7.6 %collective-permute-start.11 = (bf16[344,512]{1,0:T(8,128)(2,1)S(1)}, bf16[344,512]{1,0:T(8,128)(2,1)S(1)}, u32[]{:S(2)}, u32[]{:S(2)}) collective-permute-start(bf16[344,512]{1,0:T(8,128)(2,1)S(1)} %collective-permute-done.7), channel_id=1, source_target_pairs={{0,12},{1,13},{2,14},{3,15},{4,0},{5,1},{6,2},{7,3},{8,4},{9,5},{1... | collective-permute-start | bytes 1056776 | tf_op jit(solution)/shard_map/ppermute | solution.py:208
  100.0 4.6 %collective-permute-done.10 = bf16[344,512]{1,0:T(8,128)(2,1)S(1)} collective-permute-done((bf16[344,512]{1,0:T(8,128)(2,1)S(1)}, bf16[344,512]{1,0:T(8,128)(2,1)S(1)}, u32[]{:S(2)}, u32[]{:S(2)}) %collective-permute-start.10) | collective-permute-done | bytes 352288 | tf_op jit(solution)/shard_map/ppermute | solution.py:208
  105.6 5.1 %collective-permute-done.12 = bf16[344,512]{1,0:T(8,128)(2,1)S(1)} collective-permute-done((bf16[344,512]{1,0:T(8,128)(2,1)S(1)}, bf16[344,512]{1,0:T(8,128)(2,1)S(1)}, u32[]{:S(2)}, u32[]{:S(2)}) %collective-permute-start.12) | collective-permute-done | bytes 352288 | tf_op jit(solution)/shard_map/ppermute | solution.py:209
  112.2 2.7 %collective-permute-start.16 = (bf16[344,512]{1,0:T(8,128)(2,1)S(1)}, bf16[344,512]{1,0:T(8,128)(2,1)S(1)}, u32[]{:S(2)}, u32[]{:S(2)}) collective-permute-start(bf16[344,512]{1,0:T(8,128)(2,1)S(1)} %collective-permute-done.11), channel_id=1, source_target_pairs={{0,12},{1,13},{2,14},{3,15},{4,0},{5,1},{6,2},{7,3},{8,4},{9,5},{1... | collective-permute-start | bytes 1056776 | tf_op jit(solution)/shard_map/ppermute | solution.py:219
  118.3 6.9 %collective-permute-done.13 = bf16[344,512]{1,0:T(8,128)(2,1)S(1)} collective-permute-done((bf16[344,512]{1,0:T(8,128)(2,1)S(1)}, bf16[344,512]{1,0:T(8,128)(2,1)S(1)}, u32[]{:S(2)}, u32[]{:S(2)}) %collective-permute-start.13) | collective-permute-done | bytes 352288 | tf_op jit(solution)/shard_map/ppermute | solution.py:215
  128.4 4.8 %collective-permute-done.14 = bf16[344,512]{1,0:T(8,128)(2,1)S(1)} collective-permute-done((bf16[344,512]{1,0:T(8,128)(2,1)S(1)}, bf16[344,512]{1,0:T(8,128)(2,1)S(1)}, u32[]{:S(2)}, u32[]{:S(2)}) %collective-permute-start.14) | collective-permute-done | bytes 352288 | tf_op jit(solution)/shard_map/ppermute | solution.py:216
  135.5 2.7 %collective-permute-start.21 = (bf16[3,344,512]{2,1,0:T(8,128)(2,1)}, bf16[3,344,512]{2,1,0:T(8,128)(2,1)}, u32[]{:S(2)}, u32[]{:S(2)}) collective-permute-start(bf16[3,344,512]{2,1,0:T(8,128)(2,1)} %pad_maximum_fusion.2), channel_id=1, source_target_pairs={{0,1},{1,0},{2,3},{3,2},{4,5},{5,4},{6,7},{7,6},{8,9},{9,8},{10,11... | collective-permute-start | bytes 3170312 | tf_op jit(solution)/shard_map/ppermute | solution.py:236
  138.1 2.7 %collective-permute-start.20 = (bf16[168,512]{1,0:T(8,128)(2,1)S(1)}, bf16[168,512]{1,0:T(8,128)(2,1)S(1)}, u32[]{:S(2)}, u32[]{:S(2)}) collective-permute-start(bf16[168,512]{1,0:T(8,128)(2,1)S(1)} %slice.23), channel_id=1, source_target_pairs={{0,12},{1,13},{2,14},{3,15},{4,0},{5,1},{6,2},{7,3},{8,4},{9,5},{1... | collective-permute-start | bytes 516104 | tf_op jit(solution)/shard_map/ppermute | solution.py:231
  146.4 8.8 %shard_map.47 = bf16[2,344,688]{2,1,0:T(8,128)(2,1)} custom-call(bf16[4,2,2,344,512]{4,3,2,1,0:T(8,128)(2,1)} %bitcast.63, bf16[8,688,512]{2,1,0:T(8,128)(2,1)} %bitcast_dynamic-update-slice_fusion.6.columns_ref), custom_call_target="tpu_custom_call" | custom-call | flops 3877634048 | bytes 16777216 | tf_op jit(solution)/shard_map/pallas_call | solution.py:86
  159.3 3.2 %pad_maximum_fusion.twin0.twin1 = bf16[8,344,512]{2,1,0:T(8,128)(2,1)} fusion(bf16[1,344,512]{2,1,0:T(8,128)(2,1)} %bitcast.18, bf16[3,344,512]{2,1,0:T(8,128)(2,1)} %collective-permute-done.21, bf16[4,344,512]{2,1,0:T(8,128)(2,1)S(1)} %copy-done.2), kind=kLoop, calls=%fused_computation | loop fusion | flops 2818048 | bytes 5636096 | tf_op jit(solution)/shard_map/concatenate | solution.py:239
  162.5 10.2 %shard_map.46 = f32[2,344,688]{2,1,0:T(8,128)} custom-call(s32[10]{0:T(128)} %pad_add_fusion.where_ref, bf16[8,344,512]{2,1,0:T(8,128)(2,1)} %bitcast_dynamic-update-slice_fusion.8.own0.own1, bf16[8,344,512]{2,1,0:T(8,128)(2,1)} %bitcast_dynamic-update-slice_fusion.8.own0.own1, bf16[8,344,512]{2,1,0:T(8,128)(2,1)} %pad_maximum_fusion.twin0.twin1, ...), custom_call_target="tpu_custom_call" | custom-call | flops 3877634048 | bytes 16777216 | tf_op jit(solution)/shard_map/pallas_call | solution.py:151
  172.7 9.1 %collective-permute-done.23 = bf16[2,344,688]{2,1,0:T(8,128)(2,1)S(1)} collective-permute-done((bf16[2,344,688]{2,1,0:T(8,128)(2,1)}, bf16[2,344,688]{2,1,0:T(8,128)(2,1)S(1)}, u32[]{:S(2)}, u32[]{:S(2)}) %collective-permute-start.23) | collective-permute-done | bytes 946720 | tf_op jit(solution)/shard_map/ppermute | solution.py:241
  181.8 3.1 %add_multiply_fusion = f32[2,344,688]{2,1,0:T(8,128)} fusion(f32[2,344,688]{2,1,0:T(8,128)} %shard_map.46, bf16[2,344,688]{2,1,0:T(8,128)(2,1)S(1)} %collective-permute-done.23), kind=kLoop, calls=%fused_computation.1 | loop fusion | flops 1420032 | bytes 4733440 | tf_op jit(solution)/shard_map/mul | solution.py:244
  (69 shorter events, 43.1 us)
Async XLA Ops:
  6.5 139.9 %all-gather.3.cloned.1.call-start = ((), (), s32[]{:S(2)}) async-start(), calls=%async_computation | async-start | bytes 5988352 | tf_op jit(solution)/shard_map/all_gather | solution.py:201
  11.9 30.1 %collective-permute-start.2 = (bf16[688,512]{1,0:T(8,128)(2,1)S(1)}, bf16[688,512]{1,0:T(8,128)(2,1)}, u32[]{:S(2)}, u32[]{:S(2)}) collective-permute-start(bf16[688,512]{1,0:T(8,128)(2,1)S(1)} %fusion.4), channel_id=1, source_target_pairs={{0,16},{16,32},{32,48},{48,64},{64,80},{80,96},{96,112},{112,0},{1... | collective-permute-start | bytes 2113544 | tf_op jit(solution)/shard_map/ppermute | solution.py:191
  14.4 27.6 %collective-permute-start.3 = (bf16[688,512]{1,0:T(8,128)(2,1)S(1)}, bf16[688,512]{1,0:T(8,128)(2,1)}, u32[]{:S(2)}, u32[]{:S(2)}) collective-permute-start(bf16[688,512]{1,0:T(8,128)(2,1)S(1)} %fusion.4), channel_id=1, source_target_pairs={{0,112},{16,0},{32,16},{48,32},{64,48},{80,64},{96,80},{112,96},{1... | collective-permute-start | bytes 2113544 | tf_op jit(solution)/shard_map/ppermute | solution.py:191
  19.4 11.7 %collective-permute-start = (bf16[344,512]{1,0:T(8,128)(2,1)}, bf16[344,512]{1,0:T(8,128)(2,1)}, u32[]{:S(2)}, u32[]{:S(2)}) collective-permute-start(bf16[344,512]{1,0:T(8,128)(2,1)} %get-tuple-element.62), channel_id=1, source_target_pairs={{0,0},{1,5},{2,9},{3,13},{4,1},{5,12},{6,8},{7,4},{8,2},{9,7},{10,... | collective-permute-start | bytes 1056776 | tf_op jit(solution)/shard_map/ppermute | solution.py:189
  22.5 19.5 %collective-permute-start.1 = (bf16[344,512]{1,0:T(8,128)(2,1)}, bf16[344,512]{1,0:T(8,128)(2,1)}, u32[]{:S(2)}, u32[]{:S(2)}) collective-permute-start(bf16[344,512]{1,0:T(8,128)(2,1)} %get-tuple-element.61), channel_id=1, source_target_pairs={{0,2},{1,7},{2,11},{3,15},{4,3},{5,14},{6,10},{7,6},{8,0},{9,5},{1... | collective-permute-start | bytes 1056776 | tf_op jit(solution)/shard_map/ppermute | solution.py:189
  43.9 14.6 %collective-permute-start.4 = (bf16[344,512]{1,0:T(8,128)(2,1)S(1)}, bf16[344,512]{1,0:T(8,128)(2,1)}, u32[]{:S(2)}, u32[]{:S(2)}) collective-permute-start(bf16[344,512]{1,0:T(8,128)(2,1)S(1)} %get-tuple-element.60), channel_id=1, source_target_pairs={{0,0},{2,2},{20,4},{22,6},{40,8},{42,10},{60,12},{62,14},{65,1},{6... | collective-permute-start | bytes 1056776 | tf_op jit(solution)/shard_map/ppermute | solution.py:197
  58.5 25.7 %collective-permute-start.5 = (bf16[688,512]{1,0:T(8,128)(2,1)}, bf16[688,512]{1,0:T(8,128)(2,1)}, u32[]{:S(2)}, u32[]{:S(2)}) collective-permute-start(bf16[688,512]{1,0:T(8,128)(2,1)} %collective-permute-done.2), channel_id=1, source_target_pairs={{0,16},{16,32},{32,48},{48,64},{64,80},{80,96},{96,112},{112,0},{1... | collective-permute-start | bytes 2113544 | tf_op jit(solution)/shard_map/ppermute | solution.py:203
  58.6 25.7 %collective-permute-start.6 = (bf16[688,512]{1,0:T(8,128)(2,1)}, bf16[688,512]{1,0:T(8,128)(2,1)}, u32[]{:S(2)}, u32[]{:S(2)}) collective-permute-start(bf16[688,512]{1,0:T(8,128)(2,1)} %collective-permute-done.3), channel_id=1, source_target_pairs={{0,112},{16,0},{32,16},{48,32},{64,48},{80,64},{96,80},{112,96},{1... | collective-permute-start | bytes 2113544 | tf_op jit(solution)/shard_map/ppermute | solution.py:203
  61.3 23.0 %collective-permute-start.7 = (bf16[344,512]{1,0:T(8,128)(2,1)S(1)}, bf16[344,512]{1,0:T(8,128)(2,1)S(1)}, u32[]{:S(2)}, u32[]{:S(2)}) collective-permute-start(bf16[344,512]{1,0:T(8,128)(2,1)S(1)} %copy-done.3), channel_id=1, source_target_pairs={{0,0},{2,2},{20,4},{22,6},{40,8},{42,10},{60,12},{62,14},{65,1},{6... | collective-permute-start | bytes 1056776 | tf_op jit(solution)/shard_map/ppermute | solution.py:204
  84.3 26.4 %collective-permute-start.8 = (bf16[688,512]{1,0:T(8,128)(2,1)}, bf16[688,512]{1,0:T(8,128)(2,1)S(1)}, u32[]{:S(2)}, u32[]{:S(2)}) collective-permute-start(bf16[688,512]{1,0:T(8,128)(2,1)} %collective-permute-done.5), channel_id=1, source_target_pairs={{0,16},{16,32},{32,48},{48,64},{64,80},{80,96},{96,112},{112,0},{1... | collective-permute-start | bytes 2113544 | tf_op jit(solution)/shard_map/ppermute | solution.py:207
  84.3 26.4 %collective-permute-start.9 = (bf16[688,512]{1,0:T(8,128)(2,1)}, bf16[688,512]{1,0:T(8,128)(2,1)S(1)}, u32[]{:S(2)}, u32[]{:S(2)}) collective-permute-start(bf16[688,512]{1,0:T(8,128)(2,1)} %collective-permute-done.6), channel_id=1, source_target_pairs={{0,112},{16,0},{32,16},{48,32},{64,48},{80,64},{96,80},{112,96},{1... | collective-permute-start | bytes 2113544 | tf_op jit(solution)/shard_map/ppermute | solution.py:207
  88.3 16.3 %collective-permute-start.10 = (bf16[344,512]{1,0:T(8,128)(2,1)S(1)}, bf16[344,512]{1,0:T(8,128)(2,1)S(1)}, u32[]{:S(2)}, u32[]{:S(2)}) collective-permute-start(bf16[344,512]{1,0:T(8,128)(2,1)S(1)} %collective-permute-done.7), channel_id=1, source_target_pairs={{0,4},{1,5},{2,6},{3,7},{4,8},{5,9},{6,10},{7,11},{8,12},{9,13},{1... | collective-permute-start | bytes 1056776 | tf_op jit(solution)/shard_map/ppermute | solution.py:208
  88.3 17.3 %collective-permute-start.11 = (bf16[344,512]{1,0:T(8,128)(2,1)S(1)}, bf16[344,512]{1,0:T(8,128)(2,1)S(1)}, u32[]{:S(2)}, u32[]{:S(2)}) collective-permute-start(bf16[344,512]{1,0:T(8,128)(2,1)S(1)} %collective-permute-done.7), channel_id=1, source_target_pairs={{0,12},{1,13},{2,14},{3,15},{4,0},{5,1},{6,2},{7,3},{8,4},{9,5},{1... | collective-permute-start | bytes 1056776 | tf_op jit(solution)/shard_map/ppermute | solution.py:208
  95.9 14.7 %collective-permute-start.12 = (bf16[344,512]{1,0:T(8,128)(2,1)S(1)}, bf16[344,512]{1,0:T(8,128)(2,1)S(1)}, u32[]{:S(2)}, u32[]{:S(2)}) collective-permute-start(bf16[344,512]{1,0:T(8,128)(2,1)S(1)} %collective-permute-done.7), channel_id=1, source_target_pairs={{0,2},{1,3},{2,0},{3,1},{4,6},{5,7},{6,4},{7,5},{8,10},{9,11},{10,... | collective-permute-start | bytes 1056776 | tf_op jit(solution)/shard_map/ppermute | solution.py:209
  110.8 22.4 %collective-permute-start.18 = (bf16[4,344,512]{2,1,0:T(8,128)(2,1)S(1)}, bf16[4,344,512]{2,1,0:T(8,128)(2,1)S(1)}, u32[]{:S(2)}, u32[]{:S(2)}) collective-permute-start(bf16[4,344,512]{2,1,0:T(8,128)(2,1)S(1)} %pad_maximum_fusion.1), channel_id=1, source_target_pairs={{0,1},{1,0},{2,3},{3,2},{4,5},{5,4},{6,7},{7,6},{8,9},{9,8},{10,11... | collective-permute-start | bytes 4227080 | tf_op jit(solution)/shard_map/ppermute | solution.py:221
  112.2 21.0 %collective-permute-start.15 = (bf16[344,512]{1,0:T(8,128)(2,1)S(1)}, bf16[344,512]{1,0:T(8,128)(2,1)S(1)}, u32[]{:S(2)}, u32[]{:S(2)}) collective-permute-start(bf16[344,512]{1,0:T(8,128)(2,1)S(1)} %collective-permute-done.12), channel_id=1, source_target_pairs={{0,4},{1,5},{2,6},{3,7},{4,8},{5,9},{6,10},{7,11},{8,12},{9,13},{1... | collective-permute-start | bytes 1056776 | tf_op jit(solution)/shard_map/ppermute | solution.py:218
  112.2 21.0 %collective-permute-start.16 = (bf16[344,512]{1,0:T(8,128)(2,1)S(1)}, bf16[344,512]{1,0:T(8,128)(2,1)S(1)}, u32[]{:S(2)}, u32[]{:S(2)}) collective-permute-start(bf16[344,512]{1,0:T(8,128)(2,1)S(1)} %collective-permute-done.11), channel_id=1, source_target_pairs={{0,12},{1,13},{2,14},{3,15},{4,0},{5,1},{6,2},{7,3},{8,4},{9,5},{1... | collective-permute-start | bytes 1056776 | tf_op jit(solution)/shard_map/ppermute | solution.py:219
  114.9 18.3 %collective-permute-start.17 = (bf16[344,512]{1,0:T(8,128)(2,1)S(1)}, bf16[344,512]{1,0:T(8,128)(2,1)S(1)}, u32[]{:S(2)}, u32[]{:S(2)}) collective-permute-start(bf16[344,512]{1,0:T(8,128)(2,1)S(1)} %collective-permute-done.11), channel_id=1, source_target_pairs={{0,2},{1,3},{2,0},{3,1},{4,6},{5,7},{6,4},{7,5},{8,10},{9,11},{10,... | collective-permute-start | bytes 1056776 | tf_op jit(solution)/shard_map/ppermute | solution.py:220
  115.0 10.2 %collective-permute-start.13 = (bf16[344,512]{1,0:T(8,128)(2,1)S(1)}, bf16[344,512]{1,0:T(8,128)(2,1)S(1)}, u32[]{:S(2)}, u32[]{:S(2)}) collective-permute-start(bf16[344,512]{1,0:T(8,128)(2,1)S(1)} %slice.20), channel_id=1, source_target_pairs={{0,16},{16,32},{32,48},{48,64},{64,80},{80,96},{96,112},{112,0},{1... | collective-permute-start | bytes 1056776 | tf_op jit(solution)/shard_map/ppermute | solution.py:215
  125.2 8.0 %collective-permute-start.14 = (bf16[344,512]{1,0:T(8,128)(2,1)S(1)}, bf16[344,512]{1,0:T(8,128)(2,1)S(1)}, u32[]{:S(2)}, u32[]{:S(2)}) collective-permute-start(bf16[344,512]{1,0:T(8,128)(2,1)S(1)} %slice.21), channel_id=1, source_target_pairs={{0,112},{16,0},{32,16},{48,32},{64,48},{80,64},{96,80},{112,96},{1... | collective-permute-start | bytes 1056776 | tf_op jit(solution)/shard_map/ppermute | solution.py:216
  135.5 23.8 %collective-permute-start.21 = (bf16[3,344,512]{2,1,0:T(8,128)(2,1)}, bf16[3,344,512]{2,1,0:T(8,128)(2,1)}, u32[]{:S(2)}, u32[]{:S(2)}) collective-permute-start(bf16[3,344,512]{2,1,0:T(8,128)(2,1)} %pad_maximum_fusion.2), channel_id=1, source_target_pairs={{0,1},{1,0},{2,3},{3,2},{4,5},{5,4},{6,7},{7,6},{8,9},{9,8},{10,11... | collective-permute-start | bytes 3170312 | tf_op jit(solution)/shard_map/ppermute | solution.py:236
  138.1 7.4 %collective-permute-start.20 = (bf16[168,512]{1,0:T(8,128)(2,1)S(1)}, bf16[168,512]{1,0:T(8,128)(2,1)S(1)}, u32[]{:S(2)}, u32[]{:S(2)}) collective-permute-start(bf16[168,512]{1,0:T(8,128)(2,1)S(1)} %slice.23), channel_id=1, source_target_pairs={{0,12},{1,13},{2,14},{3,15},{4,0},{5,1},{6,2},{7,3},{8,4},{9,5},{1... | collective-permute-start | bytes 516104 | tf_op jit(solution)/shard_map/ppermute | solution.py:231
  145.6 13.7 %collective-permute-start.22 = (bf16[344,512]{1,0:T(8,128)(2,1)S(1)}, bf16[344,512]{1,0:T(8,128)(2,1)}, u32[]{:S(2)}, u32[]{:S(2)}) collective-permute-start(bf16[344,512]{1,0:T(8,128)(2,1)S(1)} %constant_dynamic-update-slice_fusion), channel_id=1, source_target_pairs={{0,1},{1,0},{2,3},{3,2},{4,5},{5,4},{6,7},{7,6},{8,9},{9,8},{10,11... | collective-permute-start | bytes 1056776 | tf_op jit(solution)/shard_map/ppermute | solution.py:237
  155.2 26.6 %collective-permute-start.23 = (bf16[2,344,688]{2,1,0:T(8,128)(2,1)}, bf16[2,344,688]{2,1,0:T(8,128)(2,1)S(1)}, u32[]{:S(2)}, u32[]{:S(2)}) collective-permute-start(bf16[2,344,688]{2,1,0:T(8,128)(2,1)} %shard_map.47), channel_id=1, source_target_pairs={{0,128},{16,144},{32,160},{48,176},{64,192},{80,208},{96,224},{112... | collective-permute-start | bytes 2840072 | tf_op jit(solution)/shard_map/ppermute | solution.py:241
  (5 other events, 32.8 us)
Sparse Core Ops, SparseCore 0:
  58.6 52.2 all-gather.2

commit v4 on v0

v4 whole, which is shorter than its diff:
```python
import jax
import jax.numpy as jnp
from jax import lax
from jax.sharding import PartitionSpec as P

BOTH = ("dp", "tensor")
RING = 8
PLACES = (0, 4, 1, 7, 2, 6, 3, 5)


def place(offset, half):
    k = PLACES.index(offset)
    return (k // 2) * 4 + half * 2 + k % 2


def in_plane(turn):
    pairs = []
    for h in range(2):
        for source in range(RING):
            for b in range(2):
                for z in range(RING):
                    plane = (h * RING + source) * 16
                    pairs.append((plane + b * RING + z, plane + place((source - z) % RING, b ^ turn)))
    return pairs


def shifted():
    pairs = []
    for h in range(2):
        for z in range(RING):
            for offset in range(RING):
                for half in range(2):
                    t = place(offset, half)
                    pairs.append(((h * RING + (z + offset) % RING) * 16 + t, (h * RING + z) * 16 + t))
    return pairs


def along_z(step):
    return [(h * RING + z, h * RING + (z + step) % RING) for h in range(2) for z in range(RING)]


ACROSS = [(i, (i + RING) % 16) for i in range(16)]


def along_x(step):
    return [
        ((x * 2 + y) * 2 + c, ((x + step) % 4 * 2 + y) * 2 + c)
        for x in range(4) for y in range(2) for c in range(2)
    ]


ACROSS_Y = [(t, t ^ 2) for t in range(16)]
ACROSS_CORE = [(t, t ^ 1) for t in range(16)]
def put(columns, block, offset, t, start=0):
    k, core = divmod(PLACES.index(offset), 2)
    return lax.dynamic_update_slice(
        columns, block[None, None], (core ^ (t % 2), (k - t // 4) % 4, start, 0)
    )


def first_half(piece):
    before, after = lax.ppermute(piece, "tensor", along_x(1)), lax.ppermute(piece, "tensor", along_x(-1))
    beside = lax.ppermute(piece, "tensor", ACROSS_Y)
    before_beside = lax.ppermute(beside, "tensor", along_x(1))
    far = lax.ppermute(after, "tensor", along_x(-1))
    after_beside = lax.ppermute(after, "tensor", ACROSS_Y)
    return piece, before, after, beside, before_beside, far, after_beside


def gathered(pieces, t):
    piece, before, after, beside, before_beside, far, after_beside = pieces
    part = piece.shape[0]
    y = (t // 2) % 2

    def placed(rows, block, x, beside, start=0):
        return lax.dynamic_update_slice(rows, block[None, None], (x, beside ^ y, start, 0))

    cut = part // 32 * 16 + 16
    far_low = lax.ppermute(before_beside[:cut], "tensor", along_x(1))
    far_high = lax.ppermute(after_beside[cut:], "tensor", along_x(-1))

    own = jnp.broadcast_to(piece[None, None], (4, 2) + piece.shape)
    own = placed(placed(placed(own, before, 3, 0), after, 1, 0), beside, 0, 1)
    own = placed(placed(placed(own, before_beside, 3, 1), far, 2, 0), after_beside, 1, 1)
    own = placed(placed(own, far_low, 2, 1), far_high, 2, 1, cut)
    own = own.reshape(4, 2 * part, piece.shape[1])
    return own, lax.ppermute(own, "tensor", ACROSS_CORE)


def product(rows, columns):
    return sum(
        lax.dot_general(
            rows[i], columns[i], (((0, 2), (0, 2)), ((), ())), preferred_element_type=jnp.float32
        )
        for i in range(2)
    )


def shards(out_grad, down_weight, gate_pre):
    n, tokens = down_weight.shape[0], out_grad.shape[0]
    part = n // 2
    hidden_grad = lax.dot_general(
        down_weight, out_grad, (((1,), (1,)), ((), ())), preferred_element_type=jnp.float32
    ).astype(jnp.bfloat16)
    up_grad = (hidden_grad.astype(jnp.float32) * jax.nn.silu(gate_pre.T.astype(jnp.float32))).astype(
        jnp.bfloat16
    )
    h = lax.axis_index("dp") // RING
    t = lax.axis_index("tensor")
    b, half = t // RING, (t // 2) % 2

    low, high = up_grad[:part], up_grad[part:]
    got = [
        lax.ppermute(jnp.where((b ^ turn) == 0, low, high), BOTH, in_plane(turn)) for turn in range(2)
    ]
    up, down = lax.ppermute(up_grad, "dp", along_z(1)), lax.ppermute(up_grad, "dp", along_z(-1))
    got[0], got[1], up, down, up_grad = lax.optimization_barrier((got[0], got[1], up, down, up_grad))

    first_turn = half ^ (1 - h)
    theirs = jnp.where(first_turn == 0, got[0], got[1])
    ours = jnp.where(first_turn == 0, got[1], got[0])
    theirs = lax.ppermute(theirs, BOTH, shifted())
    columns = jnp.broadcast_to(up_grad, (2, 4, n, tokens))
    columns = put(put(columns, up, RING - 1, t), down, 1, t)
    theirs, up, down, ours, columns = lax.optimization_barrier((theirs, up, down, ours, columns))

    pieces = first_half(theirs)
    up, down = lax.ppermute(up, "dp", along_z(1)), lax.ppermute(down, "dp", along_z(-1))
    columns = put(put(columns, up, RING - 2, t), down, 2, t)
    up, down, ours = lax.optimization_barrier((up, down, ours))

    ours = lax.ppermute(ours, BOTH, shifted())
    rows_theirs = gathered(pieces, t)
    up, down = lax.ppermute(up, "dp", along_z(1)), lax.ppermute(down, "dp", along_z(-1))
    columns = put(put(columns, up, RING - 3, t), down, 3, t)
    pieces = first_half(ours)
    up = lax.ppermute(up[:part], "dp", along_z(1))
    down = lax.ppermute(down[part:], "dp", along_z(-1))
    columns = put(put(columns, up, RING // 2, t), down, RING // 2, t, part)

    partial = product(rows_theirs, columns).astype(jnp.bfloat16)
    sent = lax.ppermute(partial, "dp", ACROSS)
    _, pieces = lax.optimization_barrier((partial, pieces))
    kept = product(gathered(pieces, t), columns)
    total = tokens * lax.axis_size("dp")
    return (kept + sent.astype(jnp.float32)) * (1.0 / total)


def solution(mesh):
    placed = (P("dp", None), P("tensor", None), P("dp", "tensor"))
    return jax.shard_map(
        shards, mesh=mesh, in_specs=placed, out_specs=P("dp", "tensor"), check_vma=False
    )
```

time: 655 us -> 186 us (0.28)
  waiting for transfers between devices: 612 us -> 65.1 us
  starting transfers between devices: 0.04 us -> 64.4 us
  local copies, waits for them, and re-layouts: 1.79 us -> 28.6 us
  between operations: 13.4 us -> 0.36 us
    reduce_scatter x1 -> x0, waiting for transfers between devices: 540 us -> none  [shards(): lax.psum_scatter(lax.dot_general(whole, up_grad, (((0,), (0,)), ((), ()))...]
    all_gather x1 -> x0, waiting for transfers between devices: 72.6 us -> none  [shards(): whole = lax.all_gather(up_grad, 'tensor', axis=1, tiled=True)]
    ppermute x0 -> x31, waiting for transfers between devices: none -> 65.1 us  [the longest x1 20 us: shards(): sent = lax.ppermute(partial, 'dp', ACROSS)]
    ppermute x0 -> x31, starting transfers between devices: none -> 64.4 us  [the longest x2 11.1 us: gathered(): return (own, lax.ppermute(own, 'tensor', ACROSS_CORE))]
    dynamic_update_slice x0 -> x24, local copies, waits for them, and re-layouts: none -> 19.7 us  [the longest x8 12.5 us: put(): lax.dynamic_update_slice(columns, block[None, None], (core ^ t % 2, (k -...]
    dot_general x2 -> x5, matrix products: 22.6 us -> 23.3 us  [the longest x4 19.7 us: product(): lax.dot_general(rows[i], columns[i], (((0, 2), (0, 2)), ((), ())), prefer...]
  transfers between devices with their start and end apart: 2 -> 31, of which waited for: 2 -> 12; matrix products, arithmetic and copies ran while one was open for 0% -> 23% of each run, Pallas kernels for 0% -> 0%
where the time goes in v4:
time: 186 us; the launch traced here: 184 us
  waiting for transfers between devices  65.1 us (35%)
  starting transfers between devices  64.4 us (35%)
  local copies, waits for them, and re-layouts  28.6 us (15%)
  matrix products  23.3 us (13%)
  other arithmetic  2.78 us (1%)
    ppermute x1, waiting for transfers between devices, shards(): sent = lax.ppermute(partial, 'dp', ACROSS)  20 us
    dot_general x4, matrix products, product(): lax.dot_general(rows[i], columns[i], (((0, 2), (0, 2)), ((), ())), prefer...  19.7 us
    ppermute x2, waiting for transfers between devices, shards(): lax.ppermute(jnp.where(b ^ turn == 0, low, high), BOTH, in_plane(turn))  15.5 us
    ppermute x1, waiting for transfers between devices, shards(): ours = lax.ppermute(ours, BOTH, shifted())  15.2 us
    dynamic_update_slice x8, local copies, waits for them, and re-layouts, put(): lax.dynamic_update_slice(columns, block[None, None], (core ^ t % 2, (k -...  12.5 us
    ppermute x2, starting transfers between devices, gathered(): return (own, lax.ppermute(own, 'tensor', ACROSS_CORE))  11.1 us
    ppermute x1, starting transfers between devices, shards(): ours = lax.ppermute(ours, BOTH, shifted())  8.16 us
    dynamic_update_slice x16, local copies, waits for them, and re-layouts, placed(): lax.dynamic_update_slice(rows, block[None, None], (x, beside ^ y, start, 0))  7.15 us
  transfers between devices with their start and end apart: 31, of which 12 were waited for; matrix products, arithmetic and copies ran while one was open for 23% of the time, Pallas kernels for 0%

profile of v4, /device:TPU:1, one launch (start us, length us, event | category | flops | bytes accessed | tf_op | source)
XLA Modules:
  0.0 184.4 jit_solution(11589933671496808212)
XLA Ops:
  1.8 3.6 %fusion.11 = bf16[688,512]{1,0:T(8,128)(2,1)S(1)} fusion(bf16[512,688]{0,1:T(8,128)(2,1)} %param.5, bf16[688,2048]{1,0:T(8,128)(2,1)S(1)} %copy-done, bf16[512,2048]{1,0:T(8,128)(2,1)} %param.3), kind=kOutput, calls=%fused_computation.17 | convolution fusion | flops 1446010880 | bytes 6324224 | tf_op jit(solution)/shard_map/dot_general | solution.py:102
  7.9 4.0 %collective-permute-start.3 = (bf16[688,512]{1,0:T(8,128)(2,1)S(1)}, bf16[688,512]{1,0:T(8,128)(2,1)}, u32[]{:S(2)}, u32[]{:S(2)}) collective-permute-start(bf16[688,512]{1,0:T(8,128)(2,1)S(1)} %fusion.11), channel_id=1, source_target_pairs={{0,112},{16,0},{32,16},{48,32},{64,48},{80,64},{96,80},{112,96},{1... | collective-permute-start | bytes 2113544 | tf_op jit(solution)/shard_map/ppermute | solution.py:116
  12.8 3.1 %collective-permute-start = (bf16[344,512]{1,0:T(8,128)(2,1)}, bf16[344,512]{1,0:T(8,128)(2,1)}, u32[]{:S(2)}, u32[]{:S(2)}) collective-permute-start(bf16[344,512]{1,0:T(8,128)(2,1)} %get-tuple-element.48), channel_id=1, source_target_pairs={{0,0},{1,5},{2,9},{3,13},{4,1},{5,12},{6,8},{7,4},{8,2},{9,7},{10,... | collective-permute-start | bytes 1056776 | tf_op jit(solution)/shard_map/ppermute | solution.py:114
  16.0 3.9 %collective-permute-start.1 = (bf16[344,512]{1,0:T(8,128)(2,1)}, bf16[344,512]{1,0:T(8,128)(2,1)}, u32[]{:S(2)}, u32[]{:S(2)}) collective-permute-start(bf16[344,512]{1,0:T(8,128)(2,1)} %get-tuple-element.47), channel_id=1, source_target_pairs={{0,2},{1,7},{2,11},{3,15},{4,3},{5,14},{6,10},{7,6},{8,0},{9,5},{1... | collective-permute-start | bytes 1056776 | tf_op jit(solution)/shard_map/ppermute | solution.py:114
  20.0 4.6 %collective-permute-done = bf16[344,512]{1,0:T(8,128)(2,1)} collective-permute-done((bf16[344,512]{1,0:T(8,128)(2,1)}, bf16[344,512]{1,0:T(8,128)(2,1)}, u32[]{:S(2)}, u32[]{:S(2)}) %collective-permute-start) | collective-permute-done | bytes 352288 | tf_op jit(solution)/shard_map/ppermute | solution.py:114
  24.6 10.9 %collective-permute-done.1 = bf16[344,512]{1,0:T(8,128)(2,1)} collective-permute-done((bf16[344,512]{1,0:T(8,128)(2,1)}, bf16[344,512]{1,0:T(8,128)(2,1)}, u32[]{:S(2)}, u32[]{:S(2)}) %collective-permute-start.1) | collective-permute-done | bytes 352288 | tf_op jit(solution)/shard_map/ppermute | solution.py:114
  37.3 4.7 %collective-permute-start.4 = (bf16[344,512]{1,0:T(8,128)(2,1)S(1)}, bf16[344,512]{1,0:T(8,128)(2,1)}, u32[]{:S(2)}, u32[]{:S(2)}) collective-permute-start(bf16[344,512]{1,0:T(8,128)(2,1)S(1)} %get-tuple-element.46), channel_id=1, source_target_pairs={{0,0},{2,2},{20,4},{22,6},{40,8},{42,10},{60,12},{62,14},{65,1},{6... | collective-permute-start | bytes 1056776 | tf_op jit(solution)/shard_map/ppermute | solution.py:122
  42.1 2.9 %broadcast_in_dim.87 = bf16[2,4,688,512]{3,2,1,0:T(8,128)(2,1)} broadcast(bf16[688,512]{1,0:T(8,128)(2,1)S(1)} %fusion.11), dimensions={2,3} | broadcast | bytes 6340608 | tf_op jit(solution)/shard_map/broadcast_in_dim | solution.py:123
  49.0 3.7 %collective-permute-done.4 = bf16[344,512]{1,0:T(8,128)(2,1)} collective-permute-done((bf16[344,512]{1,0:T(8,128)(2,1)S(1)}, bf16[344,512]{1,0:T(8,128)(2,1)}, u32[]{:S(2)}, u32[]{:S(2)}) %collective-permute-start.4) | collective-permute-done | bytes 352288 | tf_op jit(solution)/shard_map/ppermute | solution.py:122
  63.9 2.8 %broadcast_in_dim.90 = bf16[4,2,344,512]{3,2,1,0:T(8,128)(2,1)} broadcast(bf16[344,512]{1,0:T(8,128)(2,1)} %collective-permute-done.4), dimensions={2,3} | broadcast | bytes 3170304 | tf_op jit(solution)/shard_map/broadcast_in_dim | solution.py:82
  70.0 3.0 %collective-permute-done.8 = bf16[344,512]{1,0:T(8,128)(2,1)S(1)} collective-permute-done((bf16[344,512]{1,0:T(8,128)(2,1)S(1)}, bf16[344,512]{1,0:T(8,128)(2,1)S(1)}, u32[]{:S(2)}, u32[]{:S(2)}) %collective-permute-start.8) | collective-permute-done | bytes 352288 | tf_op jit(solution)/shard_map/ppermute | solution.py:64
  73.2 2.7 %collective-permute-start.12 = (bf16[168,512]{1,0:T(8,128)(2,1)S(1)}, bf16[168,512]{1,0:T(8,128)(2,1)S(1)}, u32[]{:S(2)}, u32[]{:S(2)}) collective-permute-start(bf16[168,512]{1,0:T(8,128)(2,1)S(1)} %slice.45), channel_id=1, source_target_pairs={{0,12},{1,13},{2,14},{3,15},{4,0},{5,1},{6,2},{7,3},{8,4},{9,5},{1... | collective-permute-start | bytes 516104 | tf_op jit(solution)/shard_map/ppermute | solution.py:80
  80.1 3.6 %collective-permute-start.19 = (bf16[4,688,512]{2,1,0:T(8,128)(2,1)}, bf16[4,688,512]{2,1,0:T(8,128)(2,1)}, u32[]{:S(2)}, u32[]{:S(2)}) collective-permute-start(bf16[4,688,512]{2,1,0:T(8,128)(2,1)} %bitcast.11), channel_id=1, source_target_pairs={{0,1},{1,0},{2,3},{3,2},{4,5},{5,4},{6,7},{7,6},{8,9},{9,8},{10,11... | collective-permute-start | bytes 8454152 | tf_op jit(solution)/shard_map/ppermute | solution.py:87
  86.3 8.2 %collective-permute-start.20 = (bf16[344,512]{1,0:T(8,128)(2,1)}, bf16[344,512]{1,0:T(8,128)(2,1)S(1)}, u32[]{:S(2)}, u32[]{:S(2)}) collective-permute-start(bf16[344,512]{1,0:T(8,128)(2,1)} %get-tuple-element.37), channel_id=1, source_target_pairs={{0,0},{2,2},{20,4},{22,6},{40,8},{42,10},{60,12},{62,14},{65,1},{6... | collective-permute-start | bytes 1056776 | tf_op jit(solution)/shard_map/ppermute | solution.py:132
  98.5 15.2 %collective-permute-done.20 = bf16[344,512]{1,0:T(8,128)(2,1)S(1)} collective-permute-done((bf16[344,512]{1,0:T(8,128)(2,1)}, bf16[344,512]{1,0:T(8,128)(2,1)S(1)}, u32[]{:S(2)}, u32[]{:S(2)}) %collective-permute-start.20) | collective-permute-done | bytes 352288 | tf_op jit(solution)/shard_map/ppermute | solution.py:132
  115.2 5.0 %collective-permute-start.17 = (bf16[344,512]{1,0:T(8,128)(2,1)S(1)}, bf16[344,512]{1,0:T(8,128)(2,1)S(1)}, u32[]{:S(2)}, u32[]{:S(2)}) collective-permute-start(bf16[344,512]{1,0:T(8,128)(2,1)S(1)} %slice.46), channel_id=1, source_target_pairs={{0,16},{16,32},{32,48},{48,64},{64,80},{80,96},{96,112},{112,0},{1... | collective-permute-start | bytes 1056776 | tf_op jit(solution)/shard_map/ppermute | solution.py:137
  128.6 5.0 %fusion.1 = f32[688,688,1]{1,0,2:T(8,128)S(1)} fusion(bf16[4,688,512]{2,1,0:T(8,128)(2,1)} %bitcast.11, bf16[2,4,688,512]{3,2,1,0:T(8,128)(2,1)} %bitcast_dynamic-update-slice_fusion.12), kind=kOutput, calls=%fused_computation.3 | convolution fusion | flops 1938817024 | bytes 7529472 | tf_op jit(solution)/shard_map/dot_general | solution.py:92
  133.7 5.0 %fusion.6 = bf16[688,688]{1,0:T(8,128)(2,1)S(1)} fusion(f32[688,688,1]{1,0,2:T(8,128)S(1)} %fusion.1, bf16[4,688,512]{2,1,0:T(8,128)(2,1)} %collective-permute-done.19, bf16[2,4,688,512]{3,2,1,0:T(8,128)(2,1)} %bitcast_dynamic-update-slice_fusion.12), kind=kOutput, calls=%fused_computation.10 | convolution fusion | flops 1939763712 | bytes 8476160 | tf_op jit(solution)/shard_map/dot_general | solution.py:92
  139.3 3.0 %collective-permute-start.28 = (bf16[168,512]{1,0:T(8,128)(2,1)S(1)}, bf16[168,512]{1,0:T(8,128)(2,1)S(1)}, u32[]{:S(2)}, u32[]{:S(2)}) collective-permute-start(bf16[168,512]{1,0:T(8,128)(2,1)S(1)} %slice.41), channel_id=1, source_target_pairs={{0,12},{1,13},{2,14},{3,15},{4,0},{5,1},{6,2},{7,3},{8,4},{9,5},{1... | collective-permute-start | bytes 516104 | tf_op jit(solution)/shard_map/ppermute | solution.py:80
  142.3 2.7 %collective-permute-done.27 = bf16[176,512]{1,0:T(8,128)(2,1)S(1)} collective-permute-done((bf16[176,512]{1,0:T(8,128)(2,1)S(1)}, bf16[176,512]{1,0:T(8,128)(2,1)S(1)}, u32[]{:S(2)}, u32[]{:S(2)}) %collective-permute-start.27) | collective-permute-done | bytes 180256 | tf_op jit(solution)/shard_map/ppermute | solution.py:79
  145.0 7.5 %collective-permute-start.29 = (bf16[4,688,512]{2,1,0:T(8,128)(2,1)S(1)}, bf16[4,688,512]{2,1,0:T(8,128)(2,1)S(1)}, u32[]{:S(2)}, u32[]{:S(2)}) collective-permute-start(bf16[4,688,512]{2,1,0:T(8,128)(2,1)S(1)} %bitcast.97), channel_id=1, source_target_pairs={{0,1},{1,0},{2,3},{3,2},{4,5},{5,4},{6,7},{7,6},{8,9},{9,8},{10,11... | collective-permute-start | bytes 8454152 | tf_op jit(solution)/shard_map/ppermute | solution.py:87
  154.8 4.2 %fusion = f32[688,688,1]{1,0,2:T(8,128)S(1)} fusion(bf16[4,688,512]{2,1,0:T(8,128)(2,1)S(1)} %bitcast.98, bf16[2,4,688,512]{3,2,1,0:T(8,128)(2,1)} %bitcast_dynamic-update-slice_fusion.12), kind=kOutput, calls=%fused_computation.2 | convolution fusion | flops 1938817024 | bytes 7529472 | tf_op jit(solution)/shard_map/dot_general | solution.py:92
  158.9 20.0 %collective-permute-done.30 = bf16[688,688]{1,0:T(8,128)(2,1)S(1)} collective-permute-done((bf16[688,688]{1,0:T(8,128)(2,1)S(1)}, bf16[688,688]{1,0:T(8,128)(2,1)S(1)}, u32[]{:S(2)}, u32[]{:S(2)}) %collective-permute-start.30) | collective-permute-done | bytes 946720 | tf_op jit(solution)/shard_map/ppermute | solution.py:142
  178.9 5.5 %fusion.5 = f32[688,688]{1,0:T(8,128)} fusion(f32[688,688,1]{1,0,2:T(8,128)S(1)} %fusion, bf16[688,688]{1,0:T(8,128)(2,1)S(1)} %collective-permute-done.30, bf16[4,688,512]{2,1,0:T(8,128)(2,1)S(1)} %collective-permute-done.29, bf16[2,4,688,512]{3,2,1,0:T(8,128)(2,1)} %bitcast_dynamic-update-slice_fusion.12), kind=kOutput, calls=%fused_computation.8 | convolution fusion | flops 1940710400 | bytes 10369536 | tf_op jit(solution)/shard_map/dot_general | solution.py:92
  (80 shorter events, 49.2 us)
Async XLA Ops:
  5.4 30.1 %collective-permute-start.2 = (bf16[688,512]{1,0:T(8,128)(2,1)S(1)}, bf16[688,512]{1,0:T(8,128)(2,1)}, u32[]{:S(2)}, u32[]{:S(2)}) collective-permute-start(bf16[688,512]{1,0:T(8,128)(2,1)S(1)} %fusion.11), channel_id=1, source_target_pairs={{0,16},{16,32},{32,48},{48,64},{64,80},{80,96},{96,112},{112,0},{1... | collective-permute-start | bytes 2113544 | tf_op jit(solution)/shard_map/ppermute | solution.py:116
  7.9 27.6 %collective-permute-start.3 = (bf16[688,512]{1,0:T(8,128)(2,1)S(1)}, bf16[688,512]{1,0:T(8,128)(2,1)}, u32[]{:S(2)}, u32[]{:S(2)}) collective-permute-start(bf16[688,512]{1,0:T(8,128)(2,1)S(1)} %fusion.11), channel_id=1, source_target_pairs={{0,112},{16,0},{32,16},{48,32},{64,48},{80,64},{96,80},{112,96},{1... | collective-permute-start | bytes 2113544 | tf_op jit(solution)/shard_map/ppermute | solution.py:116
  12.8 11.7 %collective-permute-start = (bf16[344,512]{1,0:T(8,128)(2,1)}, bf16[344,512]{1,0:T(8,128)(2,1)}, u32[]{:S(2)}, u32[]{:S(2)}) collective-permute-start(bf16[344,512]{1,0:T(8,128)(2,1)} %get-tuple-element.48), channel_id=1, source_target_pairs={{0,0},{1,5},{2,9},{3,13},{4,1},{5,12},{6,8},{7,4},{8,2},{9,7},{10,... | collective-permute-start | bytes 1056776 | tf_op jit(solution)/shard_map/ppermute | solution.py:114
  16.0 19.5 %collective-permute-start.1 = (bf16[344,512]{1,0:T(8,128)(2,1)}, bf16[344,512]{1,0:T(8,128)(2,1)}, u32[]{:S(2)}, u32[]{:S(2)}) collective-permute-start(bf16[344,512]{1,0:T(8,128)(2,1)} %get-tuple-element.47), channel_id=1, source_target_pairs={{0,2},{1,7},{2,11},{3,15},{4,3},{5,14},{6,10},{7,6},{8,0},{9,5},{1... | collective-permute-start | bytes 1056776 | tf_op jit(solution)/shard_map/ppermute | solution.py:114
  37.3 15.4 %collective-permute-start.4 = (bf16[344,512]{1,0:T(8,128)(2,1)S(1)}, bf16[344,512]{1,0:T(8,128)(2,1)}, u32[]{:S(2)}, u32[]{:S(2)}) collective-permute-start(bf16[344,512]{1,0:T(8,128)(2,1)S(1)} %get-tuple-element.46), channel_id=1, source_target_pairs={{0,0},{2,2},{20,4},{22,6},{40,8},{42,10},{60,12},{62,14},{65,1},{6... | collective-permute-start | bytes 1056776 | tf_op jit(solution)/shard_map/ppermute | solution.py:122
  52.7 9.3 %collective-permute-start.5 = (bf16[344,512]{1,0:T(8,128)(2,1)}, bf16[344,512]{1,0:T(8,128)(2,1)}, u32[]{:S(2)}, u32[]{:S(2)}) collective-permute-start(bf16[344,512]{1,0:T(8,128)(2,1)} %collective-permute-done.4), channel_id=1, source_target_pairs={{0,4},{1,5},{2,6},{3,7},{4,8},{5,9},{6,10},{7,11},{8,12},{9,13},{1... | collective-permute-start | bytes 1056776 | tf_op jit(solution)/shard_map/ppermute | solution.py:62
  54.2 9.4 %collective-permute-start.7 = (bf16[344,512]{1,0:T(8,128)(2,1)}, bf16[344,512]{1,0:T(8,128)(2,1)S(1)}, u32[]{:S(2)}, u32[]{:S(2)}) collective-permute-start(bf16[344,512]{1,0:T(8,128)(2,1)} %collective-permute-done.4), channel_id=1, source_target_pairs={{0,2},{1,3},{2,0},{3,1},{4,6},{5,7},{6,4},{7,5},{8,10},{9,11},{10,... | collective-permute-start | bytes 1056776 | tf_op jit(solution)/shard_map/ppermute | solution.py:63
  54.2 29.4 %collective-permute-start.13 = (bf16[688,512]{1,0:T(8,128)(2,1)}, bf16[688,512]{1,0:T(8,128)(2,1)}, u32[]{:S(2)}, u32[]{:S(2)}) collective-permute-start(bf16[688,512]{1,0:T(8,128)(2,1)} %collective-permute-done.2), channel_id=1, source_target_pairs={{0,16},{16,32},{32,48},{48,64},{64,80},{80,96},{96,112},{112,0},{1... | collective-permute-start | bytes 2113544 | tf_op jit(solution)/shard_map/ppermute | solution.py:128
  54.4 29.3 %collective-permute-start.14 = (bf16[688,512]{1,0:T(8,128)(2,1)}, bf16[688,512]{1,0:T(8,128)(2,1)}, u32[]{:S(2)}, u32[]{:S(2)}) collective-permute-start(bf16[688,512]{1,0:T(8,128)(2,1)} %collective-permute-done.3), channel_id=1, source_target_pairs={{0,112},{16,0},{32,16},{48,32},{64,48},{80,64},{96,80},{112,96},{1... | collective-permute-start | bytes 2113544 | tf_op jit(solution)/shard_map/ppermute | solution.py:128
  59.4 17.2 %collective-permute-start.9 = (bf16[344,512]{1,0:T(8,128)(2,1)S(1)}, bf16[344,512]{1,0:T(8,128)(2,1)S(1)}, u32[]{:S(2)}, u32[]{:S(2)}) collective-permute-start(bf16[344,512]{1,0:T(8,128)(2,1)S(1)} %collective-permute-done.6), channel_id=1, source_target_pairs={{0,12},{1,13},{2,14},{3,15},{4,0},{5,1},{6,2},{7,3},{8,4},{9,5},{1... | collective-permute-start | bytes 1056776 | tf_op jit(solution)/shard_map/ppermute | solution.py:65
  62.0 11.1 %collective-permute-start.10 = (bf16[344,512]{1,0:T(8,128)(2,1)S(1)}, bf16[344,512]{1,0:T(8,128)(2,1)S(1)}, u32[]{:S(2)}, u32[]{:S(2)}) collective-permute-start(bf16[344,512]{1,0:T(8,128)(2,1)S(1)} %collective-permute-done.6), channel_id=1, source_target_pairs={{0,2},{1,3},{2,0},{3,1},{4,6},{5,7},{6,4},{7,5},{8,10},{9,11},{10,... | collective-permute-start | bytes 1056776 | tf_op jit(solution)/shard_map/ppermute | solution.py:66
  63.6 9.4 %collective-permute-start.8 = (bf16[344,512]{1,0:T(8,128)(2,1)S(1)}, bf16[344,512]{1,0:T(8,128)(2,1)S(1)}, u32[]{:S(2)}, u32[]{:S(2)}) collective-permute-start(bf16[344,512]{1,0:T(8,128)(2,1)S(1)} %collective-permute-done.7), channel_id=1, source_target_pairs={{0,4},{1,5},{2,6},{3,7},{4,8},{5,9},{6,10},{7,11},{8,12},{9,13},{1... | collective-permute-start | bytes 1056776 | tf_op jit(solution)/shard_map/ppermute | solution.py:64
  80.1 53.6 %collective-permute-start.19 = (bf16[4,688,512]{2,1,0:T(8,128)(2,1)}, bf16[4,688,512]{2,1,0:T(8,128)(2,1)}, u32[]{:S(2)}, u32[]{:S(2)}) collective-permute-start(bf16[4,688,512]{2,1,0:T(8,128)(2,1)} %bitcast.11), channel_id=1, source_target_pairs={{0,1},{1,0},{2,3},{3,2},{4,5},{5,4},{6,7},{7,6},{8,9},{9,8},{10,11... | collective-permute-start | bytes 8454152 | tf_op jit(solution)/shard_map/ppermute | solution.py:87
  83.6 31.5 %collective-permute-start.15 = (bf16[688,512]{1,0:T(8,128)(2,1)}, bf16[688,512]{1,0:T(8,128)(2,1)S(1)}, u32[]{:S(2)}, u32[]{:S(2)}) collective-permute-start(bf16[688,512]{1,0:T(8,128)(2,1)} %collective-permute-done.13), channel_id=1, source_target_pairs={{0,16},{16,32},{32,48},{48,64},{64,80},{80,96},{96,112},{112,0},{1... | collective-permute-start | bytes 2113544 | tf_op jit(solution)/shard_map/ppermute | solution.py:134
  84.0 36.2 %collective-permute-start.16 = (bf16[688,512]{1,0:T(8,128)(2,1)}, bf16[688,512]{1,0:T(8,128)(2,1)}, u32[]{:S(2)}, u32[]{:S(2)}) collective-permute-start(bf16[688,512]{1,0:T(8,128)(2,1)} %collective-permute-done.14), channel_id=1, source_target_pairs={{0,112},{16,0},{32,16},{48,32},{64,48},{80,64},{96,80},{112,96},{1... | collective-permute-start | bytes 2113544 | tf_op jit(solution)/shard_map/ppermute | solution.py:134
  86.3 27.4 %collective-permute-start.20 = (bf16[344,512]{1,0:T(8,128)(2,1)}, bf16[344,512]{1,0:T(8,128)(2,1)S(1)}, u32[]{:S(2)}, u32[]{:S(2)}) collective-permute-start(bf16[344,512]{1,0:T(8,128)(2,1)} %get-tuple-element.37), channel_id=1, source_target_pairs={{0,0},{2,2},{20,4},{22,6},{40,8},{42,10},{60,12},{62,14},{65,1},{6... | collective-permute-start | bytes 1056776 | tf_op jit(solution)/shard_map/ppermute | solution.py:132
  113.8 14.0 %collective-permute-start.23 = (bf16[344,512]{1,0:T(8,128)(2,1)S(1)}, bf16[344,512]{1,0:T(8,128)(2,1)S(1)}, u32[]{:S(2)}, u32[]{:S(2)}) collective-permute-start(bf16[344,512]{1,0:T(8,128)(2,1)S(1)} %collective-permute-done.20), channel_id=1, source_target_pairs={{0,2},{1,3},{2,0},{3,1},{4,6},{5,7},{6,4},{7,5},{8,10},{9,11},{10,... | collective-permute-start | bytes 1056776 | tf_op jit(solution)/shard_map/ppermute | solution.py:63
  115.2 9.3 %collective-permute-start.17 = (bf16[344,512]{1,0:T(8,128)(2,1)S(1)}, bf16[344,512]{1,0:T(8,128)(2,1)S(1)}, u32[]{:S(2)}, u32[]{:S(2)}) collective-permute-start(bf16[344,512]{1,0:T(8,128)(2,1)S(1)} %slice.46), channel_id=1, source_target_pairs={{0,16},{16,32},{32,48},{48,64},{64,80},{80,96},{96,112},{112,0},{1... | collective-permute-start | bytes 1056776 | tf_op jit(solution)/shard_map/ppermute | solution.py:137
  124.3 14.4 %collective-permute-start.21 = (bf16[344,512]{1,0:T(8,128)(2,1)S(1)}, bf16[344,512]{1,0:T(8,128)(2,1)S(1)}, u32[]{:S(2)}, u32[]{:S(2)}) collective-permute-start(bf16[344,512]{1,0:T(8,128)(2,1)S(1)} %collective-permute-done.20), channel_id=1, source_target_pairs={{0,4},{1,5},{2,6},{3,7},{4,8},{5,9},{6,10},{7,11},{8,12},{9,13},{1... | collective-permute-start | bytes 1056776 | tf_op jit(solution)/shard_map/ppermute | solution.py:62
  124.5 14.2 %collective-permute-start.25 = (bf16[344,512]{1,0:T(8,128)(2,1)S(1)}, bf16[344,512]{1,0:T(8,128)(2,1)S(1)}, u32[]{:S(2)}, u32[]{:S(2)}) collective-permute-start(bf16[344,512]{1,0:T(8,128)(2,1)S(1)} %collective-permute-done.22), channel_id=1, source_target_pairs={{0,12},{1,13},{2,14},{3,15},{4,0},{5,1},{6,2},{7,3},{8,4},{9,5},{1... | collective-permute-start | bytes 1056776 | tf_op jit(solution)/shard_map/ppermute | solution.py:65
  127.8 11.0 %collective-permute-start.26 = (bf16[344,512]{1,0:T(8,128)(2,1)S(1)}, bf16[344,512]{1,0:T(8,128)(2,1)S(1)}, u32[]{:S(2)}, u32[]{:S(2)}) collective-permute-start(bf16[344,512]{1,0:T(8,128)(2,1)S(1)} %collective-permute-done.22), channel_id=1, source_target_pairs={{0,2},{1,3},{2,0},{3,1},{4,6},{5,7},{6,4},{7,5},{8,10},{9,11},{10,... | collective-permute-start | bytes 1056776 | tf_op jit(solution)/shard_map/ppermute | solution.py:66
  127.8 10.9 %collective-permute-start.24 = (bf16[344,512]{1,0:T(8,128)(2,1)S(1)}, bf16[344,512]{1,0:T(8,128)(2,1)S(1)}, u32[]{:S(2)}, u32[]{:S(2)}) collective-permute-start(bf16[344,512]{1,0:T(8,128)(2,1)S(1)} %collective-permute-done.23), channel_id=1, source_target_pairs={{0,4},{1,5},{2,6},{3,7},{4,8},{5,9},{6,10},{7,11},{8,12},{9,13},{1... | collective-permute-start | bytes 1056776 | tf_op jit(solution)/shard_map/ppermute | solution.py:64
  145.0 33.9 %collective-permute-start.29 = (bf16[4,688,512]{2,1,0:T(8,128)(2,1)S(1)}, bf16[4,688,512]{2,1,0:T(8,128)(2,1)S(1)}, u32[]{:S(2)}, u32[]{:S(2)}) collective-permute-start(bf16[4,688,512]{2,1,0:T(8,128)(2,1)S(1)} %bitcast.97), channel_id=1, source_target_pairs={{0,1},{1,0},{2,3},{3,2},{4,5},{5,4},{6,7},{7,6},{8,9},{9,8},{10,11... | collective-permute-start | bytes 8454152 | tf_op jit(solution)/shard_map/ppermute | solution.py:87
  152.5 26.4 %collective-permute-start.30 = (bf16[688,688]{1,0:T(8,128)(2,1)S(1)}, bf16[688,688]{1,0:T(8,128)(2,1)S(1)}, u32[]{:S(2)}, u32[]{:S(2)}) collective-permute-start(bf16[688,688]{1,0:T(8,128)(2,1)S(1)} %fusion.6), channel_id=1, source_target_pairs={{0,128},{16,144},{32,160},{48,176},{64,192},{80,208},{96,224},{112... | collective-permute-start | bytes 2840072 | tf_op jit(solution)/shard_map/ppermute | solution.py:142
  (8 other events, 47.5 us)

commit v5 on v4

v5 whole, which is shorter than its diff:
```python
import jax
import jax.numpy as jnp
from jax import lax
from jax.sharding import PartitionSpec as P

BOTH = ("dp", "tensor")
RING = 8
PLACES = (0, 4, 1, 7, 2, 6, 3, 5)


def place(offset, half):
    k = PLACES.index(offset)
    return (k // 2) * 4 + half * 2 + k % 2


def in_plane(turn):
    pairs = []
    for h in range(2):
        for source in range(RING):
            for b in range(2):
                for z in range(RING):
                    plane = (h * RING + source) * 16
                    pairs.append((plane + b * RING + z, plane + place((source - z) % RING, b ^ turn)))
    return pairs


def shifted():
    pairs = []
    for h in range(2):
        for z in range(RING):
            for offset in range(RING):
                for half in range(2):
                    t = place(offset, half)
                    pairs.append(((h * RING + (z + offset) % RING) * 16 + t, (h * RING + z) * 16 + t))
    return pairs


def along_z(step):
    return [(h * RING + z, h * RING + (z + step) % RING) for h in range(2) for z in range(RING)]


ACROSS = [(i, (i + RING) % 16) for i in range(16)]


def along_x(step):
    return [
        ((x * 2 + y) * 2 + c, ((x + step) % 4 * 2 + y) * 2 + c)
        for x in range(4) for y in range(2) for c in range(2)
    ]


ACROSS_Y = [(t, t ^ 2) for t in range(16)]
ACROSS_CORE = [(t, t ^ 1) for t in range(16)]
def neighbours(piece):
    return [
        lax.ppermute(piece, "tensor", pairs) for pairs in (along_x(1), along_x(-1), ACROSS_Y)
    ]


def second(before, after, beside):
    return [
        lax.ppermute(beside, "tensor", along_x(1)),
        lax.ppermute(after, "tensor", along_x(-1)),
        lax.ppermute(after, "tensor", ACROSS_Y),
    ]


def last(before_beside, far, after_beside):
    cut = far.shape[0] // 32 * 16 + 16
    return [
        lax.ppermute(before_beside[:cut], "tensor", along_x(1)),
        lax.ppermute(after_beside[cut:], "tensor", along_x(-1)),
    ]


def assembled(piece, near, middle, ends, t):
    part = piece.shape[0]
    x, y = t // 4, (t // 2) % 2
    own = jnp.broadcast_to(piece[None, None], (4, 2) + piece.shape)
    placed = zip((*near, *middle, *ends), (3, 1, 0, 3, 2, 1, 2, 2), (0, 0, 1, 1, 0, 1, 1, 1))
    for block, ahead, beside in placed:
        start = part - block.shape[0] if block is ends[1] else 0
        own = lax.dynamic_update_slice(
            own, block[None, None], ((x + ahead) % 4, beside ^ y, start, 0)
        )
    return own.reshape(4, 2 * part, piece.shape[1])


def product(rows, columns):
    return lax.dot_general(
        rows, columns, (((0, 2), (0, 2)), ((), ())), preferred_element_type=jnp.float32
    )


def shards(out_grad, down_weight, gate_pre):
    n, tokens = down_weight.shape[0], out_grad.shape[0]
    part = n // 2
    hidden_grad = lax.dot_general(
        down_weight, out_grad, (((1,), (1,)), ((), ())), preferred_element_type=jnp.float32
    ).astype(jnp.bfloat16)
    up_grad = (hidden_grad.astype(jnp.float32) * jax.nn.silu(gate_pre.T.astype(jnp.float32))).astype(
        jnp.bfloat16
    )
    h = lax.axis_index("dp") // RING
    t = lax.axis_index("tensor")
    b, half = t // RING, (t // 2) % 2

    low, high = up_grad[:part], up_grad[part:]
    got = [
        lax.ppermute(jnp.where((b ^ turn) == 0, low, high), BOTH, in_plane(turn)) for turn in range(2)
    ]
    up, down = lax.ppermute(up_grad, "dp", along_z(1)), lax.ppermute(up_grad, "dp", along_z(-1))
    got[0], got[1], up, down, up_grad = lax.optimization_barrier((got[0], got[1], up, down, up_grad))

    first_turn = half ^ (1 - h)
    theirs = jnp.where(first_turn == 0, got[0], got[1])
    ours = jnp.where(first_turn == 0, got[1], got[0])
    theirs = lax.ppermute(theirs, BOTH, shifted())
    early = jnp.broadcast_to(up_grad, (5, n, tokens))
    early = early.at[1].set(down).at[2].set(up)
    theirs, up, down, ours, early = lax.optimization_barrier((theirs, up, down, ours, early))

    near = neighbours(theirs)
    ours = lax.ppermute(ours, BOTH, shifted())
    near, ours, up, down = lax.optimization_barrier((near, ours, up, down))
    rows_ours = lax.all_gather(ours, "tensor", axis=0).reshape(4, 2, 2, part, tokens)

    middle = second(*near)
    up, down = lax.ppermute(up, "dp", along_z(1)), lax.ppermute(down, "dp", along_z(-1))
    early = early.at[3].set(down).at[4].set(up)
    middle, _ = lax.optimization_barrier((middle, (up, down)))

    ends = last(*middle)
    up, down = lax.ppermute(up, "dp", along_z(1)), lax.ppermute(down, "dp", along_z(-1))
    own = assembled(theirs, near, middle, ends, t)
    own, _ = lax.optimization_barrier((own, (up, down)))

    twin = lax.ppermute(own, "tensor", ACROSS_CORE)
    opposite = [
        lax.ppermute(up[:part], "dp", along_z(1)), lax.ppermute(down[part:], "dp", along_z(-1))
    ]

    twin, rows_ours = lax.optimization_barrier((twin, rows_ours))

    def their_rows(offset):
        k, core = divmod(PLACES.index(offset), 2)
        return jnp.where(t % 2 == core, own[k], twin[k])

    def our_rows(offset):
        k, core = divmod(PLACES.index(offset), 2)
        return rows_ours[k, :, core].reshape(n, tokens)

    def stacked(rows, offsets):
        return jnp.stack([rows(offset) for offset in offsets])

    partial = product(stacked(their_rows, (0, 1, 7, 2, 6)), early)
    their_late = stacked(their_rows, (3, 5, 4))
    partial, their_late, opposite = lax.optimization_barrier((partial, their_late, opposite))
    late = jnp.stack([down, up, jnp.concatenate(opposite)])
    partial += product(their_late, late)
    sent = lax.ppermute(partial.astype(jnp.bfloat16), "dp", ACROSS)
    kept = product(stacked(our_rows, (0, 1, 7, 2, 6)), early) + product(stacked(our_rows, (3, 5, 4)), late)
    total = tokens * lax.axis_size("dp")
    return (kept + sent.astype(jnp.float32)) * (1.0 / total)


def solution(mesh):
    placed = (P("dp", None), P("tensor", None), P("dp", "tensor"))
    return jax.shard_map(
        shards, mesh=mesh, in_specs=placed, out_specs=P("dp", "tensor"), check_vma=False
    )
```

time: 186 us -> 183 us (0.984)
  starting transfers between devices: 64.4 us -> 45.2 us
  between operations: 0.36 us -> 13.8 us
  other arithmetic: 2.78 us -> 12.5 us
  matrix products: 23.3 us -> 18.6 us
  local copies, waits for them, and re-layouts: 28.6 us -> 25.2 us
  waiting for transfers between devices: 65.1 us -> 67 us
    ppermute x21 -> x12, starting transfers between devices: 32.5 us -> 16.8 us  [the longest x1 3.73 us: shards(): twin = lax.ppermute(own, 'tensor', ACROSS_CORE)]
    ppermute x2, waiting for transfers between devices: 0.01 us -> 13.9 us  [shards(): lax.ppermute(up, 'dp', along_z(1))]
    dynamic_update_slice x24 -> x8, local copies, waits for them, and re-layouts: 19.7 us -> 7.93 us  [assembled(): lax.dynamic_update_slice(own, block[None, None], ((x + ahead) % 4, beside...]
    ppermute x1, waiting for transfers between devices: 15.2 us -> 5.56 us  [shards(): ours = lax.ppermute(ours, BOTH, shifted())]
    scatter x0 -> x4, local copies, waits for them, and re-layouts: none -> 7.14 us  [the longest x2 4.05 us: shards(): early = early.at[1].set(down).at[2].set(up)]
    ppermute x21 -> x12, waiting for transfers between devices: 30.6 us -> 25.7 us  [the longest x1 19 us: shards(): sent = lax.ppermute(partial.astype(jnp.bfloat16), 'dp', ACROSS)]
    dot_general x4, matrix products: 19.7 us -> 15 us  [product(): lax.dot_general(rows, columns, (((0, 2), (0, 2)), ((), ())), preferred_el...]
    unnamed x0 -> x4, other arithmetic: none -> 4.52 us
  transfers between devices with their start and end apart: 31 -> 23, of which waited for: 12 -> 12; matrix products, arithmetic and copies ran while one was open for 23% -> 22% of each run, Pallas kernels for 0% -> 0%
where the time goes in v5:
time: 183 us; the launch traced here: 182 us
  waiting for transfers between devices  67 us (37%)
  starting transfers between devices  45.2 us (25%)
  local copies, waits for them, and re-layouts  25.2 us (14%)
  matrix products  18.6 us (10%)
  between operations  13.8 us (8%)
  other arithmetic  12.5 us (7%)
    ppermute x1, waiting for transfers between devices, shards(): sent = lax.ppermute(partial.astype(jnp.bfloat16), 'dp', ACROSS)  19 us
    ppermute x2, waiting for transfers between devices, shards(): lax.ppermute(jnp.where(b ^ turn == 0, low, high), BOTH, in_plane(turn))  15.5 us
    dot_general x4, matrix products, product(): lax.dot_general(rows, columns, (((0, 2), (0, 2)), ((), ())), preferred_el...  15 us
    ppermute x2, waiting for transfers between devices, shards(): lax.ppermute(up, 'dp', along_z(1))  13.9 us
    dynamic_update_slice x8, local copies, waits for them, and re-layouts, assembled(): lax.dynamic_update_slice(own, block[None, None], ((x + ahead) % 4, beside...  7.93 us
    ppermute x2, starting transfers between devices, shards(): lax.ppermute(jnp.where(b ^ turn == 0, low, high), BOTH, in_plane(turn))  7.04 us
    ppermute x1, waiting for transfers between devices, shards(): ours = lax.ppermute(ours, BOTH, shifted())  5.56 us
    ppermute x3, waiting for transfers between devices, neighbours(): lax.ppermute(piece, 'tensor', pairs)  5.47 us
  transfers between devices with their start and end apart: 23, of which 12 were waited for; matrix products, arithmetic and copies ran while one was open for 22% of the time, Pallas kernels for 0%

profile of v5, /device:TPU:1, one launch (start us, length us, event | category | flops | bytes accessed | tf_op | source)
XLA Modules:
  0.0 182.4 jit_solution(6190640038934341426)
XLA Ops:
  8.3 3.6 %fusion.15 = bf16[688,512]{1,0:T(8,128)(2,1)S(1)} fusion(bf16[512,688]{0,1:T(8,128)(2,1)} %param.13, bf16[688,2048]{1,0:T(8,128)(2,1)S(1)} %copy-done, bf16[512,2048]{1,0:T(8,128)(2,1)} %param.11), kind=kOutput, calls=%fused_computation.20 | convolution fusion | flops 1446010880 | bytes 6324224 | tf_op jit(solution)/shard_map/dot_general | solution.py:98
  11.9 2.5 %collective-permute-start.2 = (bf16[688,512]{1,0:T(8,128)(2,1)S(1)}, bf16[688,512]{1,0:T(8,128)(2,1)}, u32[]{:S(2)}, u32[]{:S(2)}) collective-permute-start(bf16[688,512]{1,0:T(8,128)(2,1)S(1)} %fusion.15), channel_id=1, source_target_pairs={{0,16},{16,32},{32,48},{48,64},{64,80},{80,96},{96,112},{112,0},{1... | collective-permute-start | bytes 2113544 | tf_op jit(solution)/shard_map/ppermute | solution.py:112
  14.4 4.0 %collective-permute-start.3 = (bf16[688,512]{1,0:T(8,128)(2,1)S(1)}, bf16[688,512]{1,0:T(8,128)(2,1)}, u32[]{:S(2)}, u32[]{:S(2)}) collective-permute-start(bf16[688,512]{1,0:T(8,128)(2,1)S(1)} %fusion.15), channel_id=1, source_target_pairs={{0,112},{16,0},{32,16},{48,32},{64,48},{80,64},{96,80},{112,96},{1... | collective-permute-start | bytes 2113544 | tf_op jit(solution)/shard_map/ppermute | solution.py:112
  19.4 3.1 %collective-permute-start = (bf16[344,512]{1,0:T(8,128)(2,1)}, bf16[344,512]{1,0:T(8,128)(2,1)}, u32[]{:S(2)}, u32[]{:S(2)}) collective-permute-start(bf16[344,512]{1,0:T(8,128)(2,1)} %get-tuple-element.120), channel_id=1, source_target_pairs={{0,0},{1,5},{2,9},{3,13},{4,1},{5,12},{6,8},{7,4},{8,2},{9,7},{10,... | collective-permute-start | bytes 1056776 | tf_op jit(solution)/shard_map/ppermute | solution.py:110
  22.5 3.9 %collective-permute-start.1 = (bf16[344,512]{1,0:T(8,128)(2,1)}, bf16[344,512]{1,0:T(8,128)(2,1)}, u32[]{:S(2)}, u32[]{:S(2)}) collective-permute-start(bf16[344,512]{1,0:T(8,128)(2,1)} %get-tuple-element.119), channel_id=1, source_target_pairs={{0,2},{1,7},{2,11},{3,15},{4,3},{5,14},{6,10},{7,6},{8,0},{9,5},{1... | collective-permute-start | bytes 1056776 | tf_op jit(solution)/shard_map/ppermute | solution.py:110
  26.5 4.6 %collective-permute-done = bf16[344,512]{1,0:T(8,128)(2,1)} collective-permute-done((bf16[344,512]{1,0:T(8,128)(2,1)}, bf16[344,512]{1,0:T(8,128)(2,1)}, u32[]{:S(2)}, u32[]{:S(2)}) %collective-permute-start) | collective-permute-done | bytes 352288 | tf_op jit(solution)/shard_map/ppermute | solution.py:110
  31.1 10.9 %collective-permute-done.1 = bf16[344,512]{1,0:T(8,128)(2,1)} collective-permute-done((bf16[344,512]{1,0:T(8,128)(2,1)}, bf16[344,512]{1,0:T(8,128)(2,1)}, u32[]{:S(2)}, u32[]{:S(2)}) %collective-permute-start.1) | collective-permute-done | bytes 352288 | tf_op jit(solution)/shard_map/ppermute | solution.py:110
  43.1 4.7 %collective-permute-start.4 = (bf16[344,512]{1,0:T(8,128)(2,1)S(1)}, bf16[344,512]{1,0:T(8,128)(2,1)S(1)}, u32[]{:S(2)}, u32[]{:S(2)}) collective-permute-start(bf16[344,512]{1,0:T(8,128)(2,1)S(1)} %get-tuple-element.118), channel_id=1, source_target_pairs={{0,0},{2,2},{20,4},{22,6},{40,8},{42,10},{60,12},{62,14},{65,1},{6... | collective-permute-start | bytes 1056776 | tf_op jit(solution)/shard_map/ppermute | solution.py:118
  54.1 4.4 %collective-permute-done.4 = bf16[344,512]{1,0:T(8,128)(2,1)S(1)} collective-permute-done((bf16[344,512]{1,0:T(8,128)(2,1)S(1)}, bf16[344,512]{1,0:T(8,128)(2,1)S(1)}, u32[]{:S(2)}, u32[]{:S(2)}) %collective-permute-start.4) | collective-permute-done | bytes 352288 | tf_op jit(solution)/shard_map/ppermute | solution.py:118
  58.5 2.7 %collective-permute-start.6 = (bf16[344,512]{1,0:T(8,128)(2,1)S(1)}, bf16[344,512]{1,0:T(8,128)(2,1)}, u32[]{:S(2)}, u32[]{:S(2)}) collective-permute-start(bf16[344,512]{1,0:T(8,128)(2,1)S(1)} %collective-permute-done.4), channel_id=1, source_target_pairs={{0,12},{1,13},{2,14},{3,15},{4,0},{5,1},{6,2},{7,3},{8,4},{9,5},{1... | collective-permute-start | bytes 1056776 | tf_op jit(solution)/shard_map/ppermute | solution.py:56
  61.2 4.7 %collective-permute-start.8 = (bf16[344,512]{1,0:T(8,128)(2,1)S(1)}, bf16[344,512]{1,0:T(8,128)(2,1)S(1)}, u32[]{:S(2)}, u32[]{:S(2)}) collective-permute-start(bf16[344,512]{1,0:T(8,128)(2,1)S(1)} %get-tuple-element.85), channel_id=1, source_target_pairs={{0,0},{2,2},{20,4},{22,6},{40,8},{42,10},{60,12},{62,14},{65,1},{6... | collective-permute-start | bytes 1056776 | tf_op jit(solution)/shard_map/ppermute | solution.py:124
  65.9 3.1 %collective-permute-done.5 = bf16[344,512]{1,0:T(8,128)(2,1)S(1)} collective-permute-done((bf16[344,512]{1,0:T(8,128)(2,1)S(1)}, bf16[344,512]{1,0:T(8,128)(2,1)S(1)}, u32[]{:S(2)}, u32[]{:S(2)}) %collective-permute-start.5) | collective-permute-done | bytes 352288 | tf_op jit(solution)/shard_map/ppermute | solution.py:56
  69.0 2.3 %collective-permute-done.7 = bf16[344,512]{1,0:T(8,128)(2,1)} collective-permute-done((bf16[344,512]{1,0:T(8,128)(2,1)S(1)}, bf16[344,512]{1,0:T(8,128)(2,1)}, u32[]{:S(2)}, u32[]{:S(2)}) %collective-permute-start.7) | collective-permute-done | bytes 352288 | tf_op jit(solution)/shard_map/ppermute | solution.py:56
  71.3 5.6 %collective-permute-done.8 = bf16[344,512]{1,0:T(8,128)(2,1)S(1)} collective-permute-done((bf16[344,512]{1,0:T(8,128)(2,1)S(1)}, bf16[344,512]{1,0:T(8,128)(2,1)S(1)}, u32[]{:S(2)}, u32[]{:S(2)}) %collective-permute-start.8) | collective-permute-done | bytes 352288 | tf_op jit(solution)/shard_map/ppermute | solution.py:124
  83.5 2.8 %broadcast_in_dim.34 = bf16[4,2,344,512]{3,2,1,0:T(8,128)(2,1)} broadcast(bf16[344,512]{1,0:T(8,128)(2,1)} %copy-done.2), dimensions={2,3} | broadcast | bytes 3170304 | tf_op jit(solution)/shard_map/broadcast_in_dim | solution.py:79
  90.5 5.7 %collective-permute-done.12 = bf16[688,512]{1,0:T(8,128)(2,1)S(1)} collective-permute-done((bf16[688,512]{1,0:T(8,128)(2,1)}, bf16[688,512]{1,0:T(8,128)(2,1)S(1)}, u32[]{:S(2)}, u32[]{:S(2)}) %collective-permute-start.12) | collective-permute-done | bytes 704544 | tf_op jit(solution)/shard_map/ppermute | solution.py:129
  108.5 8.2 %collective-permute-done.16 = bf16[688,512]{1,0:T(8,128)(2,1)S(1)} collective-permute-done((bf16[688,512]{1,0:T(8,128)(2,1)S(1)}, bf16[688,512]{1,0:T(8,128)(2,1)S(1)}, u32[]{:S(2)}, u32[]{:S(2)}) %collective-permute-start.16) | collective-permute-done | bytes 704544 | tf_op jit(solution)/shard_map/ppermute | solution.py:134
  118.5 3.7 %collective-permute-start.18 = (bf16[4,688,512]{2,1,0:T(8,128)(2,1)}, bf16[4,688,512]{2,1,0:T(8,128)(2,1)}, u32[]{:S(2)}, u32[]{:S(2)}) collective-permute-start(bf16[4,688,512]{2,1,0:T(8,128)(2,1)} %bitcast.11), channel_id=1, source_target_pairs={{0,1},{1,0},{2,3},{3,2},{4,5},{5,4},{6,7},{7,6},{8,9},{9,8},{10,11... | collective-permute-start | bytes 8454152 | tf_op jit(solution)/shard_map/ppermute | solution.py:138
  125.5 2.7 %collective-permute-start.20 = (bf16[344,512]{1,0:T(8,128)(2,1)S(1)}, bf16[344,512]{1,0:T(8,128)(2,1)}, u32[]{:S(2)}, u32[]{:S(2)}) collective-permute-start(bf16[344,512]{1,0:T(8,128)(2,1)S(1)} %slice.178), channel_id=1, source_target_pairs={{0,112},{16,0},{32,16},{48,32},{64,48},{80,64},{96,80},{112,96},{1... | collective-permute-start | bytes 1056776 | tf_op jit(solution)/shard_map/ppermute | solution.py:140
  131.2 2.8 %broadcast_select_fusion.2 = (bf16[1,688,512]{2,1,0:T(8,128)(2,1)S(1)}, bf16[1,688,512]{2,1,0:T(8,128)(2,1)S(1)}, bf16[5,688,512]{2,1,0:T(8,128)(2,1)S(1)}, bf16[1,688,512]{2,1,0:T(8,128)(2,1)S(1)}) fusion(pred[]{:T(512)S(6)} %eq.44, bf16[4,688,512]{2,1,0:T(8,128)(2,1)} %collective-permute-done.18, bf16[4,688,512]{2,1,0:T(8,128)(2,1)} %bitcast.11, ...), kind=kLoop, calls=%fused_computation.34 | loop fusion | flops 1409024 | bytes 7045122 | tf_op jit(solution)/shard_map/jit(_where)/select_n | solution.py:147
  137.2 5.0 %convolution_bitcast_fusion = f32[688,688]{1,0:T(8,128)S(1)} fusion(bf16[5,688,512]{2,1,0:T(8,128)(2,1)S(1)} %select_dynamic-update-slice_fusion, bf16[5,688,512]{2,1,0:T(8,128)(2,1)} %bitcast_dynamic-update-slice_fusion), kind=kOutput, calls=%fused_computation.13 | convolution fusion | flops 2423521280 | bytes 8938496 | tf_op jit(solution)/shard_map/dot_general | solution.py:90
  148.4 4.9 %fusion.19 = f32[688,688,1]{1,0,2:T(8,128)S(1)} fusion(bf16[5,688,512]{2,1,0:T(8,128)(2,1)S(1)} %constant_dynamic-update-slice_fusion, bf16[5,688,512]{2,1,0:T(8,128)(2,1)} %bitcast_dynamic-update-slice_fusion), kind=kOutput, calls=%fused_computation.55 | convolution fusion | flops 2423521280 | bytes 8938496 | tf_op jit(solution)/shard_map/dot_general | solution.py:90
  153.3 19.0 %collective-permute-done.21 = bf16[688,688]{1,0:T(8,128)(2,1)S(1)} collective-permute-done((bf16[688,688]{1,0:T(8,128)(2,1)S(1)}, bf16[688,688]{1,0:T(8,128)(2,1)S(1)}, u32[]{:S(2)}, u32[]{:S(2)}) %collective-permute-start.21) | collective-permute-done | bytes 946720 | tf_op jit(solution)/shard_map/ppermute | solution.py:161
  172.3 3.2 %fusion.8 = f32[688,688]{1,0:T(8,128)} fusion(f32[688,688,1]{1,0,2:T(8,128)S(1)} %fusion.19, bf16[688,688]{1,0:T(8,128)(2,1)S(1)} %collective-permute-done.21, bf16[1,688,512]{2,1,0:T(8,128)(2,1)S(1)} %bitcast.83, bf16[1,688,512]{2,1,0:T(8,128)(2,1)S(1)} %bitcast.84, bf16[1,688,512]{2,1,0:T(8,128)(2,1)S(1)} %bitcast.82, ...), kind=kOutput, calls=%fused_computation.12 | convolution fusion | flops 1460233216 | bytes 8960512 | tf_op jit(solution)/shard_map/dot_general | solution.py:90
  (90 shorter events, 50.2 us)
Async XLA Ops:
  6.5 121.7 %all-gather.3.cloned.1.call-start = ((), (), s32[]{:S(2)}) async-start(), calls=%async_computation | async-start | bytes 5988352 | tf_op jit(solution)/shard_map/all_gather | solution.py:126
  11.9 30.1 %collective-permute-start.2 = (bf16[688,512]{1,0:T(8,128)(2,1)S(1)}, bf16[688,512]{1,0:T(8,128)(2,1)}, u32[]{:S(2)}, u32[]{:S(2)}) collective-permute-start(bf16[688,512]{1,0:T(8,128)(2,1)S(1)} %fusion.15), channel_id=1, source_target_pairs={{0,16},{16,32},{32,48},{48,64},{64,80},{80,96},{96,112},{112,0},{1... | collective-permute-start | bytes 2113544 | tf_op jit(solution)/shard_map/ppermute | solution.py:112
  14.4 27.6 %collective-permute-start.3 = (bf16[688,512]{1,0:T(8,128)(2,1)S(1)}, bf16[688,512]{1,0:T(8,128)(2,1)}, u32[]{:S(2)}, u32[]{:S(2)}) collective-permute-start(bf16[688,512]{1,0:T(8,128)(2,1)S(1)} %fusion.15), channel_id=1, source_target_pairs={{0,112},{16,0},{32,16},{48,32},{64,48},{80,64},{96,80},{112,96},{1... | collective-permute-start | bytes 2113544 | tf_op jit(solution)/shard_map/ppermute | solution.py:112
  19.4 11.7 %collective-permute-start = (bf16[344,512]{1,0:T(8,128)(2,1)}, bf16[344,512]{1,0:T(8,128)(2,1)}, u32[]{:S(2)}, u32[]{:S(2)}) collective-permute-start(bf16[344,512]{1,0:T(8,128)(2,1)} %get-tuple-element.120), channel_id=1, source_target_pairs={{0,0},{1,5},{2,9},{3,13},{4,1},{5,12},{6,8},{7,4},{8,2},{9,7},{10,... | collective-permute-start | bytes 1056776 | tf_op jit(solution)/shard_map/ppermute | solution.py:110
  22.5 19.5 %collective-permute-start.1 = (bf16[344,512]{1,0:T(8,128)(2,1)}, bf16[344,512]{1,0:T(8,128)(2,1)}, u32[]{:S(2)}, u32[]{:S(2)}) collective-permute-start(bf16[344,512]{1,0:T(8,128)(2,1)} %get-tuple-element.119), channel_id=1, source_target_pairs={{0,2},{1,7},{2,11},{3,15},{4,3},{5,14},{6,10},{7,6},{8,0},{9,5},{1... | collective-permute-start | bytes 1056776 | tf_op jit(solution)/shard_map/ppermute | solution.py:110
  43.1 15.3 %collective-permute-start.4 = (bf16[344,512]{1,0:T(8,128)(2,1)S(1)}, bf16[344,512]{1,0:T(8,128)(2,1)S(1)}, u32[]{:S(2)}, u32[]{:S(2)}) collective-permute-start(bf16[344,512]{1,0:T(8,128)(2,1)S(1)} %get-tuple-element.118), channel_id=1, source_target_pairs={{0,0},{2,2},{20,4},{22,6},{40,8},{42,10},{60,12},{62,14},{65,1},{6... | collective-permute-start | bytes 1056776 | tf_op jit(solution)/shard_map/ppermute | solution.py:118
  58.5 10.5 %collective-permute-start.5 = (bf16[344,512]{1,0:T(8,128)(2,1)S(1)}, bf16[344,512]{1,0:T(8,128)(2,1)S(1)}, u32[]{:S(2)}, u32[]{:S(2)}) collective-permute-start(bf16[344,512]{1,0:T(8,128)(2,1)S(1)} %collective-permute-done.4), channel_id=1, source_target_pairs={{0,4},{1,5},{2,6},{3,7},{4,8},{5,9},{6,10},{7,11},{8,12},{9,13},{1... | collective-permute-start | bytes 1056776 | tf_op jit(solution)/shard_map/ppermute | solution.py:56
  58.5 10.5 %collective-permute-start.6 = (bf16[344,512]{1,0:T(8,128)(2,1)S(1)}, bf16[344,512]{1,0:T(8,128)(2,1)}, u32[]{:S(2)}, u32[]{:S(2)}) collective-permute-start(bf16[344,512]{1,0:T(8,128)(2,1)S(1)} %collective-permute-done.4), channel_id=1, source_target_pairs={{0,12},{1,13},{2,14},{3,15},{4,0},{5,1},{6,2},{7,3},{8,4},{9,5},{1... | collective-permute-start | bytes 1056776 | tf_op jit(solution)/shard_map/ppermute | solution.py:56
  61.2 10.2 %collective-permute-start.7 = (bf16[344,512]{1,0:T(8,128)(2,1)S(1)}, bf16[344,512]{1,0:T(8,128)(2,1)}, u32[]{:S(2)}, u32[]{:S(2)}) collective-permute-start(bf16[344,512]{1,0:T(8,128)(2,1)S(1)} %collective-permute-done.4), channel_id=1, source_target_pairs={{0,2},{1,3},{2,0},{3,1},{4,6},{5,7},{6,4},{7,5},{8,10},{9,11},{10,... | collective-permute-start | bytes 1056776 | tf_op jit(solution)/shard_map/ppermute | solution.py:56
  61.2 15.8 %collective-permute-start.8 = (bf16[344,512]{1,0:T(8,128)(2,1)S(1)}, bf16[344,512]{1,0:T(8,128)(2,1)S(1)}, u32[]{:S(2)}, u32[]{:S(2)}) collective-permute-start(bf16[344,512]{1,0:T(8,128)(2,1)S(1)} %get-tuple-element.85), channel_id=1, source_target_pairs={{0,0},{2,2},{20,4},{22,6},{40,8},{42,10},{60,12},{62,14},{65,1},{6... | collective-permute-start | bytes 1056776 | tf_op jit(solution)/shard_map/ppermute | solution.py:124
  77.8 12.8 %collective-permute-start.10 = (bf16[344,512]{1,0:T(8,128)(2,1)}, bf16[344,512]{1,0:T(8,128)(2,1)S(1)}, u32[]{:S(2)}, u32[]{:S(2)}) collective-permute-start(bf16[344,512]{1,0:T(8,128)(2,1)} %collective-permute-done.6), channel_id=1, source_target_pairs={{0,12},{1,13},{2,14},{3,15},{4,0},{5,1},{6,2},{7,3},{8,4},{9,5},{1... | collective-permute-start | bytes 1056776 | tf_op jit(solution)/shard_map/ppermute | solution.py:63
  78.3 12.3 %collective-permute-start.11 = (bf16[344,512]{1,0:T(8,128)(2,1)}, bf16[344,512]{1,0:T(8,128)(2,1)S(1)}, u32[]{:S(2)}, u32[]{:S(2)}) collective-permute-start(bf16[344,512]{1,0:T(8,128)(2,1)} %collective-permute-done.6), channel_id=1, source_target_pairs={{0,2},{1,3},{2,0},{3,1},{4,6},{5,7},{6,4},{7,5},{8,10},{9,11},{10,... | collective-permute-start | bytes 1056776 | tf_op jit(solution)/shard_map/ppermute | solution.py:64
  79.4 11.1 %collective-permute-start.9 = (bf16[344,512]{1,0:T(8,128)(2,1)}, bf16[344,512]{1,0:T(8,128)(2,1)S(1)}, u32[]{:S(2)}, u32[]{:S(2)}) collective-permute-start(bf16[344,512]{1,0:T(8,128)(2,1)} %collective-permute-done.7), channel_id=1, source_target_pairs={{0,4},{1,5},{2,6},{3,7},{4,8},{5,9},{6,10},{7,11},{8,12},{9,13},{1... | collective-permute-start | bytes 1056776 | tf_op jit(solution)/shard_map/ppermute | solution.py:62
  80.8 15.5 %collective-permute-start.12 = (bf16[688,512]{1,0:T(8,128)(2,1)}, bf16[688,512]{1,0:T(8,128)(2,1)S(1)}, u32[]{:S(2)}, u32[]{:S(2)}) collective-permute-start(bf16[688,512]{1,0:T(8,128)(2,1)} %collective-permute-done.2), channel_id=1, source_target_pairs={{0,16},{16,32},{32,48},{48,64},{64,80},{80,96},{96,112},{112,0},{1... | collective-permute-start | bytes 2113544 | tf_op jit(solution)/shard_map/ppermute | solution.py:129
  82.0 16.2 %collective-permute-start.13 = (bf16[688,512]{1,0:T(8,128)(2,1)}, bf16[688,512]{1,0:T(8,128)(2,1)S(1)}, u32[]{:S(2)}, u32[]{:S(2)}) collective-permute-start(bf16[688,512]{1,0:T(8,128)(2,1)} %collective-permute-done.3), channel_id=1, source_target_pairs={{0,112},{16,0},{32,16},{48,32},{64,48},{80,64},{96,80},{112,96},{1... | collective-permute-start | bytes 2113544 | tf_op jit(solution)/shard_map/ppermute | solution.py:129
  98.2 18.6 %copy-start.1 = (bf16[688,512]{1,0:T(8,128)(2,1)}, bf16[688,512]{1,0:T(8,128)(2,1)S(1)}, u32[]{:S(2)}) copy-start(bf16[688,512]{1,0:T(8,128)(2,1)S(1)} %collective-permute-done.13) | copy-start | bytes 2113540
  98.2 7.9 %collective-permute-start.14 = (bf16[176,512]{1,0:T(8,128)(2,1)S(1)}, bf16[176,512]{1,0:T(8,128)(2,1)S(1)}, u32[]{:S(2)}, u32[]{:S(2)}) collective-permute-start(bf16[176,512]{1,0:T(8,128)(2,1)S(1)} %slice.155), channel_id=1, source_target_pairs={{0,4},{1,5},{2,6},{3,7},{4,8},{5,9},{6,10},{7,11},{8,12},{9,13},{1... | collective-permute-start | bytes 540680 | tf_op jit(solution)/shard_map/ppermute | solution.py:71
  98.8 9.1 %collective-permute-start.15 = (bf16[168,512]{1,0:T(8,128)(2,1)S(1)}, bf16[168,512]{1,0:T(8,128)(2,1)S(1)}, u32[]{:S(2)}, u32[]{:S(2)}) collective-permute-start(bf16[168,512]{1,0:T(8,128)(2,1)S(1)} %slice.156), channel_id=1, source_target_pairs={{0,12},{1,13},{2,14},{3,15},{4,0},{5,1},{6,2},{7,3},{8,4},{9,5},{1... | collective-permute-start | bytes 516104 | tf_op jit(solution)/shard_map/ppermute | solution.py:72
  101.0 15.7 %collective-permute-start.16 = (bf16[688,512]{1,0:T(8,128)(2,1)S(1)}, bf16[688,512]{1,0:T(8,128)(2,1)S(1)}, u32[]{:S(2)}, u32[]{:S(2)}) collective-permute-start(bf16[688,512]{1,0:T(8,128)(2,1)S(1)} %collective-permute-done.12), channel_id=1, source_target_pairs={{0,16},{16,32},{32,48},{48,64},{64,80},{80,96},{96,112},{112,0},{1... | collective-permute-start | bytes 2113544 | tf_op jit(solution)/shard_map/ppermute | solution.py:134
  101.9 14.8 %collective-permute-start.17 = (bf16[688,512]{1,0:T(8,128)(2,1)S(1)}, bf16[688,512]{1,0:T(8,128)(2,1)S(1)}, u32[]{:S(2)}, u32[]{:S(2)}) collective-permute-start(bf16[688,512]{1,0:T(8,128)(2,1)S(1)} %collective-permute-done.13), channel_id=1, source_target_pairs={{0,112},{16,0},{32,16},{48,32},{64,48},{80,64},{96,80},{112,96},{1... | collective-permute-start | bytes 2113544 | tf_op jit(solution)/shard_map/ppermute | solution.py:134
  118.5 9.7 %collective-permute-start.18 = (bf16[4,688,512]{2,1,0:T(8,128)(2,1)}, bf16[4,688,512]{2,1,0:T(8,128)(2,1)}, u32[]{:S(2)}, u32[]{:S(2)}) collective-permute-start(bf16[4,688,512]{2,1,0:T(8,128)(2,1)} %bitcast.11), channel_id=1, source_target_pairs={{0,1},{1,0},{2,3},{3,2},{4,5},{5,4},{6,7},{7,6},{8,9},{9,8},{10,11... | collective-permute-start | bytes 8454152 | tf_op jit(solution)/shard_map/ppermute | solution.py:138
  125.3 17.9 %collective-permute-start.19 = (bf16[344,512]{1,0:T(8,128)(2,1)S(1)}, bf16[344,512]{1,0:T(8,128)(2,1)}, u32[]{:S(2)}, u32[]{:S(2)}) collective-permute-start(bf16[344,512]{1,0:T(8,128)(2,1)S(1)} %slice.177), channel_id=1, source_target_pairs={{0,16},{16,32},{32,48},{48,64},{64,80},{80,96},{96,112},{112,0},{1... | collective-permute-start | bytes 1056776 | tf_op jit(solution)/shard_map/ppermute | solution.py:140
  125.5 17.7 %collective-permute-start.20 = (bf16[344,512]{1,0:T(8,128)(2,1)S(1)}, bf16[344,512]{1,0:T(8,128)(2,1)}, u32[]{:S(2)}, u32[]{:S(2)}) collective-permute-start(bf16[344,512]{1,0:T(8,128)(2,1)S(1)} %slice.178), channel_id=1, source_target_pairs={{0,112},{16,0},{32,16},{48,32},{64,48},{80,64},{96,80},{112,96},{1... | collective-permute-start | bytes 1056776 | tf_op jit(solution)/shard_map/ppermute | solution.py:140
  146.4 25.9 %collective-permute-start.21 = (bf16[688,688]{1,0:T(8,128)(2,1)S(1)}, bf16[688,688]{1,0:T(8,128)(2,1)S(1)}, u32[]{:S(2)}, u32[]{:S(2)}) collective-permute-start(bf16[688,688]{1,0:T(8,128)(2,1)S(1)} %fusion.6), channel_id=1, source_target_pairs={{0,128},{16,144},{32,160},{48,176},{64,192},{80,208},{96,224},{112... | collective-permute-start | bytes 2840072 | tf_op jit(solution)/shard_map/ppermute | solution.py:161
  (13 other events, 39.0 us)
Sparse Core Ops, SparseCore 0:
  77.8 49.6 all-gather.2

commit v6 on v0

v6 whole, which is shorter than its diff:
```python
import jax
import jax.numpy as jnp
from jax import lax
from jax.sharding import PartitionSpec as P

BOTH = ("dp", "tensor")
RING = 8
PLACES = (0, 4, 1, 7, 2, 6, 3, 5)


def place(offset, other):
    k = PLACES.index(offset)
    return (k // 2) * 4 + other * 2 + k % 2


def in_plane():
    pairs = []
    for h in range(2):
        for source in range(RING):
            for b in range(2):
                for z in range(RING):
                    plane = (h * RING + source) * 16
                    pairs.append((plane + b * RING + z, plane + place((source - z) % RING, b ^ h)))
    return pairs


def shifted():
    pairs = []
    for h in range(2):
        for z in range(RING):
            for offset in range(RING):
                for other in range(2):
                    t = place(offset, other)
                    pairs.append(((h * RING + (z + offset) % RING) * 16 + t, (h * RING + z) * 16 + t))
    return pairs


def along_z(step):
    return [(h * RING + z, h * RING + (z + step) % RING) for h in range(2) for z in range(RING)]


ACROSS = [(i, (i + RING) % 16) for i in range(16)]


def product(rows, columns):
    return lax.dot_general(
        rows, columns, (((0, 2), (0, 2)), ((), ())), preferred_element_type=jnp.float32
    )


def put(columns, block, offset, start=0):
    return lax.dynamic_update_slice(columns, block[None], (PLACES.index(offset), start, 0))


def shards(out_grad, down_weight, gate_pre):
    n, tokens = down_weight.shape[0], out_grad.shape[0]
    cut = n // 32 * 16 + 16
    hidden_grad = lax.dot_general(
        down_weight, out_grad, (((1,), (1,)), ((), ())), preferred_element_type=jnp.float32
    ).astype(jnp.bfloat16)
    up_grad = (hidden_grad.astype(jnp.float32) * jax.nn.silu(gate_pre.T.astype(jnp.float32))).astype(
        jnp.bfloat16
    )
    rows = lax.ppermute(up_grad, BOTH, in_plane())
    up, down = lax.ppermute(up_grad, "dp", along_z(1)), lax.ppermute(up_grad, "dp", along_z(-1))
    rows, up, down, up_grad = lax.optimization_barrier((rows, up, down, up_grad))

    rows = lax.ppermute(rows, BOTH, shifted())
    columns = jnp.broadcast_to(up_grad[None], (RING, n, tokens))
    columns = put(put(columns, up, RING - 1), down, 1)
    rows, up, down, columns = lax.optimization_barrier((rows, up, down, columns))
    rows = lax.all_gather(rows, "tensor", axis=0).reshape(4, 2, 2, n, tokens)

    for step in range(2, RING // 2):
        up, down = lax.ppermute(up, "dp", along_z(1)), lax.ppermute(down, "dp", along_z(-1))
        columns = put(put(columns, up, RING - step), down, step)
    up = lax.ppermute(up[:cut], "dp", along_z(1))
    down = lax.ppermute(down[cut:], "dp", along_z(-1))
    columns = put(put(columns, up, RING // 2), down, RING // 2, cut)

    def partial(rows, other):
        return product(rows[:, other].reshape(RING, n, tokens), columns)

    theirs = partial(rows, 1).astype(jnp.bfloat16)
    sent = lax.ppermute(theirs, "dp", ACROSS)
    rows, _ = lax.optimization_barrier((rows, theirs))
    kept = lax.optimization_barrier(partial(rows, 0))
    total = tokens * lax.axis_size("dp")
    return (kept + sent.astype(jnp.float32)) * (1.0 / total)


def solution(mesh):
    placed = (P("dp", None), P("tensor", None), P("dp", "tensor"))
    return jax.shard_map(
        shards, mesh=mesh, in_specs=placed, out_specs=P("dp", "tensor"), check_vma=False
    )
```

time: 655 us -> 182 us (0.28)
  waiting for transfers between devices: 612 us -> 94.4 us
  starting transfers between devices: 0.04 us -> 38.5 us
  local copies, waits for them, and re-layouts: 1.79 us -> 16.2 us
    reduce_scatter x1 -> x0, waiting for transfers between devices: 540 us -> none  [shards(): lax.psum_scatter(lax.dot_general(whole, up_grad, (((0,), (0,)), ((), ()))...]
    ppermute x0 -> x11, waiting for transfers between devices: none -> 69.9 us  [the longest x2 26.5 us: shards(): lax.ppermute(up, 'dp', along_z(1))]
    all_gather x1, waiting for transfers between devices: 72.6 us -> 24.5 us  [shards(): rows = lax.all_gather(rows, 'tensor', axis=0).reshape(4, 2, 2, n, tokens)]
    ppermute x0 -> x11, starting transfers between devices: none -> 38.5 us  [the longest x2 16.2 us: shards(): lax.ppermute(down, 'dp', along_z(-1))]
    dynamic_update_slice x0 -> x8, local copies, waits for them, and re-layouts: none -> 7.08 us  [put(): lax.dynamic_update_slice(columns, block[None], (PLACES.index(offset), sta...]
    dot_general x2 -> x3, matrix products: 22.6 us -> 18 us  [the longest x2 14.5 us: product(): lax.dot_general(rows, columns, (((0, 2), (0, 2)), ((), ())), preferred_el...]
  transfers between devices with their start and end apart: 2 -> 12, of which waited for: 2 -> 8; matrix products, arithmetic and copies ran while one was open for 0% -> 10% of each run, Pallas kernels for 0% -> 0%
where the time goes in v6:
time: 182 us
  waiting for transfers between devices  94.4 us (52%)
  starting transfers between devices  38.5 us (21%)
  matrix products  18 us (10%)
  local copies, waits for them, and re-layouts  16.2 us (9%)
  between operations  13.5 us (7%)
    ppermute x2, waiting for transfers between devices, shards(): lax.ppermute(up, 'dp', along_z(1))  26.5 us
    all_gather x1, waiting for transfers between devices, shards(): rows = lax.all_gather(rows, 'tensor', axis=0).reshape(4, 2, 2, n, tokens)  24.5 us
    ppermute x2, starting transfers between devices, shards(): lax.ppermute(down, 'dp', along_z(-1))  16.2 us
    ppermute x1, waiting for transfers between devices, shards(): sent = lax.ppermute(theirs, 'dp', ACROSS)  16 us
    dot_general x2, matrix products, product(): lax.dot_general(rows, columns, (((0, 2), (0, 2)), ((), ())), preferred_el...  14.5 us
    ppermute x1, waiting for transfers between devices, shards(): rows = lax.ppermute(rows, BOTH, shifted())  9.5 us
    ppermute x1, waiting for transfers between devices, shards(): rows = lax.ppermute(up_grad, BOTH, in_plane())  8.31 us
    dynamic_update_slice x8, local copies, waits for them, and re-layouts, put(): lax.dynamic_update_slice(columns, block[None], (PLACES.index(offset), sta...  7.08 us
  transfers between devices with their start and end apart: 12, of which 8 were waited for; matrix products, arithmetic and copies ran while one was open for 10% of the time, Pallas kernels for 0%

profile of v6, /device:TPU:1, one launch (start us, length us, event | category | flops | bytes accessed | tf_op | source)
XLA Modules:
  0.0 182.1 jit_solution(7480299561743456599)
XLA Ops:
  6.5 1.8 copy-done
  8.3 3.6 %fusion.4 = bf16[688,512]{1,0:T(8,128)(2,1)S(1)} fusion(bf16[512,688]{0,1:T(8,128)(2,1)} %param.5, bf16[688,2048]{1,0:T(8,128)(2,1)S(1)} %copy-done, bf16[512,2048]{1,0:T(8,128)(2,1)} %param.3), kind=kOutput, calls=%fused_computation.9 | convolution fusion | flops 1446010880 | bytes 6324224 | tf_op jit(solution)/shard_map/dot_general | solution.py:58
  11.9 4.0 %collective-permute-start = (bf16[688,512]{1,0:T(8,128)(2,1)S(1)}, bf16[688,512]{1,0:T(8,128)(2,1)S(1)}, u32[]{:S(2)}, u32[]{:S(2)}) collective-permute-start(bf16[688,512]{1,0:T(8,128)(2,1)S(1)} %fusion.4), channel_id=1, source_target_pairs={{0,0},{1,5},{2,9},{3,13},{4,1},{5,12},{6,8},{7,4},{8,2},{9,7},{10,... | collective-permute-start | bytes 2113544 | tf_op jit(solution)/shard_map/ppermute | solution.py:64
  15.8 1.2 collective-permute-start.1
  17.0 6.1 %collective-permute-start.2 = (bf16[688,512]{1,0:T(8,128)(2,1)S(1)}, bf16[688,512]{1,0:T(8,128)(2,1)S(1)}, u32[]{:S(2)}, u32[]{:S(2)}) collective-permute-start(bf16[688,512]{1,0:T(8,128)(2,1)S(1)} %fusion.4), channel_id=1, source_target_pairs={{0,112},{16,0},{32,16},{48,32},{64,48},{80,64},{96,80},{112,96},{1... | collective-permute-start | bytes 2113544 | tf_op jit(solution)/shard_map/ppermute | solution.py:65
  23.1 8.3 %collective-permute-done = bf16[688,512]{1,0:T(8,128)(2,1)S(1)} collective-permute-done((bf16[688,512]{1,0:T(8,128)(2,1)S(1)}, bf16[688,512]{1,0:T(8,128)(2,1)S(1)}, u32[]{:S(2)}, u32[]{:S(2)}) %collective-permute-start) | collective-permute-done | bytes 704544 | tf_op jit(solution)/shard_map/ppermute | solution.py:64
  31.4 6.7 %collective-permute-done.1 = bf16[688,512]{1,0:T(8,128)(2,1)S(1)} collective-permute-done((bf16[688,512]{1,0:T(8,128)(2,1)S(1)}, bf16[688,512]{1,0:T(8,128)(2,1)S(1)}, u32[]{:S(2)}, u32[]{:S(2)}) %collective-permute-start.1) | collective-permute-done | bytes 704544 | tf_op jit(solution)/shard_map/ppermute | solution.py:65
  38.1 5.3 %collective-permute-start.3 = (bf16[688,512]{1,0:T(8,128)(2,1)S(1)}, bf16[688,512]{1,0:T(8,128)(2,1)S(1)}, u32[]{:S(2)}, u32[]{:S(2)}) collective-permute-start(bf16[688,512]{1,0:T(8,128)(2,1)S(1)} %collective-permute-done), channel_id=1, source_target_pairs={{0,0},{2,2},{20,4},{22,6},{40,8},{42,10},{60,12},{62,14},{65,1},{6... | collective-permute-start | bytes 2113544 | tf_op jit(solution)/shard_map/ppermute | solution.py:68
  43.4 2.9 %broadcast_in_dim.30 = bf16[8,688,512]{2,1,0:T(8,128)(2,1)} broadcast(bf16[688,512]{1,0:T(8,128)(2,1)S(1)} %fusion.4), dimensions={1,2} | broadcast | bytes 6340608 | tf_op jit(solution)/shard_map/broadcast_in_dim | solution.py:69
  47.2 0.9 bitcast_dynamic-update-slice_fusion.4
  48.2 9.5 %collective-permute-done.3 = bf16[688,512]{1,0:T(8,128)(2,1)S(1)} collective-permute-done((bf16[688,512]{1,0:T(8,128)(2,1)S(1)}, bf16[688,512]{1,0:T(8,128)(2,1)S(1)}, u32[]{:S(2)}, u32[]{:S(2)}) %collective-permute-start.3) | collective-permute-done | bytes 704544 | tf_op jit(solution)/shard_map/ppermute | solution.py:68
  58.6 13.5 %collective-permute-start.5 = (bf16[688,512]{1,0:T(8,128)(2,1)}, bf16[688,512]{1,0:T(8,128)(2,1)S(1)}, u32[]{:S(2)}, u32[]{:S(2)}) collective-permute-start(bf16[688,512]{1,0:T(8,128)(2,1)} %copy-done.2), channel_id=1, source_target_pairs={{0,112},{16,0},{32,16},{48,32},{64,48},{80,64},{96,80},{112,96},{1... | collective-permute-start | bytes 2113544 | tf_op jit(solution)/shard_map/ppermute | solution.py:75
  72.2 15.9 %collective-permute-done.4 = bf16[688,512]{1,0:T(8,128)(2,1)S(1)} collective-permute-done((bf16[688,512]{1,0:T(8,128)(2,1)}, bf16[688,512]{1,0:T(8,128)(2,1)S(1)}, u32[]{:S(2)}, u32[]{:S(2)}) %collective-permute-start.4) | collective-permute-done | bytes 704544 | tf_op jit(solution)/shard_map/ppermute | solution.py:75
  88.1 2.7 %collective-permute-start.7 = (bf16[688,512]{1,0:T(8,128)(2,1)S(1)}, bf16[688,512]{1,0:T(8,128)(2,1)S(1)}, u32[]{:S(2)}, u32[]{:S(2)}) collective-permute-start(bf16[688,512]{1,0:T(8,128)(2,1)S(1)} %collective-permute-done.5), channel_id=1, source_target_pairs={{0,112},{16,0},{32,16},{48,32},{64,48},{80,64},{96,80},{112,96},{1... | collective-permute-start | bytes 2113544 | tf_op jit(solution)/shard_map/ppermute | solution.py:75
  92.6 10.5 %collective-permute-done.6 = bf16[688,512]{1,0:T(8,128)(2,1)S(1)} collective-permute-done((bf16[688,512]{1,0:T(8,128)(2,1)S(1)}, bf16[688,512]{1,0:T(8,128)(2,1)S(1)}, u32[]{:S(2)}, u32[]{:S(2)}) %collective-permute-start.6) | collective-permute-done | bytes 704544 | tf_op jit(solution)/shard_map/ppermute | solution.py:75
  103.3 2.7 %collective-permute-start.9 = (bf16[336,512]{1,0:T(8,128)(2,1)S(1)}, bf16[336,512]{1,0:T(8,128)(2,1)S(1)}, u32[]{:S(2)}, u32[]{:S(2)}) collective-permute-start(bf16[336,512]{1,0:T(8,128)(2,1)S(1)} %slice.18), channel_id=1, source_target_pairs={{0,112},{16,0},{32,16},{48,32},{64,48},{80,64},{96,80},{112,96},{1... | collective-permute-start | bytes 1032200 | tf_op jit(solution)/shard_map/ppermute | solution.py:78
  107.9 2.9 %collective-permute-done.8 = bf16[352,512]{1,0:T(8,128)(2,1)S(1)} collective-permute-done((bf16[352,512]{1,0:T(8,128)(2,1)S(1)}, bf16[352,512]{1,0:T(8,128)(2,1)S(1)}, u32[]{:S(2)}, u32[]{:S(2)}) %collective-permute-start.8) | collective-permute-done | bytes 360480 | tf_op jit(solution)/shard_map/ppermute | solution.py:77
  112.3 24.5 %all-gather.3.cloned.1.call-done = bf16[11008,512]{1,0:T(8,128)(2,1)} async-done(((bf16[688,512]{1,0:T(8,128)(2,1)}), bf16[11008,512]{1,0:T(8,128)(2,1)}) %all-gather.3.cloned.1.call-update) | async-done | bytes 11272208 | tf_op jit(solution)/shard_map/all_gather | solution.py:72
  136.8 3.1 %slice.16 = bf16[4,1,2,688,512]{4,3,2,1,0:T(8,128)(2,1)S(1)} slice(bf16[4,2,2,688,512]{4,3,2,1,0:T(8,128)(2,1)} %bitcast.44), slice={[0:4], [1:2], [0:2], [0:688], [0:512]} | slice | bytes 11272192 | tf_op jit(solution)/shard_map/slice | solution.py:82
  139.9 7.3 %bitcast_convert_fusion = bf16[688,688]{1,0:T(8,128)(2,1)S(1)} fusion(bf16[8,688,512]{2,1,0:T(8,128)(2,1)S(1)} %bitcast.49, bf16[8,688,512]{2,1,0:T(8,128)(2,1)} %bitcast_dynamic-update-slice_fusion.7), kind=kOutput, calls=%fused_computation | convolution fusion | flops 3878107392 | bytes 12218880 | tf_op jit(solution)/shard_map/dot_general | solution.py:46
  147.2 2.9 %collective-permute-start.10 = (bf16[688,688]{1,0:T(8,128)(2,1)S(1)}, bf16[688,688]{1,0:T(8,128)(2,1)S(1)}, u32[]{:S(2)}, u32[]{:S(2)}) collective-permute-start(bf16[688,688]{1,0:T(8,128)(2,1)S(1)} %bitcast_convert_fusion), channel_id=1, source_target_pairs={{0,128},{16,144},{32,160},{48,176},{64,192},{80,208},{96,224},{112... | collective-permute-start | bytes 2840072 | tf_op jit(solution)/shard_map/ppermute | solution.py:85
  150.5 7.2 %convolution_bitcast_fusion = f32[688,688]{1,0:T(8,128)S(1)} fusion(bf16[8,688,512]{2,1,0:T(8,128)(2,1)S(1)} %bitcast.48, bf16[8,688,512]{2,1,0:T(8,128)(2,1)} %bitcast_dynamic-update-slice_fusion.7), kind=kOutput, calls=%fused_computation.2 | convolution fusion | flops 3877634048 | bytes 13165568 | tf_op jit(solution)/shard_map/dot_general | solution.py:46
  157.6 16.0 %collective-permute-done.10 = bf16[688,688]{1,0:T(8,128)(2,1)S(1)} collective-permute-done((bf16[688,688]{1,0:T(8,128)(2,1)S(1)}, bf16[688,688]{1,0:T(8,128)(2,1)S(1)}, u32[]{:S(2)}, u32[]{:S(2)}) %collective-permute-start.10) | collective-permute-done | bytes 946720 | tf_op jit(solution)/shard_map/ppermute | solution.py:85
  173.7 1.6 add_multiply_fusion
  (33 shorter events, 7.6 us)
Async XLA Ops:
  6.5 1.8 copy-start
  6.5 130.2 %all-gather.3.cloned.1.call-start = ((), (), s32[]{:S(2)}) async-start(), calls=%async_computation | async-start | bytes 11976704 | tf_op jit(solution)/shard_map/all_gather | solution.py:72
  11.9 19.5 %collective-permute-start = (bf16[688,512]{1,0:T(8,128)(2,1)S(1)}, bf16[688,512]{1,0:T(8,128)(2,1)S(1)}, u32[]{:S(2)}, u32[]{:S(2)}) collective-permute-start(bf16[688,512]{1,0:T(8,128)(2,1)S(1)} %fusion.4), channel_id=1, source_target_pairs={{0,0},{1,5},{2,9},{3,13},{4,1},{5,12},{6,8},{7,4},{8,2},{9,7},{10,... | collective-permute-start | bytes 2113544 | tf_op jit(solution)/shard_map/ppermute | solution.py:64
  15.8 22.3 %collective-permute-start.1 = (bf16[688,512]{1,0:T(8,128)(2,1)S(1)}, bf16[688,512]{1,0:T(8,128)(2,1)S(1)}, u32[]{:S(2)}, u32[]{:S(2)}) collective-permute-start(bf16[688,512]{1,0:T(8,128)(2,1)S(1)} %fusion.4), channel_id=1, source_target_pairs={{0,16},{16,32},{32,48},{48,64},{64,80},{80,96},{96,112},{112,0},{1... | collective-permute-start | bytes 2113544 | tf_op jit(solution)/shard_map/ppermute | solution.py:65
  17.0 21.1 %collective-permute-start.2 = (bf16[688,512]{1,0:T(8,128)(2,1)S(1)}, bf16[688,512]{1,0:T(8,128)(2,1)S(1)}, u32[]{:S(2)}, u32[]{:S(2)}) collective-permute-start(bf16[688,512]{1,0:T(8,128)(2,1)S(1)} %fusion.4), channel_id=1, source_target_pairs={{0,112},{16,0},{32,16},{48,32},{64,48},{80,64},{96,80},{112,96},{1... | collective-permute-start | bytes 2113544 | tf_op jit(solution)/shard_map/ppermute | solution.py:65
  38.1 10.0 %copy-start.3 = (bf16[688,512]{1,0:T(8,128)(2,1)}, bf16[688,512]{1,0:T(8,128)(2,1)S(1)}, u32[]{:S(2)}) copy-start(bf16[688,512]{1,0:T(8,128)(2,1)S(1)} %collective-permute-done.1) | copy-start | bytes 2113540
  38.1 9.1 %copy-start.2 = (bf16[688,512]{1,0:T(8,128)(2,1)}, bf16[688,512]{1,0:T(8,128)(2,1)S(1)}, u32[]{:S(2)}) copy-start(bf16[688,512]{1,0:T(8,128)(2,1)S(1)} %collective-permute-done.2) | copy-start | bytes 2113540
  38.1 19.5 %collective-permute-start.3 = (bf16[688,512]{1,0:T(8,128)(2,1)S(1)}, bf16[688,512]{1,0:T(8,128)(2,1)S(1)}, u32[]{:S(2)}, u32[]{:S(2)}) collective-permute-start(bf16[688,512]{1,0:T(8,128)(2,1)S(1)} %collective-permute-done), channel_id=1, source_target_pairs={{0,0},{2,2},{20,4},{22,6},{40,8},{42,10},{60,12},{62,14},{65,1},{6... | collective-permute-start | bytes 2113544 | tf_op jit(solution)/shard_map/ppermute | solution.py:68
  57.7 0.9 copy-start.1
  58.5 29.6 %collective-permute-start.4 = (bf16[688,512]{1,0:T(8,128)(2,1)}, bf16[688,512]{1,0:T(8,128)(2,1)S(1)}, u32[]{:S(2)}, u32[]{:S(2)}) collective-permute-start(bf16[688,512]{1,0:T(8,128)(2,1)} %copy-done.3), channel_id=1, source_target_pairs={{0,16},{16,32},{32,48},{48,64},{64,80},{80,96},{96,112},{112,0},{1... | collective-permute-start | bytes 2113544 | tf_op jit(solution)/shard_map/ppermute | solution.py:75
  58.6 29.5 %collective-permute-start.5 = (bf16[688,512]{1,0:T(8,128)(2,1)}, bf16[688,512]{1,0:T(8,128)(2,1)S(1)}, u32[]{:S(2)}, u32[]{:S(2)}) collective-permute-start(bf16[688,512]{1,0:T(8,128)(2,1)} %copy-done.2), channel_id=1, source_target_pairs={{0,112},{16,0},{32,16},{48,32},{64,48},{80,64},{96,80},{112,96},{1... | collective-permute-start | bytes 2113544 | tf_op jit(solution)/shard_map/ppermute | solution.py:75
  88.1 15.0 %collective-permute-start.6 = (bf16[688,512]{1,0:T(8,128)(2,1)S(1)}, bf16[688,512]{1,0:T(8,128)(2,1)S(1)}, u32[]{:S(2)}, u32[]{:S(2)}) collective-permute-start(bf16[688,512]{1,0:T(8,128)(2,1)S(1)} %collective-permute-done.4), channel_id=1, source_target_pairs={{0,16},{16,32},{32,48},{48,64},{64,80},{80,96},{96,112},{112,0},{1... | collective-permute-start | bytes 2113544 | tf_op jit(solution)/shard_map/ppermute | solution.py:75
  88.1 15.2 %collective-permute-start.7 = (bf16[688,512]{1,0:T(8,128)(2,1)S(1)}, bf16[688,512]{1,0:T(8,128)(2,1)S(1)}, u32[]{:S(2)}, u32[]{:S(2)}) collective-permute-start(bf16[688,512]{1,0:T(8,128)(2,1)S(1)} %collective-permute-done.5), channel_id=1, source_target_pairs={{0,112},{16,0},{32,16},{48,32},{64,48},{80,64},{96,80},{112,96},{1... | collective-permute-start | bytes 2113544 | tf_op jit(solution)/shard_map/ppermute | solution.py:75
  103.2 7.6 %collective-permute-start.8 = (bf16[352,512]{1,0:T(8,128)(2,1)S(1)}, bf16[352,512]{1,0:T(8,128)(2,1)S(1)}, u32[]{:S(2)}, u32[]{:S(2)}) collective-permute-start(bf16[352,512]{1,0:T(8,128)(2,1)S(1)} %slice.17), channel_id=1, source_target_pairs={{0,16},{16,32},{32,48},{48,64},{64,80},{80,96},{96,112},{112,0},{1... | collective-permute-start | bytes 1081352 | tf_op jit(solution)/shard_map/ppermute | solution.py:77
  103.3 8.2 %collective-permute-start.9 = (bf16[336,512]{1,0:T(8,128)(2,1)S(1)}, bf16[336,512]{1,0:T(8,128)(2,1)S(1)}, u32[]{:S(2)}, u32[]{:S(2)}) collective-permute-start(bf16[336,512]{1,0:T(8,128)(2,1)S(1)} %slice.18), channel_id=1, source_target_pairs={{0,112},{16,0},{32,16},{48,32},{64,48},{80,64},{96,80},{112,96},{1... | collective-permute-start | bytes 1032200 | tf_op jit(solution)/shard_map/ppermute | solution.py:78
  136.7 13.3 %slice-start = ((s8[11272192]{0:T(1024)(128)(4,1)}), s8[4194304]{0:T(1024)(128)(4,1)S(1)}, s32[]{:S(2)}) async-start(s8[11272192]{0:T(1024)(128)(4,1)} %bitcast.45), calls=%async_computation.1 | async-start | bytes 8388608
  139.9 10.2 %slice-start.1 = ((s8[11272192]{0:T(1024)(128)(4,1)}), s8[4194304]{0:T(1024)(128)(4,1)S(1)}, s32[]{:S(2)}) async-start(s8[11272192]{0:T(1024)(128)(4,1)} %bitcast.45), calls=%async_computation.2 | async-start | bytes 8388608
  139.9 10.2 %slice-start.2 = ((s8[11272192]{0:T(1024)(128)(4,1)}), s8[2883584]{0:T(1024)(128)(4,1)S(1)}, s32[]{:S(2)}) async-start(s8[11272192]{0:T(1024)(128)(4,1)} %bitcast.45), calls=%async_computation.3 | async-start | bytes 5767168
  147.2 26.5 %collective-permute-start.10 = (bf16[688,688]{1,0:T(8,128)(2,1)S(1)}, bf16[688,688]{1,0:T(8,128)(2,1)S(1)}, u32[]{:S(2)}, u32[]{:S(2)}) collective-permute-start(bf16[688,688]{1,0:T(8,128)(2,1)S(1)} %bitcast_convert_fusion), channel_id=1, source_target_pairs={{0,128},{16,144},{32,160},{48,176},{64,192},{80,208},{96,224},{112... | collective-permute-start | bytes 2840072 | tf_op jit(solution)/shard_map/ppermute | solution.py:85
Sparse Core Ops, SparseCore 0:
  58.7 78.0 all-gather.2

commit v7 on v6

--- a/solution.py
+++ b/solution.py
@@ -42,14 +42,9 @@
 ACROSS = [(i, (i + RING) % 16) for i in range(16)]
 
 
-def product(rows, columns):
-    return lax.dot_general(
-        rows, columns, (((0, 2), (0, 2)), ((), ())), preferred_element_type=jnp.float32
-    )
-
-
 def put(columns, block, offset, start=0):
-    return lax.dynamic_update_slice(columns, block[None], (PLACES.index(offset), start, 0))
+    tokens = block.shape[1]
+    return lax.dynamic_update_slice(columns, block, (start, PLACES.index(offset) * tokens))
 
 
 def shards(out_grad, down_weight, gate_pre):
@@ -61,17 +56,13 @@
     up_grad = (hidden_grad.astype(jnp.float32) * jax.nn.silu(gate_pre.T.astype(jnp.float32))).astype(
         jnp.bfloat16
     )
-    rows = lax.ppermute(up_grad, BOTH, in_plane())
-    up, down = lax.ppermute(up_grad, "dp", along_z(1)), lax.ppermute(up_grad, "dp", along_z(-1))
-    rows, up, down, up_grad = lax.optimization_barrier((rows, up, down, up_grad))
-
-    rows = lax.ppermute(rows, BOTH, shifted())
-    columns = jnp.broadcast_to(up_grad[None], (RING, n, tokens))
-    columns = put(put(columns, up, RING - 1), down, 1)
-    rows, up, down, columns = lax.optimization_barrier((rows, up, down, columns))
+    rows = lax.ppermute(lax.ppermute(up_grad, BOTH, in_plane()), BOTH, shifted())
+    rows, up_grad = lax.optimization_barrier((rows, up_grad))
     rows = lax.all_gather(rows, "tensor", axis=0).reshape(4, 2, 2, n, tokens)
 
-    for step in range(2, RING // 2):
+    columns = put(jnp.zeros((n, RING * tokens), jnp.bfloat16), up_grad, 0)
+    up, down = up_grad, up_grad
+    for step in range(1, RING // 2):
         up, down = lax.ppermute(up, "dp", along_z(1)), lax.ppermute(down, "dp", along_z(-1))
         columns = put(put(columns, up, RING - step), down, step)
     up = lax.ppermute(up[:cut], "dp", along_z(1))
@@ -79,7 +70,11 @@
     columns = put(put(columns, up, RING // 2), down, RING // 2, cut)
 
     def partial(rows, other):
-        return product(rows[:, other].reshape(RING, n, tokens), columns)
+        blocks = [rows[k // 2, other, k % 2] for k in range(RING)]
+        return lax.dot_general(
+            jnp.concatenate(blocks, axis=1), columns, (((1,), (1,)), ((), ())),
+            preferred_element_type=jnp.float32,
+        )
 
     theirs = partial(rows, 1).astype(jnp.bfloat16)
     sent = lax.ppermute(theirs, "dp", ACROSS)

time: 182 us -> 185 us (1.016)
  starting transfers between devices: 38.5 us -> 31.9 us
  local copies, waits for them, and re-layouts: 16.2 us -> 22.7 us
  waiting for transfers between devices: 94.4 us -> 96.8 us
    all_gather x1, waiting for transfers between devices: 24.5 us -> 8.76 us  [shards(): rows = lax.all_gather(rows, 'tensor', axis=0).reshape(4, 2, 2, n, tokens)]
    ppermute x2 -> x3, waiting for transfers between devices: 26.5 us -> 36.7 us  [shards(): lax.ppermute(up, 'dp', along_z(1))]
    ppermute x4 -> x2, waiting for transfers between devices: 24.5 us -> 34.2 us  [the longest x1 18.9 us: shards(): lax.ppermute(lax.ppermute(up_grad, BOTH, in_plane()), BOTH, shifted())]
    ppermute x4 -> x2, starting transfers between devices: 16.5 us -> 7.33 us  [the longest x1 3.95 us: shards(): lax.ppermute(up_grad, BOTH, in_plane())]
    unnamed x14 -> x22, local copies, waits for them, and re-layouts: 2.67 us -> 10.8 us
    ppermute x2 -> x3, starting transfers between devices: 0.09 us -> 7.68 us  [shards(): lax.ppermute(up, 'dp', along_z(1))]
    ppermute x2 -> x3, starting transfers between devices: 16.2 us -> 11.2 us  [shards(): lax.ppermute(down, 'dp', along_z(-1))]
    slice x2 -> x0, local copies, waits for them, and re-layouts: 3.49 us -> none  [partial(): return product(rows[:, other].reshape(RING, n, tokens), columns)]
where the time goes in v7:
time: 185 us
  waiting for transfers between devices  96.8 us (52%)
  starting transfers between devices  31.9 us (17%)
  local copies, waits for them, and re-layouts  22.7 us (12%)
  matrix products  18 us (10%)
  between operations  13.6 us (7%)
    ppermute x3, waiting for transfers between devices, shards(): lax.ppermute(up, 'dp', along_z(1))  36.7 us
    ppermute x1, waiting for transfers between devices, shards(): lax.ppermute(lax.ppermute(up_grad, BOTH, in_plane()), BOTH, shifted())  18.9 us
    ppermute x1, waiting for transfers between devices, shards(): sent = lax.ppermute(theirs, 'dp', ACROSS)  15.6 us
    ppermute x1, waiting for transfers between devices, shards(): lax.ppermute(up_grad, BOTH, in_plane())  15.3 us
    dot_general x2, matrix products, partial(): lax.dot_general(jnp.concatenate(blocks, axis=1), columns, (((1,), (1,)),...  14.5 us
    ppermute x3, starting transfers between devices, shards(): lax.ppermute(down, 'dp', along_z(-1))  11.2 us
    unnamed x22, local copies, waits for them, and re-layouts  10.8 us
    dynamic_update_slice x9, local copies, waits for them, and re-layouts, put(): lax.dynamic_update_slice(columns, block, (start, PLACES.index(offset) * t...  10.4 us
  transfers between devices with their start and end apart: 12, of which 8 were waited for; matrix products, arithmetic and copies ran while one was open for 10% of the time, Pallas kernels for 0%

profile of v7, /device:TPU:1, one launch (start us, length us, event | category | flops | bytes accessed | tf_op | source)
XLA Modules:
  0.0 184.6 jit_solution(6039048414075906735)
XLA Ops:
  6.5 1.8 copy-done
  8.3 3.6 %fusion.4 = bf16[688,512]{1,0:T(8,128)(2,1)S(1)} fusion(bf16[512,688]{0,1:T(8,128)(2,1)} %param.5, bf16[688,2048]{1,0:T(8,128)(2,1)S(1)} %copy-done, bf16[512,2048]{1,0:T(8,128)(2,1)} %param.3), kind=kOutput, calls=%fused_computation.8 | convolution fusion | flops 1446010880 | bytes 6324224 | tf_op jit(solution)/shard_map/dot_general | solution.py:53
  11.9 4.0 %collective-permute-start = (bf16[688,512]{1,0:T(8,128)(2,1)S(1)}, bf16[688,512]{1,0:T(8,128)(2,1)S(1)}, u32[]{:S(2)}, u32[]{:S(2)}) collective-permute-start(bf16[688,512]{1,0:T(8,128)(2,1)S(1)} %fusion.4), channel_id=1, source_target_pairs={{0,0},{1,5},{2,9},{3,13},{4,1},{5,12},{6,8},{7,4},{8,2},{9,7},{10,... | collective-permute-start | bytes 2113544 | tf_op jit(solution)/shard_map/ppermute | solution.py:59
  15.8 15.3 %collective-permute-done = bf16[688,512]{1,0:T(8,128)(2,1)S(1)} collective-permute-done((bf16[688,512]{1,0:T(8,128)(2,1)S(1)}, bf16[688,512]{1,0:T(8,128)(2,1)S(1)}, u32[]{:S(2)}, u32[]{:S(2)}) %collective-permute-start) | collective-permute-done | bytes 704544 | tf_op jit(solution)/shard_map/ppermute | solution.py:59
  31.1 3.4 %collective-permute-start.1 = (bf16[688,512]{1,0:T(8,128)(2,1)S(1)}, bf16[688,512]{1,0:T(8,128)(2,1)}, u32[]{:S(2)}, u32[]{:S(2)}) collective-permute-start(bf16[688,512]{1,0:T(8,128)(2,1)S(1)} %collective-permute-done), channel_id=1, source_target_pairs={{0,0},{2,2},{20,4},{22,6},{40,8},{42,10},{60,12},{62,14},{65,1},{6... | collective-permute-start | bytes 2113544 | tf_op jit(solution)/shard_map/ppermute | solution.py:59
  34.5 18.9 %collective-permute-done.1 = bf16[688,512]{1,0:T(8,128)(2,1)} collective-permute-done((bf16[688,512]{1,0:T(8,128)(2,1)S(1)}, bf16[688,512]{1,0:T(8,128)(2,1)}, u32[]{:S(2)}, u32[]{:S(2)}) %collective-permute-start.1) | collective-permute-done | bytes 704544 | tf_op jit(solution)/shard_map/ppermute | solution.py:59
  53.5 7.7 %collective-permute-start.2 = (bf16[688,512]{1,0:T(8,128)(2,1)S(1)}, bf16[688,512]{1,0:T(8,128)(2,1)S(1)}, u32[]{:S(2)}, u32[]{:S(2)}) collective-permute-start(bf16[688,512]{1,0:T(8,128)(2,1)S(1)} %fusion.4), channel_id=1, source_target_pairs={{0,16},{16,32},{32,48},{48,64},{64,80},{80,96},{96,112},{112,0},{1... | collective-permute-start | bytes 2113544 | tf_op jit(solution)/shard_map/ppermute | solution.py:66
  61.1 5.2 %collective-permute-start.3 = (bf16[688,512]{1,0:T(8,128)(2,1)S(1)}, bf16[688,512]{1,0:T(8,128)(2,1)S(1)}, u32[]{:S(2)}, u32[]{:S(2)}) collective-permute-start(bf16[688,512]{1,0:T(8,128)(2,1)S(1)} %fusion.4), channel_id=1, source_target_pairs={{0,112},{16,0},{32,16},{48,32},{64,48},{80,64},{96,80},{112,96},{1... | collective-permute-start | bytes 2113544 | tf_op jit(solution)/shard_map/ppermute | solution.py:66
  66.3 14.7 %collective-permute-done.2 = bf16[688,512]{1,0:T(8,128)(2,1)S(1)} collective-permute-done((bf16[688,512]{1,0:T(8,128)(2,1)S(1)}, bf16[688,512]{1,0:T(8,128)(2,1)S(1)}, u32[]{:S(2)}, u32[]{:S(2)}) %collective-permute-start.2) | collective-permute-done | bytes 704544 | tf_op jit(solution)/shard_map/ppermute | solution.py:66
  81.0 3.0 %collective-permute-start.5 = (bf16[688,512]{1,0:T(8,128)(2,1)S(1)}, bf16[688,512]{1,0:T(8,128)(2,1)S(1)}, u32[]{:S(2)}, u32[]{:S(2)}) collective-permute-start(bf16[688,512]{1,0:T(8,128)(2,1)S(1)} %collective-permute-done.3), channel_id=1, source_target_pairs={{0,112},{16,0},{32,16},{48,32},{64,48},{80,64},{96,80},{112,96},{1... | collective-permute-start | bytes 2113544 | tf_op jit(solution)/shard_map/ppermute | solution.py:66
  84.0 15.8 %collective-permute-done.4 = bf16[688,512]{1,0:T(8,128)(2,1)S(1)} collective-permute-done((bf16[688,512]{1,0:T(8,128)(2,1)S(1)}, bf16[688,512]{1,0:T(8,128)(2,1)S(1)}, u32[]{:S(2)}, u32[]{:S(2)}) %collective-permute-start.4) | collective-permute-done | bytes 704544 | tf_op jit(solution)/shard_map/ppermute | solution.py:66
  99.9 3.0 %collective-permute-start.7 = (bf16[688,512]{1,0:T(8,128)(2,1)S(1)}, bf16[688,512]{1,0:T(8,128)(2,1)S(1)}, u32[]{:S(2)}, u32[]{:S(2)}) collective-permute-start(bf16[688,512]{1,0:T(8,128)(2,1)S(1)} %collective-permute-done.5), channel_id=1, source_target_pairs={{0,112},{16,0},{32,16},{48,32},{64,48},{80,64},{96,80},{112,96},{1... | collective-permute-start | bytes 2113544 | tf_op jit(solution)/shard_map/ppermute | solution.py:66
  102.9 3.1 %dynamic_update_slice.27 = bf16[688,4096]{1,0:T(8,128)(2,1)} pad(bf16[688,512]{1,0:T(8,128)(2,1)S(1)} %fusion.4, bf16[]{:T(256)} %constant.2.clone.1), padding=0_0x0_3584 | pad | bytes 6340610 | tf_op jit(solution)/shard_map/dynamic_update_slice | solution.py:47
  108.8 6.1 %collective-permute-done.6 = bf16[688,512]{1,0:T(8,128)(2,1)S(1)} collective-permute-done((bf16[688,512]{1,0:T(8,128)(2,1)S(1)}, bf16[688,512]{1,0:T(8,128)(2,1)S(1)}, u32[]{:S(2)}, u32[]{:S(2)}) %collective-permute-start.6) | collective-permute-done | bytes 704544 | tf_op jit(solution)/shard_map/ppermute | solution.py:66
  116.0 2.9 %collective-permute-start.9 = (bf16[336,512]{1,0:T(8,128)(2,1)S(1)}, bf16[336,512]{1,0:T(8,128)(2,1)S(1)}, u32[]{:S(2)}, u32[]{:S(2)}) collective-permute-start(bf16[336,512]{1,0:T(8,128)(2,1)S(1)} %slice.81), channel_id=1, source_target_pairs={{0,112},{16,0},{32,16},{48,32},{64,48},{80,64},{96,80},{112,96},{1... | collective-permute-start | bytes 1032200 | tf_op jit(solution)/shard_map/ppermute | solution.py:69
  120.9 1.6 collective-permute-done.8
  124.1 8.8 %all-gather.3.cloned.1.call-done = bf16[11008,512]{1,0:T(8,128)(2,1)} async-done(((bf16[688,512]{1,0:T(8,128)(2,1)}), bf16[11008,512]{1,0:T(8,128)(2,1)}) %all-gather.3.cloned.1.call-update) | async-done | bytes 11272208 | tf_op jit(solution)/shard_map/all_gather | solution.py:61
  134.0 1.2 fusion.11
  141.2 1.3 fusion.5
  142.5 7.3 %convolution_convert_fusion = bf16[688,688]{1,0:T(8,128)(2,1)S(1)} fusion(bf16[688,4096]{1,0:T(8,128)(2,1)S(1)} %fusion.5, bf16[688,4096]{1,0:T(8,128)(2,1)} %constant_dynamic-update-slice_fusion.7), kind=kOutput, calls=%fused_computation.1 | convolution fusion | flops 3878107392 | bytes 12218880 | tf_op jit(solution)/shard_map/dot_general | solution.py:74
  149.9 2.7 %collective-permute-start.10 = (bf16[688,688]{1,0:T(8,128)(2,1)S(1)}, bf16[688,688]{1,0:T(8,128)(2,1)S(1)}, u32[]{:S(2)}, u32[]{:S(2)}) collective-permute-start(bf16[688,688]{1,0:T(8,128)(2,1)S(1)} %convolution_convert_fusion), channel_id=1, source_target_pairs={{0,128},{16,144},{32,160},{48,176},{64,192},{80,208},{96,224},{112... | collective-permute-start | bytes 2840072 | tf_op jit(solution)/shard_map/ppermute | solution.py:80
  153.4 7.2 %fusion.13 = f32[688,688]{1,0:T(8,128)S(1)} fusion(bf16[688,4096]{1,0:T(8,128)(2,1)S(1)} %bitcast_dynamic-update-slice_fusion, bf16[688,4096]{1,0:T(8,128)(2,1)} %constant_dynamic-update-slice_fusion.7), kind=kOutput, calls=%fused_computation.42 | convolution fusion | flops 3877634048 | bytes 13165568 | tf_op jit(solution)/shard_map/dot_general | solution.py:74
  160.6 15.6 %collective-permute-done.10 = bf16[688,688]{1,0:T(8,128)(2,1)S(1)} collective-permute-done((bf16[688,688]{1,0:T(8,128)(2,1)S(1)}, bf16[688,688]{1,0:T(8,128)(2,1)S(1)}, u32[]{:S(2)}, u32[]{:S(2)}) %collective-permute-start.10) | collective-permute-done | bytes 946720 | tf_op jit(solution)/shard_map/ppermute | solution.py:80
  176.1 1.6 add_multiply_fusion
  (41 shorter events, 15.4 us)
Async XLA Ops:
  6.5 1.8 copy-start
  6.5 126.3 %all-gather.3.cloned.1.call-start = ((), (), s32[]{:S(2)}) async-start(), calls=%async_computation | async-start | bytes 11976704 | tf_op jit(solution)/shard_map/all_gather | solution.py:61
  11.9 19.2 %collective-permute-start = (bf16[688,512]{1,0:T(8,128)(2,1)S(1)}, bf16[688,512]{1,0:T(8,128)(2,1)S(1)}, u32[]{:S(2)}, u32[]{:S(2)}) collective-permute-start(bf16[688,512]{1,0:T(8,128)(2,1)S(1)} %fusion.4), channel_id=1, source_target_pairs={{0,0},{1,5},{2,9},{3,13},{4,1},{5,12},{6,8},{7,4},{8,2},{9,7},{10,... | collective-permute-start | bytes 2113544 | tf_op jit(solution)/shard_map/ppermute | solution.py:59
  31.1 22.3 %collective-permute-start.1 = (bf16[688,512]{1,0:T(8,128)(2,1)S(1)}, bf16[688,512]{1,0:T(8,128)(2,1)}, u32[]{:S(2)}, u32[]{:S(2)}) collective-permute-start(bf16[688,512]{1,0:T(8,128)(2,1)S(1)} %collective-permute-done), channel_id=1, source_target_pairs={{0,0},{2,2},{20,4},{22,6},{40,8},{42,10},{60,12},{62,14},{65,1},{6... | collective-permute-start | bytes 2113544 | tf_op jit(solution)/shard_map/ppermute | solution.py:59
  53.5 27.6 %collective-permute-start.2 = (bf16[688,512]{1,0:T(8,128)(2,1)S(1)}, bf16[688,512]{1,0:T(8,128)(2,1)S(1)}, u32[]{:S(2)}, u32[]{:S(2)}) collective-permute-start(bf16[688,512]{1,0:T(8,128)(2,1)S(1)} %fusion.4), channel_id=1, source_target_pairs={{0,16},{16,32},{32,48},{48,64},{64,80},{80,96},{96,112},{112,0},{1... | collective-permute-start | bytes 2113544 | tf_op jit(solution)/shard_map/ppermute | solution.py:66
  61.1 19.9 %collective-permute-start.3 = (bf16[688,512]{1,0:T(8,128)(2,1)S(1)}, bf16[688,512]{1,0:T(8,128)(2,1)S(1)}, u32[]{:S(2)}, u32[]{:S(2)}) collective-permute-start(bf16[688,512]{1,0:T(8,128)(2,1)S(1)} %fusion.4), channel_id=1, source_target_pairs={{0,112},{16,0},{32,16},{48,32},{64,48},{80,64},{96,80},{112,96},{1... | collective-permute-start | bytes 2113544 | tf_op jit(solution)/shard_map/ppermute | solution.py:66
  81.0 18.8 %collective-permute-start.4 = (bf16[688,512]{1,0:T(8,128)(2,1)S(1)}, bf16[688,512]{1,0:T(8,128)(2,1)S(1)}, u32[]{:S(2)}, u32[]{:S(2)}) collective-permute-start(bf16[688,512]{1,0:T(8,128)(2,1)S(1)} %collective-permute-done.2), channel_id=1, source_target_pairs={{0,16},{16,32},{32,48},{48,64},{64,80},{80,96},{96,112},{112,0},{1... | collective-permute-start | bytes 2113544 | tf_op jit(solution)/shard_map/ppermute | solution.py:66
  81.0 18.8 %collective-permute-start.5 = (bf16[688,512]{1,0:T(8,128)(2,1)S(1)}, bf16[688,512]{1,0:T(8,128)(2,1)S(1)}, u32[]{:S(2)}, u32[]{:S(2)}) collective-permute-start(bf16[688,512]{1,0:T(8,128)(2,1)S(1)} %collective-permute-done.3), channel_id=1, source_target_pairs={{0,112},{16,0},{32,16},{48,32},{64,48},{80,64},{96,80},{112,96},{1... | collective-permute-start | bytes 2113544 | tf_op jit(solution)/shard_map/ppermute | solution.py:66
  99.8 15.0 %collective-permute-start.6 = (bf16[688,512]{1,0:T(8,128)(2,1)S(1)}, bf16[688,512]{1,0:T(8,128)(2,1)S(1)}, u32[]{:S(2)}, u32[]{:S(2)}) collective-permute-start(bf16[688,512]{1,0:T(8,128)(2,1)S(1)} %collective-permute-done.4), channel_id=1, source_target_pairs={{0,16},{16,32},{32,48},{48,64},{64,80},{80,96},{96,112},{112,0},{1... | collective-permute-start | bytes 2113544 | tf_op jit(solution)/shard_map/ppermute | solution.py:66
  99.9 16.1 %collective-permute-start.7 = (bf16[688,512]{1,0:T(8,128)(2,1)S(1)}, bf16[688,512]{1,0:T(8,128)(2,1)S(1)}, u32[]{:S(2)}, u32[]{:S(2)}) collective-permute-start(bf16[688,512]{1,0:T(8,128)(2,1)S(1)} %collective-permute-done.5), channel_id=1, source_target_pairs={{0,112},{16,0},{32,16},{48,32},{64,48},{80,64},{96,80},{112,96},{1... | collective-permute-start | bytes 2113544 | tf_op jit(solution)/shard_map/ppermute | solution.py:66
  114.9 7.6 %collective-permute-start.8 = (bf16[352,512]{1,0:T(8,128)(2,1)S(1)}, bf16[352,512]{1,0:T(8,128)(2,1)S(1)}, u32[]{:S(2)}, u32[]{:S(2)}) collective-permute-start(bf16[352,512]{1,0:T(8,128)(2,1)S(1)} %slice.80), channel_id=1, source_target_pairs={{0,16},{16,32},{32,48},{48,64},{64,80},{80,96},{96,112},{112,0},{1... | collective-permute-start | bytes 1081352 | tf_op jit(solution)/shard_map/ppermute | solution.py:68
  116.0 7.3 %collective-permute-start.9 = (bf16[336,512]{1,0:T(8,128)(2,1)S(1)}, bf16[336,512]{1,0:T(8,128)(2,1)S(1)}, u32[]{:S(2)}, u32[]{:S(2)}) collective-permute-start(bf16[336,512]{1,0:T(8,128)(2,1)S(1)} %slice.81), channel_id=1, source_target_pairs={{0,112},{16,0},{32,16},{48,32},{64,48},{80,64},{96,80},{112,96},{1... | collective-permute-start | bytes 1032200 | tf_op jit(solution)/shard_map/ppermute | solution.py:69
  141.2 11.4 %slice-start = ((s8[11272192]{0:T(1024)(128)(4,1)}), s8[4194304]{0:T(1024)(128)(4,1)S(1)}, s32[]{:S(2)}) async-start(s8[11272192]{0:T(1024)(128)(4,1)} %bitcast.78), calls=%async_computation.1 | async-start | bytes 8388608
  142.5 10.0 %slice-start.1 = ((s8[11272192]{0:T(1024)(128)(4,1)}), s8[4194304]{0:T(1024)(128)(4,1)S(1)}, s32[]{:S(2)}) async-start(s8[11272192]{0:T(1024)(128)(4,1)} %bitcast.78), calls=%async_computation.2 | async-start | bytes 8388608
  142.5 10.0 %slice-start.2 = ((s8[11272192]{0:T(1024)(128)(4,1)}), s8[2883584]{0:T(1024)(128)(4,1)S(1)}, s32[]{:S(2)}) async-start(s8[11272192]{0:T(1024)(128)(4,1)} %bitcast.78), calls=%async_computation.3 | async-start | bytes 5767168
  149.9 26.3 %collective-permute-start.10 = (bf16[688,688]{1,0:T(8,128)(2,1)S(1)}, bf16[688,688]{1,0:T(8,128)(2,1)S(1)}, u32[]{:S(2)}, u32[]{:S(2)}) collective-permute-start(bf16[688,688]{1,0:T(8,128)(2,1)S(1)} %convolution_convert_fusion), channel_id=1, source_target_pairs={{0,128},{16,144},{32,160},{48,176},{64,192},{80,208},{96,224},{112... | collective-permute-start | bytes 2840072 | tf_op jit(solution)/shard_map/ppermute | solution.py:80
Sparse Core Ops, SparseCore 0:
  53.6 79.2 all-gather.2

commit v8 on v7

v8 whole, which is shorter than its diff:
```python
import functools

import jax
import jax.numpy as jnp
from jax import lax
from jax.experimental import pallas as pl
from jax.experimental.pallas import tpu as pltpu
from jax.sharding import PartitionSpec as P

BOTH = ("dp", "tensor")
RING = 8
PLACES = ((0, 4, 1, 7, 2, 6, 3, 5), (1, 7, 0, 4, 3, 5, 2, 6))


def place(offset, other, second):
    k = PLACES[second].index(offset)
    return (k // 2) * 4 + other * 2 + k % 2


def in_plane(second):
    pairs = []
    for h in range(2):
        for source in range(RING):
            for b in range(2):
                for z in range(RING):
                    plane = (h * RING + source) * 16
                    pairs.append((plane + b * RING + z, plane + place((source - z) % RING, b ^ h, second)))
    return pairs


def shifted(second):
    pairs = []
    for h in range(2):
        for z in range(RING):
            for offset in range(RING):
                for other in range(2):
                    t = place(offset, other, second)
                    pairs.append(((h * RING + (z + offset) % RING) * 16 + t, (h * RING + z) * 16 + t))
    return pairs


def along_z(step):
    return [(h * RING + z, h * RING + (z + step) % RING) for h in range(2) for z in range(RING)]


ACROSS = [(i, (i + RING) % 16) for i in range(16)]


def product_body(first_ref, second_ref, columns_ref, out_ref, total, *, cut):
    k = pl.program_id(0)

    def partial(ref, low, high):
        return sum(
            lax.dot_general(
                ref[0, 0, core, low:high], columns_ref[core], (((1,), (1,)), ((), ())),
                preferred_element_type=jnp.float32,
            )
            for core in range(2)
        )

    n = out_ref.shape[0]
    for ref, low, high in ((first_ref, 0, cut), (second_ref, cut, n)):
        @pl.when(k == 0)
        def _():
            total[low:high] = partial(ref, low, high)

        @pl.when((k > 0) & (k < 3))
        def _():
            total[low:high] += partial(ref, low, high)

        @pl.when(k == 3)
        def _():
            out_ref[low:high] = (total[low:high] + partial(ref, low, high)).astype(out_ref.dtype)


def product(rows, columns, other, cut, kind):
    n, tokens = columns.shape[1:]
    block = (1, 1, 2, n, tokens)
    return pl.pallas_call(
        functools.partial(product_body, cut=cut),
        grid=(4,),
        in_specs=[
            pl.BlockSpec(block, lambda k: (k, other, 0, 0, 0)),
            pl.BlockSpec(block, lambda k: (k ^ 1, other, 0, 0, 0)),
            pl.BlockSpec((2, n, tokens), lambda k: (k, 0, 0)),
        ],
        out_specs=pl.BlockSpec((n, n), lambda k: (0, 0)),
        out_shape=jax.ShapeDtypeStruct((n, n), kind),
        scratch_shapes=[pltpu.VMEM((n, n), jnp.float32)],
        compiler_params=pltpu.CompilerParams(
            dimension_semantics=("arbitrary",), vmem_limit_bytes=56 * 1024 * 1024
        ),
        cost_estimate=pl.CostEstimate(
            flops=2 * n * n * tokens * RING, bytes_accessed=24 * 1024 * 1024, transcendentals=0
        ),
    )(rows, rows, columns)


def put(columns, block, offset, start=0):
    return lax.dynamic_update_slice(columns, block[None], (PLACES[0].index(offset), start, 0))


def shards(out_grad, down_weight, gate_pre):
    n, tokens = down_weight.shape[0], out_grad.shape[0]
    cut = n // 32 * 16 + 16
    hidden_grad = lax.dot_general(
        down_weight, out_grad, (((1,), (1,)), ((), ())), preferred_element_type=jnp.float32
    ).astype(jnp.bfloat16)
    up_grad = (hidden_grad.astype(jnp.float32) * jax.nn.silu(gate_pre.T.astype(jnp.float32))).astype(
        jnp.bfloat16
    )
    parts = [
        lax.ppermute(lax.ppermute(piece, BOTH, in_plane(second)), BOTH, shifted(second))
        for second, piece in enumerate((up_grad[:cut], up_grad[cut:]))
    ]
    rows, up_grad = lax.optimization_barrier((jnp.concatenate(parts), up_grad))
    rows = lax.all_gather(rows, "tensor", axis=0).reshape(4, 2, 2, n, tokens)

    columns = jnp.broadcast_to(up_grad[None], (RING, n, tokens))
    up, down = up_grad, up_grad
    for step in range(1, RING // 2):
        up, down = lax.ppermute(up, "dp", along_z(1)), lax.ppermute(down, "dp", along_z(-1))
        columns = put(put(columns, up, RING - step), down, step)
    up = lax.ppermute(up[:cut], "dp", along_z(1))
    down = lax.ppermute(down[cut:], "dp", along_z(-1))
    columns = put(put(columns, up, RING // 2), down, RING // 2, cut)

    sent = lax.ppermute(product(rows, columns, 1, cut, jnp.bfloat16), "dp", ACROSS)
    kept = product(rows, columns, 0, cut, jnp.float32)
    total = tokens * lax.axis_size("dp")
    return (kept + sent.astype(jnp.float32)) * (1.0 / total)


def solution(mesh):
    placed = (P("dp", None), P("tensor", None), P("dp", "tensor"))
    return jax.shard_map(
        shards, mesh=mesh, in_specs=placed, out_specs=P("dp", "tensor"), check_vma=False
    )
```

time: 185 us -> 176 us (0.951)
  Pallas kernels: 0 us -> 20.5 us
  matrix products: 18 us -> 3.55 us
  local copies, waits for them, and re-layouts: 22.7 us -> 11.9 us
  starting transfers between devices: 31.9 us -> 27.3 us
  other arithmetic: 1.61 us -> 4.03 us
  waiting for transfers between devices: 96.8 us -> 94.9 us
    pallas_call x0 -> x2, Pallas kernels: none -> 20.5 us  [product(): pl.pallas_call(functools.partial(product_body, cut=cut), grid=(4,), in_sp...]
    ppermute x3 -> x5, waiting for transfers between devices: 49.8 us -> 33.7 us  [the longest x1 13.4 us: shards(): lax.ppermute(product(rows, columns, 1, cut, jnp.bfloat16), 'dp', ACROSS)]
    dot_general x2 -> x0, matrix products: 14.5 us -> none  [partial(): lax.dot_general(jnp.concatenate(blocks, axis=1), columns, (((1,), (1,)),...]
    all_gather x1, waiting for transfers between devices: 8.76 us -> 20.1 us  [shards(): rows = lax.all_gather(rows, 'tensor', axis=0).reshape(4, 2, 2, n, tokens)]
    unnamed x22 -> x2, local copies, waits for them, and re-layouts: 10.8 us -> 1.79 us
    ppermute x3, starting transfers between devices: 11.2 us -> 5.11 us  [shards(): lax.ppermute(down, 'dp', along_z(-1))]
    ppermute x3 -> x5, starting transfers between devices: 10 us -> 15.9 us  [the longest x2 8.69 us: shards(): lax.ppermute(lax.ppermute(piece, BOTH, in_plane(second)), BOTH, shifted(s...]
    ppermute x3, starting transfers between devices: 7.68 us -> 3.22 us  [shards(): lax.ppermute(up, 'dp', along_z(1))]
  transfers between devices with their start and end apart: 12 -> 14, of which waited for: 8 -> 11; matrix products, arithmetic and copies ran while one was open for 10% -> 6% of each run, Pallas kernels for 0% -> 6%
where the time goes in v8:
time: 176 us
  waiting for transfers between devices  94.9 us (54%)
  starting transfers between devices  27.3 us (16%)
  Pallas kernels  20.5 us (12%)
  between operations  13.5 us (8%)
  local copies, waits for them, and re-layouts  11.9 us (7%)
  other arithmetic  4.03 us (2%)
  matrix products  3.55 us (2%)
    ppermute x3, waiting for transfers between devices, shards(): lax.ppermute(up, 'dp', along_z(1))  32.7 us
    pallas_call x2, Pallas kernels, product(): pl.pallas_call(functools.partial(product_body, cut=cut), grid=(4,), in_sp...  20.5 us
    all_gather x1, waiting for transfers between devices, shards(): rows = lax.all_gather(rows, 'tensor', axis=0).reshape(4, 2, 2, n, tokens)  20.1 us
    ppermute x1, waiting for transfers between devices, shards(): lax.ppermute(product(rows, columns, 1, cut, jnp.bfloat16), 'dp', ACROSS)  13.4 us
    ppermute x2, waiting for transfers between devices, shards(): lax.ppermute(lax.ppermute(piece, BOTH, in_plane(second)), BOTH, shifted(s...  12.8 us
    ppermute x2, starting transfers between devices, shards(): lax.ppermute(lax.ppermute(piece, BOTH, in_plane(second)), BOTH, shifted(s...  8.69 us
    ppermute x2, waiting for transfers between devices, shards(): lax.ppermute(piece, BOTH, in_plane(second))  7.49 us
    dynamic_update_slice x8, local copies, waits for them, and re-layouts, put(): lax.dynamic_update_slice(columns, block[None], (PLACES[0].index(offset),...  7.11 us
  transfers between devices with their start and end apart: 14, of which 11 were waited for; matrix products, arithmetic and copies ran while one was open for 6% of the time, Pallas kernels for 6%

profile of v8, /device:TPU:1, one launch (start us, length us, event | category | flops | bytes accessed | tf_op | source)
XLA Modules:
  0.0 175.7 jit_solution(15767149625299967009)
XLA Ops:
  6.5 1.8 %copy-done = bf16[688,2048]{1,0:T(8,128)(2,1)S(1)} copy-done((bf16[688,2048]{1,0:T(8,128)(2,1)S(1)}, bf16[688,2048]{1,0:T(8,128)(2,1)}, u32[]{:S(2)}) %copy-start) | copy-done | bytes 2818072
  8.3 3.6 %fusion.4 = bf16[688,512]{1,0:T(8,128)(2,1)S(1)} fusion(bf16[512,688]{0,1:T(8,128)(2,1)} %param.5, bf16[688,2048]{1,0:T(8,128)(2,1)S(1)} %copy-done, bf16[512,2048]{1,0:T(8,128)(2,1)} %param.3), kind=kOutput, calls=%fused_computation.7 | convolution fusion | flops 1446010880 | bytes 6324224 | tf_op jit(solution)/shard_map/dot_general | solution.py:106
  11.9 4.0 %collective-permute-start = (bf16[352,512]{1,0:T(8,128)(2,1)S(1)}, bf16[352,512]{1,0:T(8,128)(2,1)S(1)}, u32[]{:S(2)}, u32[]{:S(2)}) collective-permute-start(bf16[352,512]{1,0:T(8,128)(2,1)S(1)} %slice.16), channel_id=1, source_target_pairs={{0,0},{1,5},{2,9},{3,13},{4,1},{5,12},{6,8},{7,4},{8,2},{9,7},{10,... | collective-permute-start | bytes 1081352 | tf_op jit(solution)/shard_map/ppermute | solution.py:113
  16.6 7.5 %collective-permute-done = bf16[352,512]{1,0:T(8,128)(2,1)S(1)} collective-permute-done((bf16[352,512]{1,0:T(8,128)(2,1)S(1)}, bf16[352,512]{1,0:T(8,128)(2,1)S(1)}, u32[]{:S(2)}, u32[]{:S(2)}) %collective-permute-start) | collective-permute-done | bytes 360480 | tf_op jit(solution)/shard_map/ppermute | solution.py:113
  24.1 6.8 %collective-permute-start.1 = (bf16[352,512]{1,0:T(8,128)(2,1)S(1)}, bf16[352,512]{1,0:T(8,128)(2,1)S(1)}, u32[]{:S(2)}, u32[]{:S(2)}) collective-permute-start(bf16[352,512]{1,0:T(8,128)(2,1)S(1)} %collective-permute-done), channel_id=1, source_target_pairs={{0,0},{2,2},{20,4},{22,6},{40,8},{42,10},{60,12},{62,14},{65,1},{6... | collective-permute-start | bytes 1081352 | tf_op jit(solution)/shard_map/ppermute | solution.py:113
  30.9 1.9 %collective-permute-start.3 = (bf16[336,512]{1,0:T(8,128)(2,1)S(1)}, bf16[336,512]{1,0:T(8,128)(2,1)S(1)}, u32[]{:S(2)}, u32[]{:S(2)}) collective-permute-start(bf16[336,512]{1,0:T(8,128)(2,1)S(1)} %collective-permute-done.2), channel_id=1, source_target_pairs={{4,4},{6,6},{16,0},{18,2},{44,12},{46,14},{56,8},{58,10},{69,5},{7... | collective-permute-start | bytes 1032200 | tf_op jit(solution)/shard_map/ppermute | solution.py:113
  32.8 12.8 %collective-permute-done.3 = bf16[336,512]{1,0:T(8,128)(2,1)S(1)} collective-permute-done((bf16[336,512]{1,0:T(8,128)(2,1)S(1)}, bf16[336,512]{1,0:T(8,128)(2,1)S(1)}, u32[]{:S(2)}, u32[]{:S(2)}) %collective-permute-start.3) | collective-permute-done | bytes 344096 | tf_op jit(solution)/shard_map/ppermute | solution.py:113
  47.2 2.1 %collective-permute-start.5 = (bf16[688,512]{1,0:T(8,128)(2,1)S(1)}, bf16[688,512]{1,0:T(8,128)(2,1)S(1)}, u32[]{:S(2)}, u32[]{:S(2)}) collective-permute-start(bf16[688,512]{1,0:T(8,128)(2,1)S(1)} %fusion.4), channel_id=1, source_target_pairs={{0,112},{16,0},{32,16},{48,32},{64,48},{80,64},{96,80},{112,96},{1... | collective-permute-start | bytes 2113544 | tf_op jit(solution)/shard_map/ppermute | solution.py:122
  49.3 12.4 %collective-permute-done.4 = bf16[688,512]{1,0:T(8,128)(2,1)S(1)} collective-permute-done((bf16[688,512]{1,0:T(8,128)(2,1)S(1)}, bf16[688,512]{1,0:T(8,128)(2,1)S(1)}, u32[]{:S(2)}, u32[]{:S(2)}) %collective-permute-start.4) | collective-permute-done | bytes 704544 | tf_op jit(solution)/shard_map/ppermute | solution.py:122
  61.7 3.0 %collective-permute-start.7 = (bf16[688,512]{1,0:T(8,128)(2,1)S(1)}, bf16[688,512]{1,0:T(8,128)(2,1)S(1)}, u32[]{:S(2)}, u32[]{:S(2)}) collective-permute-start(bf16[688,512]{1,0:T(8,128)(2,1)S(1)} %collective-permute-done.5), channel_id=1, source_target_pairs={{0,112},{16,0},{32,16},{48,32},{64,48},{80,64},{96,80},{112,96},{1... | collective-permute-start | bytes 2113544 | tf_op jit(solution)/shard_map/ppermute | solution.py:122
  64.7 2.9 %broadcast_in_dim.30 = bf16[8,688,512]{2,1,0:T(8,128)(2,1)} broadcast(bf16[688,512]{1,0:T(8,128)(2,1)S(1)} %fusion.4), dimensions={1,2} | broadcast | bytes 6340608 | tf_op jit(solution)/shard_map/broadcast_in_dim | solution.py:119
  68.5 9.8 %collective-permute-done.6 = bf16[688,512]{1,0:T(8,128)(2,1)S(1)} collective-permute-done((bf16[688,512]{1,0:T(8,128)(2,1)S(1)}, bf16[688,512]{1,0:T(8,128)(2,1)S(1)}, u32[]{:S(2)}, u32[]{:S(2)}) %collective-permute-start.6) | collective-permute-done | bytes 704544 | tf_op jit(solution)/shard_map/ppermute | solution.py:122
  78.3 2.5 %collective-permute-start.8 = (bf16[688,512]{1,0:T(8,128)(2,1)S(1)}, bf16[688,512]{1,0:T(8,128)(2,1)S(1)}, u32[]{:S(2)}, u32[]{:S(2)}) collective-permute-start(bf16[688,512]{1,0:T(8,128)(2,1)S(1)} %collective-permute-done.6), channel_id=1, source_target_pairs={{0,16},{16,32},{32,48},{48,64},{64,80},{80,96},{96,112},{112,0},{1... | collective-permute-start | bytes 2113544 | tf_op jit(solution)/shard_map/ppermute | solution.py:122
  80.9 1.9 %collective-permute-done.7 = bf16[688,512]{1,0:T(8,128)(2,1)S(1)} collective-permute-done((bf16[688,512]{1,0:T(8,128)(2,1)S(1)}, bf16[688,512]{1,0:T(8,128)(2,1)S(1)}, u32[]{:S(2)}, u32[]{:S(2)}) %collective-permute-start.7) | collective-permute-done | bytes 704544 | tf_op jit(solution)/shard_map/ppermute | solution.py:122
  85.6 10.4 %collective-permute-done.8 = bf16[688,512]{1,0:T(8,128)(2,1)S(1)} collective-permute-done((bf16[688,512]{1,0:T(8,128)(2,1)S(1)}, bf16[688,512]{1,0:T(8,128)(2,1)S(1)}, u32[]{:S(2)}, u32[]{:S(2)}) %collective-permute-start.8) | collective-permute-done | bytes 704544 | tf_op jit(solution)/shard_map/ppermute | solution.py:122
  97.5 2.2 %collective-permute-done.9 = bf16[688,512]{1,0:T(8,128)(2,1)S(1)} collective-permute-done((bf16[688,512]{1,0:T(8,128)(2,1)S(1)}, bf16[688,512]{1,0:T(8,128)(2,1)S(1)}, u32[]{:S(2)}, u32[]{:S(2)}) %collective-permute-start.9) | collective-permute-done | bytes 704544 | tf_op jit(solution)/shard_map/ppermute | solution.py:122
  99.7 1.7 collective-permute-start.11
  103.2 3.2 %collective-permute-done.10 = bf16[352,512]{1,0:T(8,128)(2,1)S(1)} collective-permute-done((bf16[352,512]{1,0:T(8,128)(2,1)S(1)}, bf16[352,512]{1,0:T(8,128)(2,1)S(1)}, u32[]{:S(2)}, u32[]{:S(2)}) %collective-permute-start.10) | collective-permute-done | bytes 360480 | tf_op jit(solution)/shard_map/ppermute | solution.py:124
  109.1 20.1 %all-gather.3.cloned.1.call-done = bf16[11008,512]{1,0:T(8,128)(2,1)} async-done(((bf16[688,512]{1,0:T(8,128)(2,1)}), bf16[11008,512]{1,0:T(8,128)(2,1)}) %all-gather.3.cloned.1.call-update) | async-done | bytes 11272208 | tf_op jit(solution)/shard_map/all_gather | solution.py:117
  129.2 10.1 %shard_map.38 = bf16[688,688]{1,0:T(8,128)(2,1)} custom-call(bf16[4,2,2,688,512]{4,3,2,1,0:T(8,128)(2,1)} %bitcast.34, bf16[4,2,2,688,512]{4,3,2,1,0:T(8,128)(2,1)} %bitcast.35, bf16[8,688,512]{2,1,0:T(8,128)(2,1)} %bitcast_dynamic-update-slice_fusion.7.columns_ref), custom_call_target="tpu_custom_call" | custom-call | flops 3877634048 | bytes 25165824 | tf_op jit(solution)/shard_map/pallas_call | solution.py:79
  139.3 2.6 %collective-permute-start.12 = (bf16[688,688]{1,0:T(8,128)(2,1)}, bf16[688,688]{1,0:T(8,128)(2,1)S(1)}, u32[]{:S(2)}, u32[]{:S(2)}) collective-permute-start(bf16[688,688]{1,0:T(8,128)(2,1)} %shard_map.38), channel_id=1, source_target_pairs={{0,128},{16,144},{32,160},{48,176},{64,192},{80,208},{96,224},{112... | collective-permute-start | bytes 2840072 | tf_op jit(solution)/shard_map/ppermute | solution.py:128
  141.9 10.4 %shard_map.37 = f32[688,688]{1,0:T(8,128)} custom-call(bf16[4,2,2,688,512]{4,3,2,1,0:T(8,128)(2,1)} %bitcast.36, bf16[4,2,2,688,512]{4,3,2,1,0:T(8,128)(2,1)} %bitcast.37, bf16[8,688,512]{2,1,0:T(8,128)(2,1)} %bitcast_dynamic-update-slice_fusion.7.columns_ref), custom_call_target="tpu_custom_call" | custom-call | flops 3877634048 | bytes 25165824 | tf_op jit(solution)/shard_map/pallas_call | solution.py:79
  152.3 13.4 %collective-permute-done.12 = bf16[688,688]{1,0:T(8,128)(2,1)S(1)} collective-permute-done((bf16[688,688]{1,0:T(8,128)(2,1)}, bf16[688,688]{1,0:T(8,128)(2,1)S(1)}, u32[]{:S(2)}, u32[]{:S(2)}) %collective-permute-start.12) | collective-permute-done | bytes 946720 | tf_op jit(solution)/shard_map/ppermute | solution.py:128
  165.7 3.1 %add_multiply_fusion = f32[688,688]{1,0:T(8,128)} fusion(f32[688,688]{1,0:T(8,128)} %shard_map.37, bf16[688,688]{1,0:T(8,128)(2,1)S(1)} %collective-permute-done.12), kind=kLoop, calls=%fused_computation | loop fusion | flops 1420032 | bytes 4733440 | tf_op jit(solution)/shard_map/mul | solution.py:131
  (25 shorter events, 12.0 us)
Async XLA Ops:
  6.5 1.8 %copy-start = (bf16[688,2048]{1,0:T(8,128)(2,1)S(1)}, bf16[688,2048]{1,0:T(8,128)(2,1)}, u32[]{:S(2)}) copy-start(bf16[688,2048]{1,0:T(8,128)(2,1)} %param.4) | copy-start | bytes 8454148
  6.5 122.6 %all-gather.3.cloned.1.call-start = ((), (), s32[]{:S(2)}) async-start(), calls=%async_computation | async-start | bytes 11976704 | tf_op jit(solution)/shard_map/all_gather | solution.py:117
  11.9 12.2 %collective-permute-start = (bf16[352,512]{1,0:T(8,128)(2,1)S(1)}, bf16[352,512]{1,0:T(8,128)(2,1)S(1)}, u32[]{:S(2)}, u32[]{:S(2)}) collective-permute-start(bf16[352,512]{1,0:T(8,128)(2,1)S(1)} %slice.16), channel_id=1, source_target_pairs={{0,0},{1,5},{2,9},{3,13},{4,1},{5,12},{6,8},{7,4},{8,2},{9,7},{10,... | collective-permute-start | bytes 1081352 | tf_op jit(solution)/shard_map/ppermute | solution.py:113
  15.9 15.0 %collective-permute-start.2 = (bf16[336,512]{1,0:T(8,128)(2,1)S(1)}, bf16[336,512]{1,0:T(8,128)(2,1)S(1)}, u32[]{:S(2)}, u32[]{:S(2)}) collective-permute-start(bf16[336,512]{1,0:T(8,128)(2,1)S(1)} %slice.17), channel_id=1, source_target_pairs={{0,4},{1,1},{2,13},{3,9},{4,5},{5,8},{6,12},{7,0},{8,6},{9,3},{10,... | collective-permute-start | bytes 1032200 | tf_op jit(solution)/shard_map/ppermute | solution.py:113
  24.1 21.5 %collective-permute-start.1 = (bf16[352,512]{1,0:T(8,128)(2,1)S(1)}, bf16[352,512]{1,0:T(8,128)(2,1)S(1)}, u32[]{:S(2)}, u32[]{:S(2)}) collective-permute-start(bf16[352,512]{1,0:T(8,128)(2,1)S(1)} %collective-permute-done), channel_id=1, source_target_pairs={{0,0},{2,2},{20,4},{22,6},{40,8},{42,10},{60,12},{62,14},{65,1},{6... | collective-permute-start | bytes 1081352 | tf_op jit(solution)/shard_map/ppermute | solution.py:113
  30.9 14.7 %collective-permute-start.3 = (bf16[336,512]{1,0:T(8,128)(2,1)S(1)}, bf16[336,512]{1,0:T(8,128)(2,1)S(1)}, u32[]{:S(2)}, u32[]{:S(2)}) collective-permute-start(bf16[336,512]{1,0:T(8,128)(2,1)S(1)} %collective-permute-done.2), channel_id=1, source_target_pairs={{4,4},{6,6},{16,0},{18,2},{44,12},{46,14},{56,8},{58,10},{69,5},{7... | collective-permute-start | bytes 1032200 | tf_op jit(solution)/shard_map/ppermute | solution.py:113
  46.5 15.2 %collective-permute-start.4 = (bf16[688,512]{1,0:T(8,128)(2,1)S(1)}, bf16[688,512]{1,0:T(8,128)(2,1)S(1)}, u32[]{:S(2)}, u32[]{:S(2)}) collective-permute-start(bf16[688,512]{1,0:T(8,128)(2,1)S(1)} %fusion.4), channel_id=1, source_target_pairs={{0,16},{16,32},{32,48},{48,64},{64,80},{80,96},{96,112},{112,0},{1... | collective-permute-start | bytes 2113544 | tf_op jit(solution)/shard_map/ppermute | solution.py:122
  47.2 14.5 %collective-permute-start.5 = (bf16[688,512]{1,0:T(8,128)(2,1)S(1)}, bf16[688,512]{1,0:T(8,128)(2,1)S(1)}, u32[]{:S(2)}, u32[]{:S(2)}) collective-permute-start(bf16[688,512]{1,0:T(8,128)(2,1)S(1)} %fusion.4), channel_id=1, source_target_pairs={{0,112},{16,0},{32,16},{48,32},{64,48},{80,64},{96,80},{112,96},{1... | collective-permute-start | bytes 2113544 | tf_op jit(solution)/shard_map/ppermute | solution.py:122
  61.7 16.6 %collective-permute-start.6 = (bf16[688,512]{1,0:T(8,128)(2,1)S(1)}, bf16[688,512]{1,0:T(8,128)(2,1)S(1)}, u32[]{:S(2)}, u32[]{:S(2)}) collective-permute-start(bf16[688,512]{1,0:T(8,128)(2,1)S(1)} %collective-permute-done.4), channel_id=1, source_target_pairs={{0,16},{16,32},{32,48},{48,64},{64,80},{80,96},{96,112},{112,0},{1... | collective-permute-start | bytes 2113544 | tf_op jit(solution)/shard_map/ppermute | solution.py:122
  61.7 21.1 %collective-permute-start.7 = (bf16[688,512]{1,0:T(8,128)(2,1)S(1)}, bf16[688,512]{1,0:T(8,128)(2,1)S(1)}, u32[]{:S(2)}, u32[]{:S(2)}) collective-permute-start(bf16[688,512]{1,0:T(8,128)(2,1)S(1)} %collective-permute-done.5), channel_id=1, source_target_pairs={{0,112},{16,0},{32,16},{48,32},{64,48},{80,64},{96,80},{112,96},{1... | collective-permute-start | bytes 2113544 | tf_op jit(solution)/shard_map/ppermute | solution.py:122
  78.3 17.7 %collective-permute-start.8 = (bf16[688,512]{1,0:T(8,128)(2,1)S(1)}, bf16[688,512]{1,0:T(8,128)(2,1)S(1)}, u32[]{:S(2)}, u32[]{:S(2)}) collective-permute-start(bf16[688,512]{1,0:T(8,128)(2,1)S(1)} %collective-permute-done.6), channel_id=1, source_target_pairs={{0,16},{16,32},{32,48},{48,64},{64,80},{80,96},{96,112},{112,0},{1... | collective-permute-start | bytes 2113544 | tf_op jit(solution)/shard_map/ppermute | solution.py:122
  82.8 16.9 %collective-permute-start.9 = (bf16[688,512]{1,0:T(8,128)(2,1)S(1)}, bf16[688,512]{1,0:T(8,128)(2,1)S(1)}, u32[]{:S(2)}, u32[]{:S(2)}) collective-permute-start(bf16[688,512]{1,0:T(8,128)(2,1)S(1)} %collective-permute-done.7), channel_id=1, source_target_pairs={{0,112},{16,0},{32,16},{48,32},{64,48},{80,64},{96,80},{112,96},{1... | collective-permute-start | bytes 2113544 | tf_op jit(solution)/shard_map/ppermute | solution.py:122
  96.1 10.4 %collective-permute-start.10 = (bf16[352,512]{1,0:T(8,128)(2,1)S(1)}, bf16[352,512]{1,0:T(8,128)(2,1)S(1)}, u32[]{:S(2)}, u32[]{:S(2)}) collective-permute-start(bf16[352,512]{1,0:T(8,128)(2,1)S(1)} %slice.18), channel_id=1, source_target_pairs={{0,16},{16,32},{32,48},{48,64},{64,80},{80,96},{96,112},{112,0},{1... | collective-permute-start | bytes 1081352 | tf_op jit(solution)/shard_map/ppermute | solution.py:124
  99.7 8.6 %collective-permute-start.11 = (bf16[336,512]{1,0:T(8,128)(2,1)S(1)}, bf16[336,512]{1,0:T(8,128)(2,1)S(1)}, u32[]{:S(2)}, u32[]{:S(2)}) collective-permute-start(bf16[336,512]{1,0:T(8,128)(2,1)S(1)} %slice.19), channel_id=1, source_target_pairs={{0,112},{16,0},{32,16},{48,32},{64,48},{80,64},{96,80},{112,96},{1... | collective-permute-start | bytes 1032200 | tf_op jit(solution)/shard_map/ppermute | solution.py:125
  139.3 26.4 %collective-permute-start.12 = (bf16[688,688]{1,0:T(8,128)(2,1)}, bf16[688,688]{1,0:T(8,128)(2,1)S(1)}, u32[]{:S(2)}, u32[]{:S(2)}) collective-permute-start(bf16[688,688]{1,0:T(8,128)(2,1)} %shard_map.38), channel_id=1, source_target_pairs={{0,128},{16,144},{32,160},{48,176},{64,192},{80,208},{96,224},{112... | collective-permute-start | bytes 2840072 | tf_op jit(solution)/shard_map/ppermute | solution.py:128
Sparse Core Ops, SparseCore 0:
  46.6 82.5 all-gather.2

commit v9 on v8

--- a/solution.py
+++ b/solution.py
@@ -1,5 +1,3 @@
-import functools
-
 import jax
 import jax.numpy as jnp
 from jax import lax
@@ -46,54 +44,52 @@
 ACROSS = [(i, (i + RING) % 16) for i in range(16)]
 
 
-def product_body(first_ref, second_ref, columns_ref, out_ref, total, *, cut):
+def product_body(rows_ref, columns_ref, out_ref, total):
     k = pl.program_id(0)
+    count = out_ref.shape[0]
 
-    def partial(ref, low, high):
+    def partial():
         return sum(
             lax.dot_general(
-                ref[0, 0, core, low:high], columns_ref[core], (((1,), (1,)), ((), ())),
+                rows_ref[0, 0, core, :count], columns_ref[2 * k + core], (((1,), (1,)), ((), ())),
                 preferred_element_type=jnp.float32,
             )
             for core in range(2)
         )
 
-    n = out_ref.shape[0]
-    for ref, low, high in ((first_ref, 0, cut), (second_ref, cut, n)):
-        @pl.when(k == 0)
-        def _():
-            total[low:high] = partial(ref, low, high)
+    @pl.when(k == 0)
+    def _():
+        total[...] = partial()
 
-        @pl.when((k > 0) & (k < 3))
-        def _():
-            total[low:high] += partial(ref, low, high)
+    @pl.when((k > 0) & (k < 3))
+    def _():
+        total[...] += partial()
 
-        @pl.when(k == 3)
-        def _():
-            out_ref[low:high] = (total[low:high] + partial(ref, low, high)).astype(out_ref.dtype)
+    @pl.when(k == 3)
+    def _():
+        out_ref[...] = (total[...] + partial()).astype(out_ref.dtype)
 
 
-def product(rows, columns, other, cut, kind):
+def product(rows, columns, other, second, cut, kind):
     n, tokens = columns.shape[1:]
-    block = (1, 1, 2, n, tokens)
+    count = n - cut if second else cut
     return pl.pallas_call(
-        functools.partial(product_body, cut=cut),
+        product_body,
         grid=(4,),
         in_specs=[
-            pl.BlockSpec(block, lambda k: (k, other, 0, 0, 0)),
-            pl.BlockSpec(block, lambda k: (k ^ 1, other, 0, 0, 0)),
-            pl.BlockSpec((2, n, tokens), lambda k: (k, 0, 0)),
+            pl.BlockSpec((1, 1, 2, cut, tokens), lambda k: (k ^ second, other, 0, second, 0)),
+            pl.BlockSpec(memory_space=pltpu.VMEM),
         ],
-        out_specs=pl.BlockSpec((n, n), lambda k: (0, 0)),
-        out_shape=jax.ShapeDtypeStruct((n, n), kind),
-        scratch_shapes=[pltpu.VMEM((n, n), jnp.float32)],
+        out_specs=pl.BlockSpec((count, n), lambda k: (0, 0)),
+        out_shape=jax.ShapeDtypeStruct((count, n), kind),
+        scratch_shapes=[pltpu.VMEM((count, n), jnp.float32)],
         compiler_params=pltpu.CompilerParams(
-            dimension_semantics=("arbitrary",), vmem_limit_bytes=56 * 1024 * 1024
+            dimension_semantics=("arbitrary",), vmem_limit_bytes=48 * 1024 * 1024
         ),
         cost_estimate=pl.CostEstimate(
-            flops=2 * n * n * tokens * RING, bytes_accessed=24 * 1024 * 1024, transcendentals=0
+            flops=2 * count * n * tokens * RING, bytes_accessed=8 * 1024 * 1024, transcendentals=0
         ),
-    )(rows, rows, columns)
+    )(rows, columns)
 
 
 def put(columns, block, offset, start=0):
@@ -125,10 +121,17 @@
     down = lax.ppermute(down[cut:], "dp", along_z(-1))
     columns = put(put(columns, up, RING // 2), down, RING // 2, cut)
 
-    sent = lax.ppermute(product(rows, columns, 1, cut, jnp.bfloat16), "dp", ACROSS)
-    kept = product(rows, columns, 0, cut, jnp.float32)
     total = tokens * lax.axis_size("dp")
-    return (kept + sent.astype(jnp.float32)) * (1.0 / total)
+    theirs = [
+        product(rows, columns, 1, second, cut, jnp.bfloat16).reshape(-1, 16, n) for second in range(2)
+    ]
+    sent = [lax.ppermute(part, "dp", ACROSS) for part in theirs]
+    out = jnp.zeros((n, n), jnp.float32)
+    for second in (1, 0):
+        ours = product(rows, columns, 0, second, cut, jnp.float32)
+        part = (ours + sent[second].reshape(-1, n).astype(jnp.float32)) * (1.0 / total)
+        out = lax.dynamic_update_slice(lax.optimization_barrier(out), part, (second * cut, 0))
+    return out
 
 
 def solution(mesh):

time: 176 us -> 171 us (0.972)
  local copies, waits for them, and re-layouts: 11.9 us -> 7.83 us
  other arithmetic: 4.03 us -> 2.09 us
    ppermute x1 -> x2, waiting for transfers between devices: 13.4 us -> 5.71 us  [shards(): sent = [lax.ppermute(part, 'dp', ACROSS) for part in theirs]]
    dynamic_update_slice x8, local copies, waits for them, and re-layouts: 7.11 us -> 0.33 us  [put(): lax.dynamic_update_slice(columns, block[None], (PLACES[0].index(offset),...]
    ppermute x3, waiting for transfers between devices: 32.7 us -> 38.5 us  [shards(): lax.ppermute(up, 'dp', along_z(1))]
    unnamed x2 -> x8, local copies, waits for them, and re-layouts: 1.79 us -> 6.78 us
    mul x1 -> x0, other arithmetic: 3.13 us -> none  [shards(): return (kept + sent.astype(jnp.float32)) * (1.0 / total)]
    broadcast_in_dim x1, local copies, waits for them, and re-layouts: 2.88 us -> 0.48 us  [shards(): columns = jnp.broadcast_to(up_grad[None], (RING, n, tokens))]
    ppermute x1, waiting for transfers between devices: 3.21 us -> 5.13 us  [shards(): up = lax.ppermute(up[:cut], 'dp', along_z(1))]
    pallas_call x2 -> x4, Pallas kernels: 20.5 us -> 21.6 us  [product(): pl.pallas_call(product_body, grid=(4,), in_specs=[pl.BlockSpec((1, 1, 2,...]
  transfers between devices with their start and end apart: 14 -> 15, of which waited for: 11 -> 11; matrix products, arithmetic and copies ran while one was open for 6% -> 1% of each run, Pallas kernels for 6% -> 10%
where the time goes in v9:
time: 171 us
  waiting for transfers between devices  94.1 us (55%)
  starting transfers between devices  27.9 us (16%)
  Pallas kernels  21.6 us (13%)
  between operations  13.6 us (8%)
  local copies, waits for them, and re-layouts  7.83 us (5%)
  matrix products  3.55 us (2%)
  other arithmetic  2.09 us (1%)
    ppermute x3, waiting for transfers between devices, shards(): lax.ppermute(up, 'dp', along_z(1))  38.5 us
    pallas_call x4, Pallas kernels, product(): pl.pallas_call(product_body, grid=(4,), in_specs=[pl.BlockSpec((1, 1, 2,...  21.6 us
    all_gather x1, waiting for transfers between devices, shards(): rows = lax.all_gather(rows, 'tensor', axis=0).reshape(4, 2, 2, n, tokens)  18.6 us
    ppermute x2, waiting for transfers between devices, shards(): lax.ppermute(lax.ppermute(piece, BOTH, in_plane(second)), BOTH, shifted(s...  12.8 us
    ppermute x2, starting transfers between devices, shards(): lax.ppermute(lax.ppermute(piece, BOTH, in_plane(second)), BOTH, shifted(s...  8.69 us
    ppermute x2, waiting for transfers between devices, shards(): lax.ppermute(piece, BOTH, in_plane(second))  7.49 us
    unnamed x8, local copies, waits for them, and re-layouts  6.78 us
    ppermute x2, waiting for transfers between devices, shards(): sent = [lax.ppermute(part, 'dp', ACROSS) for part in theirs]  5.71 us
  transfers between devices with their start and end apart: 15, of which 11 were waited for; matrix products, arithmetic and copies ran while one was open for 1% of the time, Pallas kernels for 10%

profile of v9, /device:TPU:1, one launch (start us, length us, event | category | flops | bytes accessed | tf_op | source)
XLA Modules:
  0.0 170.7 jit_solution(4606708892714972429)
XLA Ops:
  8.3 3.6 %fusion.4 = bf16[688,512]{1,0:T(8,128)(2,1)S(1)} fusion(bf16[512,688]{0,1:T(8,128)(2,1)} %param.5, bf16[688,2048]{1,0:T(8,128)(2,1)S(1)} %copy-done, bf16[512,2048]{1,0:T(8,128)(2,1)} %param.3), kind=kOutput, calls=%fused_computation.6 | convolution fusion | flops 1446010880 | bytes 6324224 | tf_op jit(solution)/shard_map/dot_general | solution.py:102
  11.9 4.0 %collective-permute-start = (bf16[352,512]{1,0:T(8,128)(2,1)S(1)}, bf16[352,512]{1,0:T(8,128)(2,1)S(1)}, u32[]{:S(2)}, u32[]{:S(2)}) collective-permute-start(bf16[352,512]{1,0:T(8,128)(2,1)S(1)} %slice.16), channel_id=1, source_target_pairs={{0,0},{1,5},{2,9},{3,13},{4,1},{5,12},{6,8},{7,4},{8,2},{9,7},{10,... | collective-permute-start | bytes 1081352 | tf_op jit(solution)/shard_map/ppermute | solution.py:109
  16.6 7.5 %collective-permute-done = bf16[352,512]{1,0:T(8,128)(2,1)S(1)} collective-permute-done((bf16[352,512]{1,0:T(8,128)(2,1)S(1)}, bf16[352,512]{1,0:T(8,128)(2,1)S(1)}, u32[]{:S(2)}, u32[]{:S(2)}) %collective-permute-start) | collective-permute-done | bytes 360480 | tf_op jit(solution)/shard_map/ppermute | solution.py:109
  24.1 6.8 %collective-permute-start.1 = (bf16[352,512]{1,0:T(8,128)(2,1)S(1)}, bf16[352,512]{1,0:T(8,128)(2,1)S(1)}, u32[]{:S(2)}, u32[]{:S(2)}) collective-permute-start(bf16[352,512]{1,0:T(8,128)(2,1)S(1)} %collective-permute-done), channel_id=1, source_target_pairs={{0,0},{2,2},{20,4},{22,6},{40,8},{42,10},{60,12},{62,14},{65,1},{6... | collective-permute-start | bytes 1081352 | tf_op jit(solution)/shard_map/ppermute | solution.py:109
  30.9 1.9 %collective-permute-start.3 = (bf16[336,512]{1,0:T(8,128)(2,1)S(1)}, bf16[336,512]{1,0:T(8,128)(2,1)S(1)}, u32[]{:S(2)}, u32[]{:S(2)}) collective-permute-start(bf16[336,512]{1,0:T(8,128)(2,1)S(1)} %collective-permute-done.2), channel_id=1, source_target_pairs={{4,4},{6,6},{16,0},{18,2},{44,12},{46,14},{56,8},{58,10},{69,5},{7... | collective-permute-start | bytes 1032200 | tf_op jit(solution)/shard_map/ppermute | solution.py:109
  32.8 12.8 %collective-permute-done.3 = bf16[336,512]{1,0:T(8,128)(2,1)S(1)} collective-permute-done((bf16[336,512]{1,0:T(8,128)(2,1)S(1)}, bf16[336,512]{1,0:T(8,128)(2,1)S(1)}, u32[]{:S(2)}, u32[]{:S(2)}) %collective-permute-start.3) | collective-permute-done | bytes 344096 | tf_op jit(solution)/shard_map/ppermute | solution.py:109
  47.2 2.1 %collective-permute-start.5 = (bf16[688,512]{1,0:T(8,128)(2,1)S(1)}, bf16[688,512]{1,0:T(8,128)(2,1)S(1)}, u32[]{:S(2)}, u32[]{:S(2)}) collective-permute-start(bf16[688,512]{1,0:T(8,128)(2,1)S(1)} %fusion.4), channel_id=1, source_target_pairs={{0,112},{16,0},{32,16},{48,32},{64,48},{80,64},{96,80},{112,96},{1... | collective-permute-start | bytes 2113544 | tf_op jit(solution)/shard_map/ppermute | solution.py:118
  49.3 12.4 %collective-permute-done.4 = bf16[688,512]{1,0:T(8,128)(2,1)S(1)} collective-permute-done((bf16[688,512]{1,0:T(8,128)(2,1)S(1)}, bf16[688,512]{1,0:T(8,128)(2,1)S(1)}, u32[]{:S(2)}, u32[]{:S(2)}) %collective-permute-start.4) | collective-permute-done | bytes 704544 | tf_op jit(solution)/shard_map/ppermute | solution.py:118
  61.7 3.0 %collective-permute-start.7 = (bf16[688,512]{1,0:T(8,128)(2,1)S(1)}, bf16[688,512]{1,0:T(8,128)(2,1)S(1)}, u32[]{:S(2)}, u32[]{:S(2)}) collective-permute-start(bf16[688,512]{1,0:T(8,128)(2,1)S(1)} %collective-permute-done.5), channel_id=1, source_target_pairs={{0,112},{16,0},{32,16},{48,32},{64,48},{80,64},{96,80},{112,96},{1... | collective-permute-start | bytes 2113544 | tf_op jit(solution)/shard_map/ppermute | solution.py:118
  65.3 13.0 %collective-permute-done.6 = bf16[688,512]{1,0:T(8,128)(2,1)S(1)} collective-permute-done((bf16[688,512]{1,0:T(8,128)(2,1)S(1)}, bf16[688,512]{1,0:T(8,128)(2,1)S(1)}, u32[]{:S(2)}, u32[]{:S(2)}) %collective-permute-start.6) | collective-permute-done | bytes 704544 | tf_op jit(solution)/shard_map/ppermute | solution.py:118
  78.3 2.5 %collective-permute-start.8 = (bf16[688,512]{1,0:T(8,128)(2,1)S(1)}, bf16[688,512]{1,0:T(8,128)(2,1)S(1)}, u32[]{:S(2)}, u32[]{:S(2)}) collective-permute-start(bf16[688,512]{1,0:T(8,128)(2,1)S(1)} %collective-permute-done.6), channel_id=1, source_target_pairs={{0,16},{16,32},{32,48},{48,64},{64,80},{80,96},{96,112},{112,0},{1... | collective-permute-start | bytes 2113544 | tf_op jit(solution)/shard_map/ppermute | solution.py:118
  80.9 1.9 %collective-permute-done.7 = bf16[688,512]{1,0:T(8,128)(2,1)S(1)} collective-permute-done((bf16[688,512]{1,0:T(8,128)(2,1)S(1)}, bf16[688,512]{1,0:T(8,128)(2,1)S(1)}, u32[]{:S(2)}, u32[]{:S(2)}) %collective-permute-start.7) | collective-permute-done | bytes 704544 | tf_op jit(solution)/shard_map/ppermute | solution.py:118
  82.9 13.1 %collective-permute-done.8 = bf16[688,512]{1,0:T(8,128)(2,1)S(1)} collective-permute-done((bf16[688,512]{1,0:T(8,128)(2,1)S(1)}, bf16[688,512]{1,0:T(8,128)(2,1)S(1)}, u32[]{:S(2)}, u32[]{:S(2)}) %collective-permute-start.8) | collective-permute-done | bytes 704544 | tf_op jit(solution)/shard_map/ppermute | solution.py:118
  97.5 2.2 %collective-permute-done.9 = bf16[688,512]{1,0:T(8,128)(2,1)S(1)} collective-permute-done((bf16[688,512]{1,0:T(8,128)(2,1)S(1)}, bf16[688,512]{1,0:T(8,128)(2,1)S(1)}, u32[]{:S(2)}, u32[]{:S(2)}) %collective-permute-start.9) | collective-permute-done | bytes 704544 | tf_op jit(solution)/shard_map/ppermute | solution.py:118
  101.3 5.1 %collective-permute-done.10 = bf16[352,512]{1,0:T(8,128)(2,1)S(1)} collective-permute-done((bf16[352,512]{1,0:T(8,128)(2,1)S(1)}, bf16[352,512]{1,0:T(8,128)(2,1)S(1)}, u32[]{:S(2)}, u32[]{:S(2)}) %collective-permute-start.10) | collective-permute-done | bytes 360480 | tf_op jit(solution)/shard_map/ppermute | solution.py:120
  108.2 2.4 %copy-done.1 = bf16[8,688,512]{2,1,0:T(8,128)(2,1)} copy-done((bf16[8,688,512]{2,1,0:T(8,128)(2,1)}, bf16[8,688,512]{2,1,0:T(8,128)(2,1)S(1)}, u32[]{:S(2)}) %copy-start.1) | copy-done | bytes 5636120
  110.6 18.6 %all-gather.3.cloned.1.call-done = bf16[11008,512]{1,0:T(8,128)(2,1)} async-done(((bf16[688,512]{1,0:T(8,128)(2,1)}), bf16[11008,512]{1,0:T(8,128)(2,1)}) %all-gather.3.cloned.1.call-update) | async-done | bytes 11272208 | tf_op jit(solution)/shard_map/all_gather | solution.py:113
  129.2 2.6 %copy-done.2 = bf16[8,688,512]{2,1,0:T(8,128)(2,1)S(1)} copy-done((bf16[8,688,512]{2,1,0:T(8,128)(2,1)S(1)}, bf16[8,688,512]{2,1,0:T(8,128)(2,1)}, u32[]{:S(2)}) %copy-start.2) | copy-done | bytes 5636120
  131.8 4.5 %shard_map.38 = bf16[336,688]{1,0:T(8,128)(2,1)S(1)} custom-call(bf16[4,2,2,688,512]{4,3,2,1,0:T(8,128)(2,1)} %bitcast.42, bf16[8,688,512]{2,1,0:T(8,128)(2,1)S(1)} %copy-done.2), custom_call_target="tpu_custom_call" | custom-call | flops 1893728256 | bytes 8388608 | tf_op jit(solution)/shard_map/pallas_call | solution.py:76
  136.3 2.9 %collective-permute-start.12 = (bf16[21,16,688]{2,1,0:T(8,128)(2,1)S(1)}, bf16[21,16,688]{2,1,0:T(8,128)(2,1)S(1)}, u32[]{:S(2)}, u32[]{:S(2)}) collective-permute-start(bf16[21,16,688]{2,1,0:T(8,128)(2,1)S(1)} %bitcast.41), channel_id=1, source_target_pairs={{0,128},{16,144},{32,160},{48,176},{64,192},{80,208},{96,224},{112... | collective-permute-start | bytes 1387016 | tf_op jit(solution)/shard_map/ppermute | solution.py:128
  139.1 4.6 %shard_map.40 = bf16[352,688]{1,0:T(8,128)(2,1)S(1)} custom-call(bf16[4,2,2,688,512]{4,3,2,1,0:T(8,128)(2,1)} %bitcast.43, bf16[8,688,512]{2,1,0:T(8,128)(2,1)S(1)} %copy-done.2), custom_call_target="tpu_custom_call" | custom-call | flops 1983905792 | bytes 8388608 | tf_op jit(solution)/shard_map/pallas_call | solution.py:76
  144.2 6.2 %shard_map.37 = f32[336,688]{1,0:T(8,128)S(1)} custom-call(bf16[4,2,2,688,512]{4,3,2,1,0:T(8,128)(2,1)} %bitcast.44, bf16[8,688,512]{2,1,0:T(8,128)(2,1)} %copy-done.1), custom_call_target="tpu_custom_call" | custom-call | flops 1893728256 | bytes 8388608 | tf_op jit(solution)/shard_map/pallas_call | solution.py:76
  150.4 6.3 %shard_map.39 = f32[352,688]{1,0:T(8,128)S(1)} custom-call(bf16[4,2,2,688,512]{4,3,2,1,0:T(8,128)(2,1)} %bitcast.45, bf16[8,688,512]{2,1,0:T(8,128)(2,1)} %copy-done.1), custom_call_target="tpu_custom_call" | custom-call | flops 1983905792 | bytes 8388608 | tf_op jit(solution)/shard_map/pallas_call | solution.py:76
  157.0 5.7 %collective-permute-done.13 = bf16[22,16,688]{2,1,0:T(8,128)(2,1)S(1)} collective-permute-done((bf16[22,16,688]{2,1,0:T(8,128)(2,1)S(1)}, bf16[22,16,688]{2,1,0:T(8,128)(2,1)S(1)}, u32[]{:S(2)}, u32[]{:S(2)}) %collective-permute-start.13) | collective-permute-done | bytes 484384 | tf_op jit(solution)/shard_map/ppermute | solution.py:128
  (37 shorter events, 11.4 us)
Async XLA Ops:
  6.5 1.8 %copy-start = (bf16[688,2048]{1,0:T(8,128)(2,1)S(1)}, bf16[688,2048]{1,0:T(8,128)(2,1)}, u32[]{:S(2)}) copy-start(bf16[688,2048]{1,0:T(8,128)(2,1)} %param.4) | copy-start | bytes 8454148
  6.5 122.6 %all-gather.3.cloned.1.call-start = ((), (), s32[]{:S(2)}) async-start(), calls=%async_computation | async-start | bytes 11976704 | tf_op jit(solution)/shard_map/all_gather | solution.py:113
  11.9 12.2 %collective-permute-start = (bf16[352,512]{1,0:T(8,128)(2,1)S(1)}, bf16[352,512]{1,0:T(8,128)(2,1)S(1)}, u32[]{:S(2)}, u32[]{:S(2)}) collective-permute-start(bf16[352,512]{1,0:T(8,128)(2,1)S(1)} %slice.16), channel_id=1, source_target_pairs={{0,0},{1,5},{2,9},{3,13},{4,1},{5,12},{6,8},{7,4},{8,2},{9,7},{10,... | collective-permute-start | bytes 1081352 | tf_op jit(solution)/shard_map/ppermute | solution.py:109
  15.9 15.0 %collective-permute-start.2 = (bf16[336,512]{1,0:T(8,128)(2,1)S(1)}, bf16[336,512]{1,0:T(8,128)(2,1)S(1)}, u32[]{:S(2)}, u32[]{:S(2)}) collective-permute-start(bf16[336,512]{1,0:T(8,128)(2,1)S(1)} %slice.17), channel_id=1, source_target_pairs={{0,4},{1,1},{2,13},{3,9},{4,5},{5,8},{6,12},{7,0},{8,6},{9,3},{10,... | collective-permute-start | bytes 1032200 | tf_op jit(solution)/shard_map/ppermute | solution.py:109
  24.1 21.5 %collective-permute-start.1 = (bf16[352,512]{1,0:T(8,128)(2,1)S(1)}, bf16[352,512]{1,0:T(8,128)(2,1)S(1)}, u32[]{:S(2)}, u32[]{:S(2)}) collective-permute-start(bf16[352,512]{1,0:T(8,128)(2,1)S(1)} %collective-permute-done), channel_id=1, source_target_pairs={{0,0},{2,2},{20,4},{22,6},{40,8},{42,10},{60,12},{62,14},{65,1},{6... | collective-permute-start | bytes 1081352 | tf_op jit(solution)/shard_map/ppermute | solution.py:109
  30.9 14.7 %collective-permute-start.3 = (bf16[336,512]{1,0:T(8,128)(2,1)S(1)}, bf16[336,512]{1,0:T(8,128)(2,1)S(1)}, u32[]{:S(2)}, u32[]{:S(2)}) collective-permute-start(bf16[336,512]{1,0:T(8,128)(2,1)S(1)} %collective-permute-done.2), channel_id=1, source_target_pairs={{4,4},{6,6},{16,0},{18,2},{44,12},{46,14},{56,8},{58,10},{69,5},{7... | collective-permute-start | bytes 1032200 | tf_op jit(solution)/shard_map/ppermute | solution.py:109
  46.5 15.2 %collective-permute-start.4 = (bf16[688,512]{1,0:T(8,128)(2,1)S(1)}, bf16[688,512]{1,0:T(8,128)(2,1)S(1)}, u32[]{:S(2)}, u32[]{:S(2)}) collective-permute-start(bf16[688,512]{1,0:T(8,128)(2,1)S(1)} %fusion.4), channel_id=1, source_target_pairs={{0,16},{16,32},{32,48},{48,64},{64,80},{80,96},{96,112},{112,0},{1... | collective-permute-start | bytes 2113544 | tf_op jit(solution)/shard_map/ppermute | solution.py:118
  47.2 14.5 %collective-permute-start.5 = (bf16[688,512]{1,0:T(8,128)(2,1)S(1)}, bf16[688,512]{1,0:T(8,128)(2,1)S(1)}, u32[]{:S(2)}, u32[]{:S(2)}) collective-permute-start(bf16[688,512]{1,0:T(8,128)(2,1)S(1)} %fusion.4), channel_id=1, source_target_pairs={{0,112},{16,0},{32,16},{48,32},{64,48},{80,64},{96,80},{112,96},{1... | collective-permute-start | bytes 2113544 | tf_op jit(solution)/shard_map/ppermute | solution.py:118
  61.7 16.6 %collective-permute-start.6 = (bf16[688,512]{1,0:T(8,128)(2,1)S(1)}, bf16[688,512]{1,0:T(8,128)(2,1)S(1)}, u32[]{:S(2)}, u32[]{:S(2)}) collective-permute-start(bf16[688,512]{1,0:T(8,128)(2,1)S(1)} %collective-permute-done.4), channel_id=1, source_target_pairs={{0,16},{16,32},{32,48},{48,64},{64,80},{80,96},{96,112},{112,0},{1... | collective-permute-start | bytes 2113544 | tf_op jit(solution)/shard_map/ppermute | solution.py:118
  61.7 21.1 %collective-permute-start.7 = (bf16[688,512]{1,0:T(8,128)(2,1)S(1)}, bf16[688,512]{1,0:T(8,128)(2,1)S(1)}, u32[]{:S(2)}, u32[]{:S(2)}) collective-permute-start(bf16[688,512]{1,0:T(8,128)(2,1)S(1)} %collective-permute-done.5), channel_id=1, source_target_pairs={{0,112},{16,0},{32,16},{48,32},{64,48},{80,64},{96,80},{112,96},{1... | collective-permute-start | bytes 2113544 | tf_op jit(solution)/shard_map/ppermute | solution.py:118
  78.3 17.7 %collective-permute-start.8 = (bf16[688,512]{1,0:T(8,128)(2,1)S(1)}, bf16[688,512]{1,0:T(8,128)(2,1)S(1)}, u32[]{:S(2)}, u32[]{:S(2)}) collective-permute-start(bf16[688,512]{1,0:T(8,128)(2,1)S(1)} %collective-permute-done.6), channel_id=1, source_target_pairs={{0,16},{16,32},{32,48},{48,64},{64,80},{80,96},{96,112},{112,0},{1... | collective-permute-start | bytes 2113544 | tf_op jit(solution)/shard_map/ppermute | solution.py:118
  82.8 16.9 %collective-permute-start.9 = (bf16[688,512]{1,0:T(8,128)(2,1)S(1)}, bf16[688,512]{1,0:T(8,128)(2,1)S(1)}, u32[]{:S(2)}, u32[]{:S(2)}) collective-permute-start(bf16[688,512]{1,0:T(8,128)(2,1)S(1)} %collective-permute-done.7), channel_id=1, source_target_pairs={{0,112},{16,0},{32,16},{48,32},{64,48},{80,64},{96,80},{112,96},{1... | collective-permute-start | bytes 2113544 | tf_op jit(solution)/shard_map/ppermute | solution.py:118
  96.1 10.4 %collective-permute-start.10 = (bf16[352,512]{1,0:T(8,128)(2,1)S(1)}, bf16[352,512]{1,0:T(8,128)(2,1)S(1)}, u32[]{:S(2)}, u32[]{:S(2)}) collective-permute-start(bf16[352,512]{1,0:T(8,128)(2,1)S(1)} %slice.18), channel_id=1, source_target_pairs={{0,16},{16,32},{32,48},{48,64},{64,80},{80,96},{96,112},{112,0},{1... | collective-permute-start | bytes 1081352 | tf_op jit(solution)/shard_map/ppermute | solution.py:120
  99.7 8.4 %collective-permute-start.11 = (bf16[336,512]{1,0:T(8,128)(2,1)S(1)}, bf16[336,512]{1,0:T(8,128)(2,1)S(1)}, u32[]{:S(2)}, u32[]{:S(2)}) collective-permute-start(bf16[336,512]{1,0:T(8,128)(2,1)S(1)} %slice.19), channel_id=1, source_target_pairs={{0,112},{16,0},{32,16},{48,32},{64,48},{80,64},{96,80},{112,96},{1... | collective-permute-start | bytes 1032200 | tf_op jit(solution)/shard_map/ppermute | solution.py:121
  108.2 2.4 %copy-start.1 = (bf16[8,688,512]{2,1,0:T(8,128)(2,1)}, bf16[8,688,512]{2,1,0:T(8,128)(2,1)S(1)}, u32[]{:S(2)}) copy-start(bf16[8,688,512]{2,1,0:T(8,128)(2,1)S(1)} %bitcast_dynamic-update-slice_fusion.7.columns_ref) | copy-start | bytes 16908292
  129.2 2.6 %copy-start.2 = (bf16[8,688,512]{2,1,0:T(8,128)(2,1)S(1)}, bf16[8,688,512]{2,1,0:T(8,128)(2,1)}, u32[]{:S(2)}) copy-start(bf16[8,688,512]{2,1,0:T(8,128)(2,1)} %copy-done.1) | copy-start | bytes 16908292
  136.3 20.5 %collective-permute-start.12 = (bf16[21,16,688]{2,1,0:T(8,128)(2,1)S(1)}, bf16[21,16,688]{2,1,0:T(8,128)(2,1)S(1)}, u32[]{:S(2)}, u32[]{:S(2)}) collective-permute-start(bf16[21,16,688]{2,1,0:T(8,128)(2,1)S(1)} %bitcast.41), channel_id=1, source_target_pairs={{0,128},{16,144},{32,160},{48,176},{64,192},{80,208},{96,224},{112... | collective-permute-start | bytes 1387016 | tf_op jit(solution)/shard_map/ppermute | solution.py:128
  143.7 19.0 %collective-permute-start.13 = (bf16[22,16,688]{2,1,0:T(8,128)(2,1)S(1)}, bf16[22,16,688]{2,1,0:T(8,128)(2,1)S(1)}, u32[]{:S(2)}, u32[]{:S(2)}) collective-permute-start(bf16[22,16,688]{2,1,0:T(8,128)(2,1)S(1)} %bitcast.40), channel_id=1, source_target_pairs={{0,128},{16,144},{32,160},{48,176},{64,192},{80,208},{96,224},{112... | collective-permute-start | bytes 1453064 | tf_op jit(solution)/shard_map/ppermute | solution.py:128
  157.0 5.7 %copy-start.3 = (f32[688,688]{1,0:T(8,128)}, f32[688,688]{1,0:T(8,128)S(1)}, u32[]{:S(2)}) copy-start(f32[688,688]{1,0:T(8,128)S(1)} %fusion.8) | copy-start | bytes 5680132
Sparse Core Ops, SparseCore 0:
  46.6 82.5 all-gather.2

commit v10 on v9

v10 whole, which is shorter than its diff:
```python
import jax
import jax.numpy as jnp
from jax import lax
from jax.experimental import pallas as pl
from jax.experimental.pallas import tpu as pltpu
from jax.sharding import PartitionSpec as P

BOTH = ("dp", "tensor")
RING = 8
PARTS = 4
PLACES = (0, 4, 1, 7, 2, 6, 3, 5)


def place(offset, other, part):
    pair, core = divmod(PLACES.index(offset), 2)
    return (pair + part) % 4 * 4 + other * 2 + core


def in_plane(part):
    pairs = []
    for h in range(2):
        for source in range(RING):
            for b in range(2):
                for z in range(RING):
                    plane = (h * RING + source) * 16
                    pairs.append((plane + b * RING + z, plane + place((source - z) % RING, b ^ h, part)))
    return pairs


def shifted(part):
    pairs = []
    for h in range(2):
        for z in range(RING):
            for offset in range(RING):
                for other in range(2):
                    t = place(offset, other, part)
                    pairs.append(((h * RING + (z + offset) % RING) * 16 + t, (h * RING + z) * 16 + t))
    return pairs


def along_z(step):
    return [(h * RING + z, h * RING + (z + step) % RING) for h in range(2) for z in range(RING)]


ACROSS = [(i, (i + RING) % 16) for i in range(16)]


def product_body(low_ref, high_ref, columns_ref, out_ref, total):
    k = pl.program_id(0)
    low = low_ref.shape[3]
    high = out_ref.shape[0] - low

    def partial():
        return sum(
            lax.dot_general(
                jnp.concatenate([low_ref[0, 0, core], high_ref[0, 0, core, :high]]),
                columns_ref[2 * k + core], (((1,), (1,)), ((), ())),
                preferred_element_type=jnp.float32,
            )
            for core in range(2)
        )

    @pl.when(k == 0)
    def _():
        total[...] = partial()

    @pl.when((k > 0) & (k < 3))
    def _():
        total[...] += partial()

    @pl.when(k == 3)
    def _():
        out_ref[...] = (total[...] + partial()).astype(out_ref.dtype)


def product(rows, columns, other, second, size, kind):
    n, tokens = columns.shape[1:]
    count = n - 2 * size if second else 2 * size

    def part_spec(part):
        return pl.BlockSpec((1, 1, 2, size, tokens), lambda k: ((k + part) & 3, other, 0, part, 0))

    return pl.pallas_call(
        product_body,
        grid=(4,),
        in_specs=[
            part_spec(2 * second), part_spec(2 * second + 1), pl.BlockSpec(memory_space=pltpu.VMEM)
        ],
        out_specs=pl.BlockSpec((count, n), lambda k: (0, 0)),
        out_shape=jax.ShapeDtypeStruct((count, n), kind),
        scratch_shapes=[pltpu.VMEM((count, n), jnp.float32)],
        compiler_params=pltpu.CompilerParams(
            dimension_semantics=("arbitrary",), vmem_limit_bytes=48 * 1024 * 1024
        ),
        cost_estimate=pl.CostEstimate(
            flops=2 * count * n * tokens * RING, bytes_accessed=8 * 1024 * 1024, transcendentals=0
        ),
    )(rows, rows, columns)


def put(columns, block, offset, start=0):
    return lax.dynamic_update_slice(columns, block[None], (PLACES.index(offset), start, 0))


def shards(out_grad, down_weight, gate_pre):
    n, tokens = down_weight.shape[0], out_grad.shape[0]
    size = -(-n // (16 * PARTS)) * 16
    cut = 2 * size
    hidden_grad = lax.dot_general(
        down_weight, out_grad, (((1,), (1,)), ((), ())), preferred_element_type=jnp.float32
    ).astype(jnp.bfloat16)
    up_grad = (hidden_grad.astype(jnp.float32) * jax.nn.silu(gate_pre.T.astype(jnp.float32))).astype(
        jnp.bfloat16
    )
    parts = [
        lax.ppermute(
            lax.ppermute(up_grad[part * size : (part + 1) * size], BOTH, in_plane(part)), BOTH, shifted(part)
        )
        for part in range(PARTS)
    ]
    rows, up_grad = lax.optimization_barrier((jnp.concatenate(parts), up_grad))
    rows = lax.all_gather(rows, "tensor", axis=0).reshape(4, 2, 2, n, tokens)

    columns = jnp.broadcast_to(up_grad[None], (RING, n, tokens))
    up, down = up_grad, up_grad
    for step in range(1, RING // 2):
        up, down = lax.ppermute(up, "dp", along_z(1)), lax.ppermute(down, "dp", along_z(-1))
        columns = put(put(columns, up, RING - step), down, step)
    up = lax.ppermute(up[:cut], "dp", along_z(1))
    down = lax.ppermute(down[cut:], "dp", along_z(-1))
    columns = put(put(columns, up, RING // 2), down, RING // 2, cut)

    total = tokens * lax.axis_size("dp")
    theirs = [
        product(rows, columns, 1, second, size, jnp.bfloat16).reshape(-1, 16, n) for second in range(2)
    ]
    sent = [lax.ppermute(part, "dp", ACROSS) for part in theirs]
    out = jnp.zeros((n, n), jnp.float32)
    for second in (1, 0):
        ours = product(rows, columns, 0, second, size, jnp.float32)
        part = (ours + sent[second].reshape(-1, n).astype(jnp.float32)) * (1.0 / total)
        out = lax.dynamic_update_slice(lax.optimization_barrier(out), part, (second * cut, 0))
    return out


def solution(mesh):
    placed = (P("dp", None), P("tensor", None), P("dp", "tensor"))
    return jax.shard_map(
        shards, mesh=mesh, in_specs=placed, out_specs=P("dp", "tensor"), check_vma=False
    )
```

time: 171 us -> 164 us (0.959); the launches traced: 171 us -> 162 us
  waiting for transfers between devices: 94.1 us -> 65.8 us
  starting transfers between devices: 27.9 us -> 47.2 us
    ppermute x4 -> x8, starting transfers between devices: 13.3 us -> 31.5 us  [the longest x4 17.7 us: shards(): lax.ppermute(lax.ppermute(up_grad[part * size:(part + 1) * size], BOTH, i...]
    all_gather x1, waiting for transfers between devices: 18.6 us -> 1.36 us  [shards(): rows = lax.all_gather(rows, 'tensor', axis=0).reshape(4, 2, 2, n, tokens)]
    ppermute x4 -> x8, waiting for transfers between devices: 20.3 us -> 10.5 us  [the longest x4 10.5 us: shards(): lax.ppermute(lax.ppermute(up_grad[part * size:(part + 1) * size], BOTH, i...]
    ppermute x3, waiting for transfers between devices: 38.5 us -> 44 us  [shards(): lax.ppermute(up, 'dp', along_z(1))]
    ppermute x3, waiting for transfers between devices: 4.16 us -> 0.01 us  [shards(): lax.ppermute(down, 'dp', along_z(-1))]
    ppermute x3, starting transfers between devices: 5.11 us -> 9.12 us  [shards(): lax.ppermute(down, 'dp', along_z(-1))]
    ppermute x3, starting transfers between devices: 3.22 us -> 0.09 us  [shards(): lax.ppermute(up, 'dp', along_z(1))]
  transfers between devices with their start and end apart: 15 -> 19, of which waited for: 11 -> 7; matrix products, arithmetic and copies ran while one was open for 1% -> 1% of each run, Pallas kernels for 10% -> 11%
where the time goes in v10:
time: 164 us; the launch traced here: 162 us
  waiting for transfers between devices  65.8 us (40%)
  starting transfers between devices  47.2 us (29%)
  Pallas kernels  21.6 us (13%)
  between operations  13.7 us (8%)
  local copies, waits for them, and re-layouts  7.84 us (5%)
  matrix products  3.55 us (2%)
  other arithmetic  2.09 us (1%)
    ppermute x3, waiting for transfers between devices, shards(): lax.ppermute(up, 'dp', along_z(1))  44 us
    pallas_call x4, Pallas kernels, product(): pl.pallas_call(product_body, grid=(4,), in_specs=[part_spec(2 * second),...  21.6 us
    ppermute x4, starting transfers between devices, shards(): lax.ppermute(lax.ppermute(up_grad[part * size:(part + 1) * size], BOTH, i...  17.7 us
    ppermute x4, starting transfers between devices, shards(): lax.ppermute(up_grad[part * size:(part + 1) * size], BOTH, in_plane(part))  13.8 us
    ppermute x4, waiting for transfers between devices, shards(): lax.ppermute(lax.ppermute(up_grad[part * size:(part + 1) * size], BOTH, i...  10.5 us
    ppermute x3, starting transfers between devices, shards(): lax.ppermute(down, 'dp', along_z(-1))  9.12 us
    unnamed x8, local copies, waits for them, and re-layouts  6.79 us
    ppermute x1, waiting for transfers between devices, shards(): up = lax.ppermute(up[:cut], 'dp', along_z(1))  5.79 us
  transfers between devices with their start and end apart: 19, of which 7 were waited for; matrix products, arithmetic and copies ran while one was open for 1% of the time, Pallas kernels for 11%

profile of v10, /device:TPU:1, one launch (start us, length us, event | category | flops | bytes accessed | tf_op | source)
XLA Modules:
  0.0 161.9 jit_solution(10778163064099671703)
XLA Ops:
  8.3 3.6 %fusion.4 = bf16[688,512]{1,0:T(8,128)(2,1)S(1)} fusion(bf16[512,688]{0,1:T(8,128)(2,1)} %param.5, bf16[688,2048]{1,0:T(8,128)(2,1)S(1)} %copy-done, bf16[512,2048]{1,0:T(8,128)(2,1)} %param.3), kind=kOutput, calls=%fused_computation.6 | convolution fusion | flops 1446010880 | bytes 6324224 | tf_op jit(solution)/shard_map/dot_general | solution.py:109
  11.9 4.0 %collective-permute-start = (bf16[176,512]{1,0:T(8,128)(2,1)S(1)}, bf16[176,512]{1,0:T(8,128)(2,1)S(1)}, u32[]{:S(2)}, u32[]{:S(2)}) collective-permute-start(bf16[176,512]{1,0:T(8,128)(2,1)S(1)} %get-tuple-element.9), channel_id=1, source_target_pairs={{0,0},{1,5},{2,9},{3,13},{4,1},{5,12},{6,8},{7,4},{8,2},{9,7},{10,... | collective-permute-start | bytes 540680 | tf_op jit(solution)/shard_map/ppermute | solution.py:117
  15.9 4.7 %collective-permute-start.2 = (bf16[176,512]{1,0:T(8,128)(2,1)S(1)}, bf16[176,512]{1,0:T(8,128)(2,1)S(1)}, u32[]{:S(2)}, u32[]{:S(2)}) collective-permute-start(bf16[176,512]{1,0:T(8,128)(2,1)S(1)} %get-tuple-element.11), channel_id=1, source_target_pairs={{0,4},{1,9},{2,13},{3,1},{4,5},{5,0},{6,12},{7,8},{8,6},{9,11},{10... | collective-permute-start | bytes 540680 | tf_op jit(solution)/shard_map/ppermute | solution.py:117
  20.6 4.5 %collective-permute-start.4 = (bf16[176,512]{1,0:T(8,128)(2,1)S(1)}, bf16[176,512]{1,0:T(8,128)(2,1)S(1)}, u32[]{:S(2)}, u32[]{:S(2)}) collective-permute-start(bf16[176,512]{1,0:T(8,128)(2,1)S(1)} %get-tuple-element.10), channel_id=1, source_target_pairs={{0,8},{1,13},{2,1},{3,5},{4,9},{5,4},{6,0},{7,12},{8,10},{9,15},{1... | collective-permute-start | bytes 540680 | tf_op jit(solution)/shard_map/ppermute | solution.py:117
  25.8 9.5 %collective-permute-start.1 = (bf16[176,512]{1,0:T(8,128)(2,1)S(1)}, bf16[176,512]{1,0:T(8,128)(2,1)S(1)}, u32[]{:S(2)}, u32[]{:S(2)}) collective-permute-start(bf16[176,512]{1,0:T(8,128)(2,1)S(1)} %collective-permute-done), channel_id=1, source_target_pairs={{0,0},{2,2},{20,4},{22,6},{40,8},{42,10},{60,12},{62,14},{65,1},{6... | collective-permute-start | bytes 540680 | tf_op jit(solution)/shard_map/ppermute | solution.py:116
  35.3 3.3 %collective-permute-start.3 = (bf16[176,512]{1,0:T(8,128)(2,1)S(1)}, bf16[176,512]{1,0:T(8,128)(2,1)S(1)}, u32[]{:S(2)}, u32[]{:S(2)}) collective-permute-start(bf16[176,512]{1,0:T(8,128)(2,1)S(1)} %collective-permute-done.2), channel_id=1, source_target_pairs={{4,4},{6,6},{24,8},{26,10},{44,12},{46,14},{48,0},{50,2},{69,5},{7... | collective-permute-start | bytes 540680 | tf_op jit(solution)/shard_map/ppermute | solution.py:116
  38.7 3.0 %collective-permute-start.5 = (bf16[176,512]{1,0:T(8,128)(2,1)S(1)}, bf16[176,512]{1,0:T(8,128)(2,1)S(1)}, u32[]{:S(2)}, u32[]{:S(2)}) collective-permute-start(bf16[176,512]{1,0:T(8,128)(2,1)S(1)} %collective-permute-done.4), channel_id=1, source_target_pairs={{8,8},{10,10},{28,12},{30,14},{32,0},{34,2},{52,4},{54,6},{73,9},{... | collective-permute-start | bytes 540680 | tf_op jit(solution)/shard_map/ppermute | solution.py:116
  43.6 10.5 %collective-permute-done.7 = bf16[160,512]{1,0:T(8,128)(2,1)S(1)} collective-permute-done((bf16[160,512]{1,0:T(8,128)(2,1)S(1)}, bf16[160,512]{1,0:T(8,128)(2,1)S(1)}, u32[]{:S(2)}, u32[]{:S(2)}) %collective-permute-start.7) | collective-permute-done | bytes 163872 | tf_op jit(solution)/shard_map/ppermute | solution.py:116
  55.1 2.7 %collective-permute-start.9 = (bf16[688,512]{1,0:T(8,128)(2,1)S(1)}, bf16[688,512]{1,0:T(8,128)(2,1)S(1)}, u32[]{:S(2)}, u32[]{:S(2)}) collective-permute-start(bf16[688,512]{1,0:T(8,128)(2,1)S(1)} %fusion.4), channel_id=1, source_target_pairs={{0,112},{16,0},{32,16},{48,32},{64,48},{80,64},{96,80},{112,96},{1... | collective-permute-start | bytes 2113544 | tf_op jit(solution)/shard_map/ppermute | solution.py:127
  57.8 15.6 %collective-permute-done.8 = bf16[688,512]{1,0:T(8,128)(2,1)S(1)} collective-permute-done((bf16[688,512]{1,0:T(8,128)(2,1)S(1)}, bf16[688,512]{1,0:T(8,128)(2,1)S(1)}, u32[]{:S(2)}, u32[]{:S(2)}) %collective-permute-start.8) | collective-permute-done | bytes 704544 | tf_op jit(solution)/shard_map/ppermute | solution.py:127
  73.4 3.3 %collective-permute-start.11 = (bf16[688,512]{1,0:T(8,128)(2,1)S(1)}, bf16[688,512]{1,0:T(8,128)(2,1)S(1)}, u32[]{:S(2)}, u32[]{:S(2)}) collective-permute-start(bf16[688,512]{1,0:T(8,128)(2,1)S(1)} %collective-permute-done.9), channel_id=1, source_target_pairs={{0,112},{16,0},{32,16},{48,32},{64,48},{80,64},{96,80},{112,96},{1... | collective-permute-start | bytes 2113544 | tf_op jit(solution)/shard_map/ppermute | solution.py:127
  77.2 14.4 %collective-permute-done.10 = bf16[688,512]{1,0:T(8,128)(2,1)S(1)} collective-permute-done((bf16[688,512]{1,0:T(8,128)(2,1)S(1)}, bf16[688,512]{1,0:T(8,128)(2,1)S(1)}, u32[]{:S(2)}, u32[]{:S(2)}) %collective-permute-start.10) | collective-permute-done | bytes 704544 | tf_op jit(solution)/shard_map/ppermute | solution.py:127
  91.6 3.2 %collective-permute-start.13 = (bf16[688,512]{1,0:T(8,128)(2,1)S(1)}, bf16[688,512]{1,0:T(8,128)(2,1)S(1)}, u32[]{:S(2)}, u32[]{:S(2)}) collective-permute-start(bf16[688,512]{1,0:T(8,128)(2,1)S(1)} %collective-permute-done.11), channel_id=1, source_target_pairs={{0,112},{16,0},{32,16},{48,32},{64,48},{80,64},{96,80},{112,96},{1... | collective-permute-start | bytes 2113544 | tf_op jit(solution)/shard_map/ppermute | solution.py:127
  95.0 14.0 %collective-permute-done.12 = bf16[688,512]{1,0:T(8,128)(2,1)S(1)} collective-permute-done((bf16[688,512]{1,0:T(8,128)(2,1)S(1)}, bf16[688,512]{1,0:T(8,128)(2,1)S(1)}, u32[]{:S(2)}, u32[]{:S(2)}) %collective-permute-start.12) | collective-permute-done | bytes 704544 | tf_op jit(solution)/shard_map/ppermute | solution.py:127
  109.1 3.1 %collective-permute-start.15 = (bf16[336,512]{1,0:T(8,128)(2,1)S(1)}, bf16[336,512]{1,0:T(8,128)(2,1)S(1)}, u32[]{:S(2)}, u32[]{:S(2)}) collective-permute-start(bf16[336,512]{1,0:T(8,128)(2,1)S(1)} %slice.29), channel_id=1, source_target_pairs={{0,112},{16,0},{32,16},{48,32},{64,48},{80,64},{96,80},{112,96},{1... | collective-permute-start | bytes 1032200 | tf_op jit(solution)/shard_map/ppermute | solution.py:130
  112.3 5.8 %collective-permute-done.14 = bf16[352,512]{1,0:T(8,128)(2,1)S(1)} collective-permute-done((bf16[352,512]{1,0:T(8,128)(2,1)S(1)}, bf16[352,512]{1,0:T(8,128)(2,1)S(1)}, u32[]{:S(2)}, u32[]{:S(2)}) %collective-permute-start.14) | collective-permute-done | bytes 360480 | tf_op jit(solution)/shard_map/ppermute | solution.py:129
  118.2 2.4 %copy-done.1 = bf16[8,688,512]{2,1,0:T(8,128)(2,1)} copy-done((bf16[8,688,512]{2,1,0:T(8,128)(2,1)}, bf16[8,688,512]{2,1,0:T(8,128)(2,1)S(1)}, u32[]{:S(2)}) %copy-start.1) | copy-done | bytes 5636120
  121.9 2.6 %copy-done.2 = bf16[8,688,512]{2,1,0:T(8,128)(2,1)S(1)} copy-done((bf16[8,688,512]{2,1,0:T(8,128)(2,1)S(1)}, bf16[8,688,512]{2,1,0:T(8,128)(2,1)}, u32[]{:S(2)}) %copy-start.2) | copy-done | bytes 5636120
  124.5 4.5 %shard_map.38 = bf16[336,688]{1,0:T(8,128)(2,1)S(1)} custom-call(bf16[4,2,2,688,512]{4,3,2,1,0:T(8,128)(2,1)} %bitcast.42, bf16[4,2,2,688,512]{4,3,2,1,0:T(8,128)(2,1)} %bitcast.43, bf16[8,688,512]{2,1,0:T(8,128)(2,1)S(1)} %copy-done.2), custom_call_target="tpu_custom_call" | custom-call | flops 1893728256 | bytes 8388608 | tf_op jit(solution)/shard_map/pallas_call | solution.py:83
  129.0 2.9 %collective-permute-start.16 = (bf16[21,16,688]{2,1,0:T(8,128)(2,1)S(1)}, bf16[21,16,688]{2,1,0:T(8,128)(2,1)S(1)}, u32[]{:S(2)}, u32[]{:S(2)}) collective-permute-start(bf16[21,16,688]{2,1,0:T(8,128)(2,1)S(1)} %bitcast.41), channel_id=1, source_target_pairs={{0,128},{16,144},{32,160},{48,176},{64,192},{80,208},{96,224},{112... | collective-permute-start | bytes 1387016 | tf_op jit(solution)/shard_map/ppermute | solution.py:137
  131.9 4.6 %shard_map.40 = bf16[352,688]{1,0:T(8,128)(2,1)S(1)} custom-call(bf16[4,2,2,688,512]{4,3,2,1,0:T(8,128)(2,1)} %bitcast.44, bf16[4,2,2,688,512]{4,3,2,1,0:T(8,128)(2,1)} %bitcast.45, bf16[8,688,512]{2,1,0:T(8,128)(2,1)S(1)} %copy-done.2), custom_call_target="tpu_custom_call" | custom-call | flops 1983905792 | bytes 8388608 | tf_op jit(solution)/shard_map/pallas_call | solution.py:83
  136.9 6.2 %shard_map.37 = f32[336,688]{1,0:T(8,128)S(1)} custom-call(bf16[4,2,2,688,512]{4,3,2,1,0:T(8,128)(2,1)} %bitcast.46, bf16[4,2,2,688,512]{4,3,2,1,0:T(8,128)(2,1)} %bitcast.47, bf16[8,688,512]{2,1,0:T(8,128)(2,1)} %copy-done.1), custom_call_target="tpu_custom_call" | custom-call | flops 1893728256 | bytes 8388608 | tf_op jit(solution)/shard_map/pallas_call | solution.py:83
  143.1 6.4 %shard_map.39 = f32[352,688]{1,0:T(8,128)S(1)} custom-call(bf16[4,2,2,688,512]{4,3,2,1,0:T(8,128)(2,1)} %bitcast.48, bf16[4,2,2,688,512]{4,3,2,1,0:T(8,128)(2,1)} %bitcast.49, bf16[8,688,512]{2,1,0:T(8,128)(2,1)} %copy-done.1), custom_call_target="tpu_custom_call" | custom-call | flops 1983905792 | bytes 8388608 | tf_op jit(solution)/shard_map/pallas_call | solution.py:83
  149.8 4.2 %collective-permute-done.17 = bf16[22,16,688]{2,1,0:T(8,128)(2,1)S(1)} collective-permute-done((bf16[22,16,688]{2,1,0:T(8,128)(2,1)S(1)}, bf16[22,16,688]{2,1,0:T(8,128)(2,1)S(1)}, u32[]{:S(2)}, u32[]{:S(2)}) %collective-permute-start.17) | collective-permute-done | bytes 484384 | tf_op jit(solution)/shard_map/ppermute | solution.py:137
  (45 shorter events, 9.6 us)
Async XLA Ops:
  6.5 1.8 %copy-start = (bf16[688,2048]{1,0:T(8,128)(2,1)S(1)}, bf16[688,2048]{1,0:T(8,128)(2,1)}, u32[]{:S(2)}) copy-start(bf16[688,2048]{1,0:T(8,128)(2,1)} %param.4) | copy-start | bytes 8454148
  6.5 115.4 %all-gather.3.cloned.1.call-start = ((), (), s32[]{:S(2)}) async-start(), calls=%async_computation | async-start | bytes 11976704 | tf_op jit(solution)/shard_map/all_gather | solution.py:122
  11.9 13.9 %collective-permute-start = (bf16[176,512]{1,0:T(8,128)(2,1)S(1)}, bf16[176,512]{1,0:T(8,128)(2,1)S(1)}, u32[]{:S(2)}, u32[]{:S(2)}) collective-permute-start(bf16[176,512]{1,0:T(8,128)(2,1)S(1)} %get-tuple-element.9), channel_id=1, source_target_pairs={{0,0},{1,5},{2,9},{3,13},{4,1},{5,12},{6,8},{7,4},{8,2},{9,7},{10,... | collective-permute-start | bytes 540680 | tf_op jit(solution)/shard_map/ppermute | solution.py:117
  15.9 19.4 %collective-permute-start.2 = (bf16[176,512]{1,0:T(8,128)(2,1)S(1)}, bf16[176,512]{1,0:T(8,128)(2,1)S(1)}, u32[]{:S(2)}, u32[]{:S(2)}) collective-permute-start(bf16[176,512]{1,0:T(8,128)(2,1)S(1)} %get-tuple-element.11), channel_id=1, source_target_pairs={{0,4},{1,9},{2,13},{3,1},{4,5},{5,0},{6,12},{7,8},{8,6},{9,11},{10... | collective-permute-start | bytes 540680 | tf_op jit(solution)/shard_map/ppermute | solution.py:117
  20.6 18.0 %collective-permute-start.4 = (bf16[176,512]{1,0:T(8,128)(2,1)S(1)}, bf16[176,512]{1,0:T(8,128)(2,1)S(1)}, u32[]{:S(2)}, u32[]{:S(2)}) collective-permute-start(bf16[176,512]{1,0:T(8,128)(2,1)S(1)} %get-tuple-element.10), channel_id=1, source_target_pairs={{0,8},{1,13},{2,1},{3,5},{4,9},{5,4},{6,0},{7,12},{8,10},{9,15},{1... | collective-permute-start | bytes 540680 | tf_op jit(solution)/shard_map/ppermute | solution.py:117
  25.1 16.5 %collective-permute-start.6 = (bf16[160,512]{1,0:T(8,128)(2,1)S(1)}, bf16[160,512]{1,0:T(8,128)(2,1)S(1)}, u32[]{:S(2)}, u32[]{:S(2)}) collective-permute-start(bf16[160,512]{1,0:T(8,128)(2,1)S(1)} %slice.27), channel_id=1, source_target_pairs={{0,12},{1,1},{2,5},{3,9},{4,13},{5,8},{6,4},{7,0},{8,14},{9,3},{10... | collective-permute-start | bytes 491528 | tf_op jit(solution)/shard_map/ppermute | solution.py:117
  25.8 28.3 %collective-permute-start.1 = (bf16[176,512]{1,0:T(8,128)(2,1)S(1)}, bf16[176,512]{1,0:T(8,128)(2,1)S(1)}, u32[]{:S(2)}, u32[]{:S(2)}) collective-permute-start(bf16[176,512]{1,0:T(8,128)(2,1)S(1)} %collective-permute-done), channel_id=1, source_target_pairs={{0,0},{2,2},{20,4},{22,6},{40,8},{42,10},{60,12},{62,14},{65,1},{6... | collective-permute-start | bytes 540680 | tf_op jit(solution)/shard_map/ppermute | solution.py:116
  35.3 18.7 %collective-permute-start.3 = (bf16[176,512]{1,0:T(8,128)(2,1)S(1)}, bf16[176,512]{1,0:T(8,128)(2,1)S(1)}, u32[]{:S(2)}, u32[]{:S(2)}) collective-permute-start(bf16[176,512]{1,0:T(8,128)(2,1)S(1)} %collective-permute-done.2), channel_id=1, source_target_pairs={{4,4},{6,6},{24,8},{26,10},{44,12},{46,14},{48,0},{50,2},{69,5},{7... | collective-permute-start | bytes 540680 | tf_op jit(solution)/shard_map/ppermute | solution.py:116
  38.7 15.4 %collective-permute-start.5 = (bf16[176,512]{1,0:T(8,128)(2,1)S(1)}, bf16[176,512]{1,0:T(8,128)(2,1)S(1)}, u32[]{:S(2)}, u32[]{:S(2)}) collective-permute-start(bf16[176,512]{1,0:T(8,128)(2,1)S(1)} %collective-permute-done.4), channel_id=1, source_target_pairs={{8,8},{10,10},{28,12},{30,14},{32,0},{34,2},{52,4},{54,6},{73,9},{... | collective-permute-start | bytes 540680 | tf_op jit(solution)/shard_map/ppermute | solution.py:116
  41.6 12.4 %collective-permute-start.7 = (bf16[160,512]{1,0:T(8,128)(2,1)S(1)}, bf16[160,512]{1,0:T(8,128)(2,1)S(1)}, u32[]{:S(2)}, u32[]{:S(2)}) collective-permute-start(bf16[160,512]{1,0:T(8,128)(2,1)S(1)} %collective-permute-done.6), channel_id=1, source_target_pairs={{12,12},{14,14},{16,0},{18,2},{36,4},{38,6},{56,8},{58,10},{77,13}... | collective-permute-start | bytes 491528 | tf_op jit(solution)/shard_map/ppermute | solution.py:116
  55.0 18.4 %collective-permute-start.8 = (bf16[688,512]{1,0:T(8,128)(2,1)S(1)}, bf16[688,512]{1,0:T(8,128)(2,1)S(1)}, u32[]{:S(2)}, u32[]{:S(2)}) collective-permute-start(bf16[688,512]{1,0:T(8,128)(2,1)S(1)} %fusion.4), channel_id=1, source_target_pairs={{0,16},{16,32},{32,48},{48,64},{64,80},{80,96},{96,112},{112,0},{1... | collective-permute-start | bytes 2113544 | tf_op jit(solution)/shard_map/ppermute | solution.py:127
  55.1 18.3 %collective-permute-start.9 = (bf16[688,512]{1,0:T(8,128)(2,1)S(1)}, bf16[688,512]{1,0:T(8,128)(2,1)S(1)}, u32[]{:S(2)}, u32[]{:S(2)}) collective-permute-start(bf16[688,512]{1,0:T(8,128)(2,1)S(1)} %fusion.4), channel_id=1, source_target_pairs={{0,112},{16,0},{32,16},{48,32},{64,48},{80,64},{96,80},{112,96},{1... | collective-permute-start | bytes 2113544 | tf_op jit(solution)/shard_map/ppermute | solution.py:127
  73.4 18.2 %collective-permute-start.10 = (bf16[688,512]{1,0:T(8,128)(2,1)S(1)}, bf16[688,512]{1,0:T(8,128)(2,1)S(1)}, u32[]{:S(2)}, u32[]{:S(2)}) collective-permute-start(bf16[688,512]{1,0:T(8,128)(2,1)S(1)} %collective-permute-done.8), channel_id=1, source_target_pairs={{0,16},{16,32},{32,48},{48,64},{64,80},{80,96},{96,112},{112,0},{1... | collective-permute-start | bytes 2113544 | tf_op jit(solution)/shard_map/ppermute | solution.py:127
  73.4 18.2 %collective-permute-start.11 = (bf16[688,512]{1,0:T(8,128)(2,1)S(1)}, bf16[688,512]{1,0:T(8,128)(2,1)S(1)}, u32[]{:S(2)}, u32[]{:S(2)}) collective-permute-start(bf16[688,512]{1,0:T(8,128)(2,1)S(1)} %collective-permute-done.9), channel_id=1, source_target_pairs={{0,112},{16,0},{32,16},{48,32},{64,48},{80,64},{96,80},{112,96},{1... | collective-permute-start | bytes 2113544 | tf_op jit(solution)/shard_map/ppermute | solution.py:127
  91.6 17.3 %collective-permute-start.12 = (bf16[688,512]{1,0:T(8,128)(2,1)S(1)}, bf16[688,512]{1,0:T(8,128)(2,1)S(1)}, u32[]{:S(2)}, u32[]{:S(2)}) collective-permute-start(bf16[688,512]{1,0:T(8,128)(2,1)S(1)} %collective-permute-done.10), channel_id=1, source_target_pairs={{0,16},{16,32},{32,48},{48,64},{64,80},{80,96},{96,112},{112,0},{1... | collective-permute-start | bytes 2113544 | tf_op jit(solution)/shard_map/ppermute | solution.py:127
  91.6 17.4 %collective-permute-start.13 = (bf16[688,512]{1,0:T(8,128)(2,1)S(1)}, bf16[688,512]{1,0:T(8,128)(2,1)S(1)}, u32[]{:S(2)}, u32[]{:S(2)}) collective-permute-start(bf16[688,512]{1,0:T(8,128)(2,1)S(1)} %collective-permute-done.11), channel_id=1, source_target_pairs={{0,112},{16,0},{32,16},{48,32},{64,48},{80,64},{96,80},{112,96},{1... | collective-permute-start | bytes 2113544 | tf_op jit(solution)/shard_map/ppermute | solution.py:127
  109.0 9.1 %collective-permute-start.14 = (bf16[352,512]{1,0:T(8,128)(2,1)S(1)}, bf16[352,512]{1,0:T(8,128)(2,1)S(1)}, u32[]{:S(2)}, u32[]{:S(2)}) collective-permute-start(bf16[352,512]{1,0:T(8,128)(2,1)S(1)} %slice.28), channel_id=1, source_target_pairs={{0,16},{16,32},{32,48},{48,64},{64,80},{80,96},{96,112},{112,0},{1... | collective-permute-start | bytes 1081352 | tf_op jit(solution)/shard_map/ppermute | solution.py:129
  109.1 9.0 %collective-permute-start.15 = (bf16[336,512]{1,0:T(8,128)(2,1)S(1)}, bf16[336,512]{1,0:T(8,128)(2,1)S(1)}, u32[]{:S(2)}, u32[]{:S(2)}) collective-permute-start(bf16[336,512]{1,0:T(8,128)(2,1)S(1)} %slice.29), channel_id=1, source_target_pairs={{0,112},{16,0},{32,16},{48,32},{64,48},{80,64},{96,80},{112,96},{1... | collective-permute-start | bytes 1032200 | tf_op jit(solution)/shard_map/ppermute | solution.py:130
  118.2 2.4 %copy-start.1 = (bf16[8,688,512]{2,1,0:T(8,128)(2,1)}, bf16[8,688,512]{2,1,0:T(8,128)(2,1)S(1)}, u32[]{:S(2)}) copy-start(bf16[8,688,512]{2,1,0:T(8,128)(2,1)S(1)} %bitcast_dynamic-update-slice_fusion.7.columns_ref) | copy-start | bytes 16908292
  121.9 2.6 %copy-start.2 = (bf16[8,688,512]{2,1,0:T(8,128)(2,1)S(1)}, bf16[8,688,512]{2,1,0:T(8,128)(2,1)}, u32[]{:S(2)}) copy-start(bf16[8,688,512]{2,1,0:T(8,128)(2,1)} %copy-done.1) | copy-start | bytes 16908292
  129.0 20.5 %collective-permute-start.16 = (bf16[21,16,688]{2,1,0:T(8,128)(2,1)S(1)}, bf16[21,16,688]{2,1,0:T(8,128)(2,1)S(1)}, u32[]{:S(2)}, u32[]{:S(2)}) collective-permute-start(bf16[21,16,688]{2,1,0:T(8,128)(2,1)S(1)} %bitcast.41), channel_id=1, source_target_pairs={{0,128},{16,144},{32,160},{48,176},{64,192},{80,208},{96,224},{112... | collective-permute-start | bytes 1387016 | tf_op jit(solution)/shard_map/ppermute | solution.py:137
  136.5 17.5 %collective-permute-start.17 = (bf16[22,16,688]{2,1,0:T(8,128)(2,1)S(1)}, bf16[22,16,688]{2,1,0:T(8,128)(2,1)S(1)}, u32[]{:S(2)}, u32[]{:S(2)}) collective-permute-start(bf16[22,16,688]{2,1,0:T(8,128)(2,1)S(1)} %bitcast.40), channel_id=1, source_target_pairs={{0,128},{16,144},{32,160},{48,176},{64,192},{80,208},{96,224},{112... | collective-permute-start | bytes 1453064 | tf_op jit(solution)/shard_map/ppermute | solution.py:137
  149.8 4.2 %copy-start.3 = (f32[688,688]{1,0:T(8,128)}, f32[688,688]{1,0:T(8,128)S(1)}, u32[]{:S(2)}) copy-start(f32[688,688]{1,0:T(8,128)S(1)} %fusion.8) | copy-start | bytes 5680132
Sparse Core Ops, SparseCore 0:
  55.1 66.7 all-gather.2

commit v11 on v10

--- a/solution.py
+++ b/solution.py
@@ -54,7 +54,7 @@
         return sum(
             lax.dot_general(
                 jnp.concatenate([low_ref[0, 0, core], high_ref[0, 0, core, :high]]),
-                columns_ref[2 * k + core], (((1,), (1,)), ((), ())),
+                columns_ref[core], (((1,), (1,)), ((), ())),
                 preferred_element_type=jnp.float32,
             )
             for core in range(2)
@@ -84,16 +84,17 @@
         product_body,
         grid=(4,),
         in_specs=[
-            part_spec(2 * second), part_spec(2 * second + 1), pl.BlockSpec(memory_space=pltpu.VMEM)
+            part_spec(2 * second), part_spec(2 * second + 1),
+            pl.BlockSpec((2, n, tokens), lambda k: (k, 0, 0)),
         ],
         out_specs=pl.BlockSpec((count, n), lambda k: (0, 0)),
         out_shape=jax.ShapeDtypeStruct((count, n), kind),
         scratch_shapes=[pltpu.VMEM((count, n), jnp.float32)],
         compiler_params=pltpu.CompilerParams(
-            dimension_semantics=("arbitrary",), vmem_limit_bytes=48 * 1024 * 1024
+            dimension_semantics=("arbitrary",), vmem_limit_bytes=56 * 1024 * 1024
         ),
         cost_estimate=pl.CostEstimate(
-            flops=2 * count * n * tokens * RING, bytes_accessed=8 * 1024 * 1024, transcendentals=0
+            flops=2 * count * n * tokens * RING, bytes_accessed=12 * 1024 * 1024, transcendentals=0
         ),
     )(rows, rows, columns)
 

time: 164 us -> 163 us (level)
  waiting for transfers between devices: 65.8 us -> 57 us
  local copies, waits for them, and re-layouts: 7.84 us -> 13.1 us
  Pallas kernels: 21.6 us -> 25.9 us
    dynamic_update_slice x8, local copies, waits for them, and re-layouts: 0.33 us -> 7.08 us  [put(): lax.dynamic_update_slice(columns, block[None], (PLACES.index(offset), sta...]
    ppermute x3, waiting for transfers between devices: 44 us -> 38.1 us  [shards(): lax.ppermute(up, 'dp', along_z(1))]
    pallas_call x4, Pallas kernels: 21.6 us -> 25.9 us  [product(): pl.pallas_call(product_body, grid=(4,), in_specs=[part_spec(2 * second),...]
    unnamed x8, local copies, waits for them, and re-layouts: 6.79 us -> 2.87 us
    broadcast_in_dim x1, local copies, waits for them, and re-layouts: 0.48 us -> 2.89 us  [shards(): columns = jnp.broadcast_to(up_grad[None], (RING, n, tokens))]
    ppermute x2, waiting for transfers between devices: 4.16 us -> 2.02 us  [shards(): sent = [lax.ppermute(part, 'dp', ACROSS) for part in theirs]]
    ppermute x1, waiting for transfers between devices: 5.79 us -> 4.08 us  [shards(): up = lax.ppermute(up[:cut], 'dp', along_z(1))]
  transfers between devices with their start and end apart: 19 -> 19, of which waited for: 7 -> 7; matrix products, arithmetic and copies ran while one was open for 1% -> 6% of each run, Pallas kernels for 11% -> 12%
where the time goes in v11:
time: 163 us; the launch traced here: 162 us
  waiting for transfers between devices  57 us (35%)
  starting transfers between devices  46.9 us (29%)
  Pallas kernels  25.9 us (16%)
  between operations  13.6 us (8%)
  local copies, waits for them, and re-layouts  13.1 us (8%)
  matrix products  3.55 us (2%)
  other arithmetic  2.09 us (1%)
    ppermute x3, waiting for transfers between devices, shards(): lax.ppermute(up, 'dp', along_z(1))  38.1 us
    pallas_call x4, Pallas kernels, product(): pl.pallas_call(product_body, grid=(4,), in_specs=[part_spec(2 * second),...  25.9 us
    ppermute x4, starting transfers between devices, shards(): lax.ppermute(lax.ppermute(up_grad[part * size:(part + 1) * size], BOTH, i...  17.7 us
    ppermute x4, starting transfers between devices, shards(): lax.ppermute(up_grad[part * size:(part + 1) * size], BOTH, in_plane(part))  13.8 us
    ppermute x4, waiting for transfers between devices, shards(): lax.ppermute(lax.ppermute(up_grad[part * size:(part + 1) * size], BOTH, i...  10.5 us
    ppermute x3, starting transfers between devices, shards(): lax.ppermute(down, 'dp', along_z(-1))  9.12 us
    dynamic_update_slice x8, local copies, waits for them, and re-layouts, put(): lax.dynamic_update_slice(columns, block[None], (PLACES.index(offset), sta...  7.08 us
    ppermute x1, waiting for transfers between devices, shards(): up = lax.ppermute(up[:cut], 'dp', along_z(1))  4.08 us
  transfers between devices with their start and end apart: 19, of which 7 were waited for; matrix products, arithmetic and copies ran while one was open for 6% of the time, Pallas kernels for 12%

profile of v11, /device:TPU:1, one launch (start us, length us, event | category | flops | bytes accessed | tf_op | source)
XLA Modules:
  0.0 162.1 jit_solution(2887022016853736466)
XLA Ops:
  8.3 3.6 %fusion.4 = bf16[688,512]{1,0:T(8,128)(2,1)S(1)} fusion(bf16[512,688]{0,1:T(8,128)(2,1)} %param.5, bf16[688,2048]{1,0:T(8,128)(2,1)S(1)} %copy-done, bf16[512,2048]{1,0:T(8,128)(2,1)} %param.3), kind=kOutput, calls=%fused_computation.6 | convolution fusion | flops 1446010880 | bytes 6324224 | tf_op jit(solution)/shard_map/dot_general | solution.py:110
  11.9 4.0 %collective-permute-start = (bf16[176,512]{1,0:T(8,128)(2,1)S(1)}, bf16[176,512]{1,0:T(8,128)(2,1)S(1)}, u32[]{:S(2)}, u32[]{:S(2)}) collective-permute-start(bf16[176,512]{1,0:T(8,128)(2,1)S(1)} %get-tuple-element.9), channel_id=1, source_target_pairs={{0,0},{1,5},{2,9},{3,13},{4,1},{5,12},{6,8},{7,4},{8,2},{9,7},{10,... | collective-permute-start | bytes 540680 | tf_op jit(solution)/shard_map/ppermute | solution.py:118
  15.9 4.7 %collective-permute-start.2 = (bf16[176,512]{1,0:T(8,128)(2,1)S(1)}, bf16[176,512]{1,0:T(8,128)(2,1)S(1)}, u32[]{:S(2)}, u32[]{:S(2)}) collective-permute-start(bf16[176,512]{1,0:T(8,128)(2,1)S(1)} %get-tuple-element.11), channel_id=1, source_target_pairs={{0,4},{1,9},{2,13},{3,1},{4,5},{5,0},{6,12},{7,8},{8,6},{9,11},{10... | collective-permute-start | bytes 540680 | tf_op jit(solution)/shard_map/ppermute | solution.py:118
  20.6 4.5 %collective-permute-start.4 = (bf16[176,512]{1,0:T(8,128)(2,1)S(1)}, bf16[176,512]{1,0:T(8,128)(2,1)S(1)}, u32[]{:S(2)}, u32[]{:S(2)}) collective-permute-start(bf16[176,512]{1,0:T(8,128)(2,1)S(1)} %get-tuple-element.10), channel_id=1, source_target_pairs={{0,8},{1,13},{2,1},{3,5},{4,9},{5,4},{6,0},{7,12},{8,10},{9,15},{1... | collective-permute-start | bytes 540680 | tf_op jit(solution)/shard_map/ppermute | solution.py:118
  25.8 9.5 %collective-permute-start.1 = (bf16[176,512]{1,0:T(8,128)(2,1)S(1)}, bf16[176,512]{1,0:T(8,128)(2,1)S(1)}, u32[]{:S(2)}, u32[]{:S(2)}) collective-permute-start(bf16[176,512]{1,0:T(8,128)(2,1)S(1)} %collective-permute-done), channel_id=1, source_target_pairs={{0,0},{2,2},{20,4},{22,6},{40,8},{42,10},{60,12},{62,14},{65,1},{6... | collective-permute-start | bytes 540680 | tf_op jit(solution)/shard_map/ppermute | solution.py:117
  35.3 3.3 %collective-permute-start.3 = (bf16[176,512]{1,0:T(8,128)(2,1)S(1)}, bf16[176,512]{1,0:T(8,128)(2,1)S(1)}, u32[]{:S(2)}, u32[]{:S(2)}) collective-permute-start(bf16[176,512]{1,0:T(8,128)(2,1)S(1)} %collective-permute-done.2), channel_id=1, source_target_pairs={{4,4},{6,6},{24,8},{26,10},{44,12},{46,14},{48,0},{50,2},{69,5},{7... | collective-permute-start | bytes 540680 | tf_op jit(solution)/shard_map/ppermute | solution.py:117
  38.7 3.0 %collective-permute-start.5 = (bf16[176,512]{1,0:T(8,128)(2,1)S(1)}, bf16[176,512]{1,0:T(8,128)(2,1)S(1)}, u32[]{:S(2)}, u32[]{:S(2)}) collective-permute-start(bf16[176,512]{1,0:T(8,128)(2,1)S(1)} %collective-permute-done.4), channel_id=1, source_target_pairs={{8,8},{10,10},{28,12},{30,14},{32,0},{34,2},{52,4},{54,6},{73,9},{... | collective-permute-start | bytes 540680 | tf_op jit(solution)/shard_map/ppermute | solution.py:117
  43.6 10.5 %collective-permute-done.7 = bf16[160,512]{1,0:T(8,128)(2,1)S(1)} collective-permute-done((bf16[160,512]{1,0:T(8,128)(2,1)S(1)}, bf16[160,512]{1,0:T(8,128)(2,1)S(1)}, u32[]{:S(2)}, u32[]{:S(2)}) %collective-permute-start.7) | collective-permute-done | bytes 163872 | tf_op jit(solution)/shard_map/ppermute | solution.py:117
  55.1 2.7 %collective-permute-start.9 = (bf16[688,512]{1,0:T(8,128)(2,1)S(1)}, bf16[688,512]{1,0:T(8,128)(2,1)S(1)}, u32[]{:S(2)}, u32[]{:S(2)}) collective-permute-start(bf16[688,512]{1,0:T(8,128)(2,1)S(1)} %fusion.4), channel_id=1, source_target_pairs={{0,112},{16,0},{32,16},{48,32},{64,48},{80,64},{96,80},{112,96},{1... | collective-permute-start | bytes 2113544 | tf_op jit(solution)/shard_map/ppermute | solution.py:128
  57.8 15.6 %collective-permute-done.8 = bf16[688,512]{1,0:T(8,128)(2,1)S(1)} collective-permute-done((bf16[688,512]{1,0:T(8,128)(2,1)S(1)}, bf16[688,512]{1,0:T(8,128)(2,1)S(1)}, u32[]{:S(2)}, u32[]{:S(2)}) %collective-permute-start.8) | collective-permute-done | bytes 704544 | tf_op jit(solution)/shard_map/ppermute | solution.py:128
  73.4 3.3 %collective-permute-start.11 = (bf16[688,512]{1,0:T(8,128)(2,1)S(1)}, bf16[688,512]{1,0:T(8,128)(2,1)S(1)}, u32[]{:S(2)}, u32[]{:S(2)}) collective-permute-start(bf16[688,512]{1,0:T(8,128)(2,1)S(1)} %collective-permute-done.9), channel_id=1, source_target_pairs={{0,112},{16,0},{32,16},{48,32},{64,48},{80,64},{96,80},{112,96},{1... | collective-permute-start | bytes 2113544 | tf_op jit(solution)/shard_map/ppermute | solution.py:128
  76.6 2.9 %broadcast_in_dim.34 = bf16[8,688,512]{2,1,0:T(8,128)(2,1)} broadcast(bf16[688,512]{1,0:T(8,128)(2,1)S(1)} %fusion.4), dimensions={1,2} | broadcast | bytes 6340608 | tf_op jit(solution)/shard_map/broadcast_in_dim | solution.py:125
  80.4 11.2 %collective-permute-done.10 = bf16[688,512]{1,0:T(8,128)(2,1)S(1)} collective-permute-done((bf16[688,512]{1,0:T(8,128)(2,1)S(1)}, bf16[688,512]{1,0:T(8,128)(2,1)S(1)}, u32[]{:S(2)}, u32[]{:S(2)}) %collective-permute-start.10) | collective-permute-done | bytes 704544 | tf_op jit(solution)/shard_map/ppermute | solution.py:128
  91.6 3.2 %collective-permute-start.13 = (bf16[688,512]{1,0:T(8,128)(2,1)S(1)}, bf16[688,512]{1,0:T(8,128)(2,1)S(1)}, u32[]{:S(2)}, u32[]{:S(2)}) collective-permute-start(bf16[688,512]{1,0:T(8,128)(2,1)S(1)} %collective-permute-done.11), channel_id=1, source_target_pairs={{0,112},{16,0},{32,16},{48,32},{64,48},{80,64},{96,80},{112,96},{1... | collective-permute-start | bytes 2113544 | tf_op jit(solution)/shard_map/ppermute | solution.py:128
  97.6 11.3 %collective-permute-done.12 = bf16[688,512]{1,0:T(8,128)(2,1)S(1)} collective-permute-done((bf16[688,512]{1,0:T(8,128)(2,1)S(1)}, bf16[688,512]{1,0:T(8,128)(2,1)S(1)}, u32[]{:S(2)}, u32[]{:S(2)}) %collective-permute-start.12) | collective-permute-done | bytes 704544 | tf_op jit(solution)/shard_map/ppermute | solution.py:128
  109.1 3.1 %collective-permute-start.15 = (bf16[336,512]{1,0:T(8,128)(2,1)S(1)}, bf16[336,512]{1,0:T(8,128)(2,1)S(1)}, u32[]{:S(2)}, u32[]{:S(2)}) collective-permute-start(bf16[336,512]{1,0:T(8,128)(2,1)S(1)} %slice.29), channel_id=1, source_target_pairs={{0,112},{16,0},{32,16},{48,32},{64,48},{80,64},{96,80},{112,96},{1... | collective-permute-start | bytes 1032200 | tf_op jit(solution)/shard_map/ppermute | solution.py:131
  114.0 4.1 %collective-permute-done.14 = bf16[352,512]{1,0:T(8,128)(2,1)S(1)} collective-permute-done((bf16[352,512]{1,0:T(8,128)(2,1)S(1)}, bf16[352,512]{1,0:T(8,128)(2,1)S(1)}, u32[]{:S(2)}, u32[]{:S(2)}) %collective-permute-start.14) | collective-permute-done | bytes 360480 | tf_op jit(solution)/shard_map/ppermute | solution.py:130
  119.6 2.3 %all-gather.3.cloned.1.call-done = bf16[11008,512]{1,0:T(8,128)(2,1)} async-done(((bf16[688,512]{1,0:T(8,128)(2,1)}), bf16[11008,512]{1,0:T(8,128)(2,1)}) %all-gather.3.cloned.1.call-update) | async-done | bytes 11272208 | tf_op jit(solution)/shard_map/all_gather | solution.py:123
  121.9 6.3 %shard_map.38 = bf16[336,688]{1,0:T(8,128)(2,1)} custom-call(bf16[4,2,2,688,512]{4,3,2,1,0:T(8,128)(2,1)} %bitcast.40, bf16[4,2,2,688,512]{4,3,2,1,0:T(8,128)(2,1)} %bitcast.41, bf16[8,688,512]{2,1,0:T(8,128)(2,1)} %bitcast_dynamic-update-slice_fusion.7.columns_ref), custom_call_target="tpu_custom_call" | custom-call | flops 1893728256 | bytes 12582912 | tf_op jit(solution)/shard_map/pallas_call | solution.py:83
  128.3 2.6 %collective-permute-start.16 = (bf16[21,16,688]{2,1,0:T(8,128)(2,1)}, bf16[21,16,688]{2,1,0:T(8,128)(2,1)S(1)}, u32[]{:S(2)}, u32[]{:S(2)}) collective-permute-start(bf16[21,16,688]{2,1,0:T(8,128)(2,1)} %bitcast.51), channel_id=1, source_target_pairs={{0,128},{16,144},{32,160},{48,176},{64,192},{80,208},{96,224},{112... | collective-permute-start | bytes 1387016 | tf_op jit(solution)/shard_map/ppermute | solution.py:138
  130.9 6.4 %shard_map.40 = bf16[352,688]{1,0:T(8,128)(2,1)} custom-call(bf16[4,2,2,688,512]{4,3,2,1,0:T(8,128)(2,1)} %bitcast.42, bf16[4,2,2,688,512]{4,3,2,1,0:T(8,128)(2,1)} %bitcast.43, bf16[8,688,512]{2,1,0:T(8,128)(2,1)} %bitcast_dynamic-update-slice_fusion.7.columns_ref), custom_call_target="tpu_custom_call" | custom-call | flops 1983905792 | bytes 12582912 | tf_op jit(solution)/shard_map/pallas_call | solution.py:83
  137.7 6.5 %shard_map.37 = f32[336,688]{1,0:T(8,128)} custom-call(bf16[4,2,2,688,512]{4,3,2,1,0:T(8,128)(2,1)} %bitcast.44, bf16[4,2,2,688,512]{4,3,2,1,0:T(8,128)(2,1)} %bitcast.45, bf16[8,688,512]{2,1,0:T(8,128)(2,1)} %bitcast_dynamic-update-slice_fusion.7.columns_ref), custom_call_target="tpu_custom_call" | custom-call | flops 1893728256 | bytes 12582912 | tf_op jit(solution)/shard_map/pallas_call | solution.py:83
  144.2 6.6 %shard_map.39 = f32[352,688]{1,0:T(8,128)} custom-call(bf16[4,2,2,688,512]{4,3,2,1,0:T(8,128)(2,1)} %bitcast.46, bf16[4,2,2,688,512]{4,3,2,1,0:T(8,128)(2,1)} %bitcast.47, bf16[8,688,512]{2,1,0:T(8,128)(2,1)} %bitcast_dynamic-update-slice_fusion.7.columns_ref), custom_call_target="tpu_custom_call" | custom-call | flops 1983905792 | bytes 12582912 | tf_op jit(solution)/shard_map/pallas_call | solution.py:83
  152.1 2.0 %collective-permute-done.17 = bf16[22,16,688]{2,1,0:T(8,128)(2,1)S(1)} collective-permute-done((bf16[22,16,688]{2,1,0:T(8,128)(2,1)}, bf16[22,16,688]{2,1,0:T(8,128)(2,1)S(1)}, u32[]{:S(2)}, u32[]{:S(2)}) %collective-permute-start.17) | collective-permute-done | bytes 484384 | tf_op jit(solution)/shard_map/ppermute | solution.py:138
  (45 shorter events, 15.5 us)
Async XLA Ops:
  6.5 1.8 %copy-start = (bf16[688,2048]{1,0:T(8,128)(2,1)S(1)}, bf16[688,2048]{1,0:T(8,128)(2,1)}, u32[]{:S(2)}) copy-start(bf16[688,2048]{1,0:T(8,128)(2,1)} %param.4) | copy-start | bytes 8454148
  6.5 115.4 %all-gather.3.cloned.1.call-start = ((), (), s32[]{:S(2)}) async-start(), calls=%async_computation | async-start | bytes 11976704 | tf_op jit(solution)/shard_map/all_gather | solution.py:123
  11.9 13.9 %collective-permute-start = (bf16[176,512]{1,0:T(8,128)(2,1)S(1)}, bf16[176,512]{1,0:T(8,128)(2,1)S(1)}, u32[]{:S(2)}, u32[]{:S(2)}) collective-permute-start(bf16[176,512]{1,0:T(8,128)(2,1)S(1)} %get-tuple-element.9), channel_id=1, source_target_pairs={{0,0},{1,5},{2,9},{3,13},{4,1},{5,12},{6,8},{7,4},{8,2},{9,7},{10,... | collective-permute-start | bytes 540680 | tf_op jit(solution)/shard_map/ppermute | solution.py:118
  15.9 19.4 %collective-permute-start.2 = (bf16[176,512]{1,0:T(8,128)(2,1)S(1)}, bf16[176,512]{1,0:T(8,128)(2,1)S(1)}, u32[]{:S(2)}, u32[]{:S(2)}) collective-permute-start(bf16[176,512]{1,0:T(8,128)(2,1)S(1)} %get-tuple-element.11), channel_id=1, source_target_pairs={{0,4},{1,9},{2,13},{3,1},{4,5},{5,0},{6,12},{7,8},{8,6},{9,11},{10... | collective-permute-start | bytes 540680 | tf_op jit(solution)/shard_map/ppermute | solution.py:118
  20.6 18.0 %collective-permute-start.4 = (bf16[176,512]{1,0:T(8,128)(2,1)S(1)}, bf16[176,512]{1,0:T(8,128)(2,1)S(1)}, u32[]{:S(2)}, u32[]{:S(2)}) collective-permute-start(bf16[176,512]{1,0:T(8,128)(2,1)S(1)} %get-tuple-element.10), channel_id=1, source_target_pairs={{0,8},{1,13},{2,1},{3,5},{4,9},{5,4},{6,0},{7,12},{8,10},{9,15},{1... | collective-permute-start | bytes 540680 | tf_op jit(solution)/shard_map/ppermute | solution.py:118
  25.1 16.5 %collective-permute-start.6 = (bf16[160,512]{1,0:T(8,128)(2,1)S(1)}, bf16[160,512]{1,0:T(8,128)(2,1)S(1)}, u32[]{:S(2)}, u32[]{:S(2)}) collective-permute-start(bf16[160,512]{1,0:T(8,128)(2,1)S(1)} %slice.27), channel_id=1, source_target_pairs={{0,12},{1,1},{2,5},{3,9},{4,13},{5,8},{6,4},{7,0},{8,14},{9,3},{10... | collective-permute-start | bytes 491528 | tf_op jit(solution)/shard_map/ppermute | solution.py:118
  25.8 28.3 %collective-permute-start.1 = (bf16[176,512]{1,0:T(8,128)(2,1)S(1)}, bf16[176,512]{1,0:T(8,128)(2,1)S(1)}, u32[]{:S(2)}, u32[]{:S(2)}) collective-permute-start(bf16[176,512]{1,0:T(8,128)(2,1)S(1)} %collective-permute-done), channel_id=1, source_target_pairs={{0,0},{2,2},{20,4},{22,6},{40,8},{42,10},{60,12},{62,14},{65,1},{6... | collective-permute-start | bytes 540680 | tf_op jit(solution)/shard_map/ppermute | solution.py:117
  35.3 18.7 %collective-permute-start.3 = (bf16[176,512]{1,0:T(8,128)(2,1)S(1)}, bf16[176,512]{1,0:T(8,128)(2,1)S(1)}, u32[]{:S(2)}, u32[]{:S(2)}) collective-permute-start(bf16[176,512]{1,0:T(8,128)(2,1)S(1)} %collective-permute-done.2), channel_id=1, source_target_pairs={{4,4},{6,6},{24,8},{26,10},{44,12},{46,14},{48,0},{50,2},{69,5},{7... | collective-permute-start | bytes 540680 | tf_op jit(solution)/shard_map/ppermute | solution.py:117
  38.7 15.4 %collective-permute-start.5 = (bf16[176,512]{1,0:T(8,128)(2,1)S(1)}, bf16[176,512]{1,0:T(8,128)(2,1)S(1)}, u32[]{:S(2)}, u32[]{:S(2)}) collective-permute-start(bf16[176,512]{1,0:T(8,128)(2,1)S(1)} %collective-permute-done.4), channel_id=1, source_target_pairs={{8,8},{10,10},{28,12},{30,14},{32,0},{34,2},{52,4},{54,6},{73,9},{... | collective-permute-start | bytes 540680 | tf_op jit(solution)/shard_map/ppermute | solution.py:117
  41.6 12.4 %collective-permute-start.7 = (bf16[160,512]{1,0:T(8,128)(2,1)S(1)}, bf16[160,512]{1,0:T(8,128)(2,1)S(1)}, u32[]{:S(2)}, u32[]{:S(2)}) collective-permute-start(bf16[160,512]{1,0:T(8,128)(2,1)S(1)} %collective-permute-done.6), channel_id=1, source_target_pairs={{12,12},{14,14},{16,0},{18,2},{36,4},{38,6},{56,8},{58,10},{77,13}... | collective-permute-start | bytes 491528 | tf_op jit(solution)/shard_map/ppermute | solution.py:117
  55.0 18.4 %collective-permute-start.8 = (bf16[688,512]{1,0:T(8,128)(2,1)S(1)}, bf16[688,512]{1,0:T(8,128)(2,1)S(1)}, u32[]{:S(2)}, u32[]{:S(2)}) collective-permute-start(bf16[688,512]{1,0:T(8,128)(2,1)S(1)} %fusion.4), channel_id=1, source_target_pairs={{0,16},{16,32},{32,48},{48,64},{64,80},{80,96},{96,112},{112,0},{1... | collective-permute-start | bytes 2113544 | tf_op jit(solution)/shard_map/ppermute | solution.py:128
  55.1 18.3 %collective-permute-start.9 = (bf16[688,512]{1,0:T(8,128)(2,1)S(1)}, bf16[688,512]{1,0:T(8,128)(2,1)S(1)}, u32[]{:S(2)}, u32[]{:S(2)}) collective-permute-start(bf16[688,512]{1,0:T(8,128)(2,1)S(1)} %fusion.4), channel_id=1, source_target_pairs={{0,112},{16,0},{32,16},{48,32},{64,48},{80,64},{96,80},{112,96},{1... | collective-permute-start | bytes 2113544 | tf_op jit(solution)/shard_map/ppermute | solution.py:128
  73.4 18.2 %collective-permute-start.10 = (bf16[688,512]{1,0:T(8,128)(2,1)S(1)}, bf16[688,512]{1,0:T(8,128)(2,1)S(1)}, u32[]{:S(2)}, u32[]{:S(2)}) collective-permute-start(bf16[688,512]{1,0:T(8,128)(2,1)S(1)} %collective-permute-done.8), channel_id=1, source_target_pairs={{0,16},{16,32},{32,48},{48,64},{64,80},{80,96},{96,112},{112,0},{1... | collective-permute-start | bytes 2113544 | tf_op jit(solution)/shard_map/ppermute | solution.py:128
  73.4 18.2 %collective-permute-start.11 = (bf16[688,512]{1,0:T(8,128)(2,1)S(1)}, bf16[688,512]{1,0:T(8,128)(2,1)S(1)}, u32[]{:S(2)}, u32[]{:S(2)}) collective-permute-start(bf16[688,512]{1,0:T(8,128)(2,1)S(1)} %collective-permute-done.9), channel_id=1, source_target_pairs={{0,112},{16,0},{32,16},{48,32},{64,48},{80,64},{96,80},{112,96},{1... | collective-permute-start | bytes 2113544 | tf_op jit(solution)/shard_map/ppermute | solution.py:128
  91.6 17.3 %collective-permute-start.12 = (bf16[688,512]{1,0:T(8,128)(2,1)S(1)}, bf16[688,512]{1,0:T(8,128)(2,1)S(1)}, u32[]{:S(2)}, u32[]{:S(2)}) collective-permute-start(bf16[688,512]{1,0:T(8,128)(2,1)S(1)} %collective-permute-done.10), channel_id=1, source_target_pairs={{0,16},{16,32},{32,48},{48,64},{64,80},{80,96},{96,112},{112,0},{1... | collective-permute-start | bytes 2113544 | tf_op jit(solution)/shard_map/ppermute | solution.py:128
  91.6 17.4 %collective-permute-start.13 = (bf16[688,512]{1,0:T(8,128)(2,1)S(1)}, bf16[688,512]{1,0:T(8,128)(2,1)S(1)}, u32[]{:S(2)}, u32[]{:S(2)}) collective-permute-start(bf16[688,512]{1,0:T(8,128)(2,1)S(1)} %collective-permute-done.11), channel_id=1, source_target_pairs={{0,112},{16,0},{32,16},{48,32},{64,48},{80,64},{96,80},{112,96},{1... | collective-permute-start | bytes 2113544 | tf_op jit(solution)/shard_map/ppermute | solution.py:128
  109.0 9.1 %collective-permute-start.14 = (bf16[352,512]{1,0:T(8,128)(2,1)S(1)}, bf16[352,512]{1,0:T(8,128)(2,1)S(1)}, u32[]{:S(2)}, u32[]{:S(2)}) collective-permute-start(bf16[352,512]{1,0:T(8,128)(2,1)S(1)} %slice.28), channel_id=1, source_target_pairs={{0,16},{16,32},{32,48},{48,64},{64,80},{80,96},{96,112},{112,0},{1... | collective-permute-start | bytes 1081352 | tf_op jit(solution)/shard_map/ppermute | solution.py:130
  109.1 9.8 %collective-permute-start.15 = (bf16[336,512]{1,0:T(8,128)(2,1)S(1)}, bf16[336,512]{1,0:T(8,128)(2,1)S(1)}, u32[]{:S(2)}, u32[]{:S(2)}) collective-permute-start(bf16[336,512]{1,0:T(8,128)(2,1)S(1)} %slice.29), channel_id=1, source_target_pairs={{0,112},{16,0},{32,16},{48,32},{64,48},{80,64},{96,80},{112,96},{1... | collective-permute-start | bytes 1032200 | tf_op jit(solution)/shard_map/ppermute | solution.py:131
  128.3 22.5 %collective-permute-start.16 = (bf16[21,16,688]{2,1,0:T(8,128)(2,1)}, bf16[21,16,688]{2,1,0:T(8,128)(2,1)S(1)}, u32[]{:S(2)}, u32[]{:S(2)}) collective-permute-start(bf16[21,16,688]{2,1,0:T(8,128)(2,1)} %bitcast.51), channel_id=1, source_target_pairs={{0,128},{16,144},{32,160},{48,176},{64,192},{80,208},{96,224},{112... | collective-permute-start | bytes 1387016 | tf_op jit(solution)/shard_map/ppermute | solution.py:138
  137.3 16.9 %collective-permute-start.17 = (bf16[22,16,688]{2,1,0:T(8,128)(2,1)}, bf16[22,16,688]{2,1,0:T(8,128)(2,1)S(1)}, u32[]{:S(2)}, u32[]{:S(2)}) collective-permute-start(bf16[22,16,688]{2,1,0:T(8,128)(2,1)} %bitcast.49), channel_id=1, source_target_pairs={{0,128},{16,144},{32,160},{48,176},{64,192},{80,208},{96,224},{112... | collective-permute-start | bytes 1453064 | tf_op jit(solution)/shard_map/ppermute | solution.py:138
  150.8 1.2 copy-start.2
  150.8 3.4 %copy-start.1 = (f32[352,688]{1,0:T(8,128)S(1)}, f32[352,688]{1,0:T(8,128)}, u32[]{:S(2)}) copy-start(f32[352,688]{1,0:T(8,128)} %shard_map.39) | copy-start | bytes 2906116
  152.1 2.0 %copy-start.3 = (f32[688,688]{1,0:T(8,128)}, f32[688,688]{1,0:T(8,128)S(1)}, u32[]{:S(2)}) copy-start(f32[688,688]{1,0:T(8,128)S(1)} %fusion.8) | copy-start | bytes 5680132
Sparse Core Ops, SparseCore 0:
  55.1 66.7 all-gather.2

commit v12 on v11

--- a/solution.py
+++ b/solution.py
@@ -107,6 +107,18 @@
     n, tokens = down_weight.shape[0], out_grad.shape[0]
     size = -(-n // (16 * PARTS)) * 16
     cut = 2 * size
+    size = -(-n // (16 * PARTS)) * 16
+    cut = 2 * size
+
+    def some_units(low, high):
+        hidden_grad = lax.dot_general(
+            down_weight[low:high], out_grad, (((1,), (1,)), ((), ())), preferred_element_type=jnp.float32
+        ).astype(jnp.bfloat16)
+        gate = gate_pre[:, low:high].T.astype(jnp.float32)
+        return (hidden_grad.astype(jnp.float32) * jax.nn.silu(gate)).astype(jnp.bfloat16)
+
+    pieces = [some_units(0, cut), some_units(cut, n)]
+    up_grad = jnp.concatenate(pieces)
     hidden_grad = lax.dot_general(
         down_weight, out_grad, (((1,), (1,)), ((), ())), preferred_element_type=jnp.float32
     ).astype(jnp.bfloat16)
@@ -115,7 +127,7 @@
     )
     parts = [
         lax.ppermute(
-            lax.ppermute(up_grad[part * size : (part + 1) * size], BOTH, in_plane(part)), BOTH, shifted(part)
+            lax.ppermute(pieces[part // 2][part % 2 * size : (part % 2 + 1) * size], BOTH, in_plane(part)), BOTH, shifted(part)
         )
         for part in range(PARTS)
     ]

time: 163 us -> 168 us (1.031)
  starting transfers between devices: 46.9 us -> 48.9 us
  waiting for transfers between devices: 57 us -> 59 us
  matrix products: 3.55 us -> 5.35 us
    ppermute x8, starting transfers between devices: 31.5 us -> 35.1 us  [the longest x4 21.3 us: shards(): lax.ppermute(lax.ppermute(pieces[part // 2][part % 2 * size:(part % 2 + 1...]
    dot_general x0 -> x2, matrix products: none -> 3.52 us  [some_units(): lax.dot_general(down_weight[low:high], out_grad, (((1,), (1,)), ((), ()))...]
    ppermute x3, starting transfers between devices: 9.12 us -> 6.36 us  [shards(): lax.ppermute(down, 'dp', along_z(-1))]
    dot_general x1, matrix products: 3.55 us -> 1.82 us  [shards(): lax.dot_general(down_weight, out_grad, (((1,), (1,)), ((), ())), preferre...]
  transfers between devices with their start and end apart: 19 -> 19, of which waited for: 7 -> 9; matrix products, arithmetic and copies ran while one was open for 6% -> 8% of each run, Pallas kernels for 12% -> 12%
where the time goes in v12:
time: 168 us
  waiting for transfers between devices  59 us (35%)
  starting transfers between devices  48.9 us (29%)
  Pallas kernels  25.9 us (15%)
  between operations  13.6 us (8%)
  local copies, waits for them, and re-layouts  12.9 us (8%)
  matrix products  5.35 us (3%)
  other arithmetic  2.09 us (1%)
    ppermute x3, waiting for transfers between devices, shards(): lax.ppermute(up, 'dp', along_z(1))  39.8 us
    pallas_call x4, Pallas kernels, product(): pl.pallas_call(product_body, grid=(4,), in_specs=[part_spec(2 * second),...  25.9 us
    ppermute x4, starting transfers between devices, shards(): lax.ppermute(lax.ppermute(pieces[part // 2][part % 2 * size:(part % 2 + 1...  21.3 us
    ppermute x4, starting transfers between devices, shards(): lax.ppermute(pieces[part // 2][part % 2 * size:(part % 2 + 1) * size], BO...  13.8 us
    ppermute x4, waiting for transfers between devices, shards(): lax.ppermute(lax.ppermute(pieces[part // 2][part % 2 * size:(part % 2 + 1...  8.84 us
    dynamic_update_slice x8, local copies, waits for them, and re-layouts, put(): lax.dynamic_update_slice(columns, block[None], (PLACES.index(offset), sta...  7.08 us
    ppermute x3, starting transfers between devices, shards(): lax.ppermute(down, 'dp', along_z(-1))  6.36 us
    ppermute x1, waiting for transfers between devices, shards(): up = lax.ppermute(up[:cut], 'dp', along_z(1))  4.19 us
  transfers between devices with their start and end apart: 19, of which 9 were waited for; matrix products, arithmetic and copies ran while one was open for 8% of the time, Pallas kernels for 12%

profile of v12, /device:TPU:1, one launch (start us, length us, event | category | flops | bytes accessed | tf_op | source)
XLA Modules:
  0.0 167.8 jit_solution(17034621305818247851)
XLA Ops:
  8.1 2.6 %fusion.18 = bf16[352,512]{1,0:T(8,128)(2,1)S(1)} fusion(bf16[512,2048]{1,0:T(8,128)(2,1)S(1)} %copy-done, bf16[688,2048]{1,0:T(8,128)(2,1)} %param.4, bf16[512,688]{0,1:T(8,128)(2,1)} %param.5), kind=kOutput, calls=%fused_computation.15 | convolution fusion | flops 739819520 | bytes 4259840 | tf_op jit(solution)/shard_map/dot_general | solution.py:114
  10.7 3.9 %collective-permute-start = (bf16[176,512]{1,0:T(8,128)(2,1)S(1)}, bf16[176,512]{1,0:T(8,128)(2,1)S(1)}, u32[]{:S(2)}, u32[]{:S(2)}) collective-permute-start(bf16[176,512]{1,0:T(8,128)(2,1)S(1)} %get-tuple-element.9), channel_id=1, source_target_pairs={{0,0},{1,5},{2,9},{3,13},{4,1},{5,12},{6,8},{7,4},{8,2},{9,7},{10,... | collective-permute-start | bytes 540680 | tf_op jit(solution)/shard_map/ppermute | solution.py:130
  14.7 4.7 %collective-permute-start.2 = (bf16[176,512]{1,0:T(8,128)(2,1)S(1)}, bf16[176,512]{1,0:T(8,128)(2,1)S(1)}, u32[]{:S(2)}, u32[]{:S(2)}) collective-permute-start(bf16[176,512]{1,0:T(8,128)(2,1)S(1)} %get-tuple-element.10), channel_id=1, source_target_pairs={{0,4},{1,9},{2,13},{3,1},{4,5},{5,0},{6,12},{7,8},{8,6},{9,11},{10... | collective-permute-start | bytes 540680 | tf_op jit(solution)/shard_map/ppermute | solution.py:130
  20.4 4.5 %collective-permute-start.4 = (bf16[176,512]{1,0:T(8,128)(2,1)S(1)}, bf16[176,512]{1,0:T(8,128)(2,1)S(1)}, u32[]{:S(2)}, u32[]{:S(2)}) collective-permute-start(bf16[176,512]{1,0:T(8,128)(2,1)S(1)} %slice.42), channel_id=1, source_target_pairs={{0,8},{1,13},{2,1},{3,5},{4,9},{5,4},{6,0},{7,12},{8,10},{9,15},{1... | collective-permute-start | bytes 540680 | tf_op jit(solution)/shard_map/ppermute | solution.py:130
  25.6 9.3 %collective-permute-start.7 = (bf16[160,512]{1,0:T(8,128)(2,1)S(1)}, bf16[160,512]{1,0:T(8,128)(2,1)S(1)}, u32[]{:S(2)}, u32[]{:S(2)}) collective-permute-start(bf16[160,512]{1,0:T(8,128)(2,1)S(1)} %collective-permute-done.6), channel_id=1, source_target_pairs={{12,12},{14,14},{16,0},{18,2},{36,4},{38,6},{56,8},{58,10},{77,13}... | collective-permute-start | bytes 491528 | tf_op jit(solution)/shard_map/ppermute | solution.py:129
  35.0 8.1 %collective-permute-start.1 = (bf16[176,512]{1,0:T(8,128)(2,1)S(1)}, bf16[176,512]{1,0:T(8,128)(2,1)S(1)}, u32[]{:S(2)}, u32[]{:S(2)}) collective-permute-start(bf16[176,512]{1,0:T(8,128)(2,1)S(1)} %collective-permute-done), channel_id=1, source_target_pairs={{0,0},{2,2},{20,4},{22,6},{40,8},{42,10},{60,12},{62,14},{65,1},{6... | collective-permute-start | bytes 540680 | tf_op jit(solution)/shard_map/ppermute | solution.py:129
  43.1 1.9 %collective-permute-start.3 = (bf16[176,512]{1,0:T(8,128)(2,1)S(1)}, bf16[176,512]{1,0:T(8,128)(2,1)S(1)}, u32[]{:S(2)}, u32[]{:S(2)}) collective-permute-start(bf16[176,512]{1,0:T(8,128)(2,1)S(1)} %collective-permute-done.2), channel_id=1, source_target_pairs={{4,4},{6,6},{24,8},{26,10},{44,12},{46,14},{48,0},{50,2},{69,5},{7... | collective-permute-start | bytes 540680 | tf_op jit(solution)/shard_map/ppermute | solution.py:129
  45.0 1.9 %collective-permute-start.5 = (bf16[176,512]{1,0:T(8,128)(2,1)S(1)}, bf16[176,512]{1,0:T(8,128)(2,1)S(1)}, u32[]{:S(2)}, u32[]{:S(2)}) collective-permute-start(bf16[176,512]{1,0:T(8,128)(2,1)S(1)} %collective-permute-done.4), channel_id=1, source_target_pairs={{8,8},{10,10},{28,12},{30,14},{32,0},{34,2},{52,4},{54,6},{73,9},{... | collective-permute-start | bytes 540680 | tf_op jit(solution)/shard_map/ppermute | solution.py:129
  48.8 8.0 %collective-permute-done.3 = bf16[176,512]{1,0:T(8,128)(2,1)S(1)} collective-permute-done((bf16[176,512]{1,0:T(8,128)(2,1)S(1)}, bf16[176,512]{1,0:T(8,128)(2,1)S(1)}, u32[]{:S(2)}, u32[]{:S(2)}) %collective-permute-start.3) | collective-permute-done | bytes 180256 | tf_op jit(solution)/shard_map/ppermute | solution.py:129
  61.3 16.3 %collective-permute-done.8 = bf16[688,512]{1,0:T(8,128)(2,1)S(1)} collective-permute-done((bf16[688,512]{1,0:T(8,128)(2,1)S(1)}, bf16[688,512]{1,0:T(8,128)(2,1)S(1)}, u32[]{:S(2)}, u32[]{:S(2)}) %collective-permute-start.8) | collective-permute-done | bytes 704544 | tf_op jit(solution)/shard_map/ppermute | solution.py:140
  77.9 2.5 %collective-permute-start.11 = (bf16[688,512]{1,0:T(8,128)(2,1)S(1)}, bf16[688,512]{1,0:T(8,128)(2,1)S(1)}, u32[]{:S(2)}, u32[]{:S(2)}) collective-permute-start(bf16[688,512]{1,0:T(8,128)(2,1)S(1)} %collective-permute-done.9), channel_id=1, source_target_pairs={{0,112},{16,0},{32,16},{48,32},{64,48},{80,64},{96,80},{112,96},{1... | collective-permute-start | bytes 2113544 | tf_op jit(solution)/shard_map/ppermute | solution.py:140
  80.3 2.9 %broadcast_in_dim.34 = bf16[8,688,512]{2,1,0:T(8,128)(2,1)} broadcast(bf16[688,512]{1,0:T(8,128)(2,1)S(1)} %fusion.6), dimensions={1,2} | broadcast | bytes 6340608 | tf_op jit(solution)/shard_map/broadcast_in_dim | solution.py:137
  84.1 11.7 %collective-permute-done.10 = bf16[688,512]{1,0:T(8,128)(2,1)S(1)} collective-permute-done((bf16[688,512]{1,0:T(8,128)(2,1)S(1)}, bf16[688,512]{1,0:T(8,128)(2,1)S(1)}, u32[]{:S(2)}, u32[]{:S(2)}) %collective-permute-start.10) | collective-permute-done | bytes 704544 | tf_op jit(solution)/shard_map/ppermute | solution.py:140
  95.8 2.7 %collective-permute-start.13 = (bf16[688,512]{1,0:T(8,128)(2,1)S(1)}, bf16[688,512]{1,0:T(8,128)(2,1)S(1)}, u32[]{:S(2)}, u32[]{:S(2)}) collective-permute-start(bf16[688,512]{1,0:T(8,128)(2,1)S(1)} %collective-permute-done.11), channel_id=1, source_target_pairs={{0,112},{16,0},{32,16},{48,32},{64,48},{80,64},{96,80},{112,96},{1... | collective-permute-start | bytes 2113544 | tf_op jit(solution)/shard_map/ppermute | solution.py:140
  101.3 11.8 %collective-permute-done.12 = bf16[688,512]{1,0:T(8,128)(2,1)S(1)} collective-permute-done((bf16[688,512]{1,0:T(8,128)(2,1)S(1)}, bf16[688,512]{1,0:T(8,128)(2,1)S(1)}, u32[]{:S(2)}, u32[]{:S(2)}) %collective-permute-start.12) | collective-permute-done | bytes 704544 | tf_op jit(solution)/shard_map/ppermute | solution.py:140
  113.2 2.9 %collective-permute-start.15 = (bf16[336,512]{1,0:T(8,128)(2,1)S(1)}, bf16[336,512]{1,0:T(8,128)(2,1)S(1)}, u32[]{:S(2)}, u32[]{:S(2)}) collective-permute-start(bf16[336,512]{1,0:T(8,128)(2,1)S(1)} %slice.45), channel_id=1, source_target_pairs={{0,112},{16,0},{32,16},{48,32},{64,48},{80,64},{96,80},{112,96},{1... | collective-permute-start | bytes 1032200 | tf_op jit(solution)/shard_map/ppermute | solution.py:143
  118.0 4.2 %collective-permute-done.14 = bf16[352,512]{1,0:T(8,128)(2,1)S(1)} collective-permute-done((bf16[352,512]{1,0:T(8,128)(2,1)S(1)}, bf16[352,512]{1,0:T(8,128)(2,1)S(1)}, u32[]{:S(2)}, u32[]{:S(2)}) %collective-permute-start.14) | collective-permute-done | bytes 360480 | tf_op jit(solution)/shard_map/ppermute | solution.py:142
  123.7 3.4 %all-gather.3.cloned.1.call-done = bf16[11008,512]{1,0:T(8,128)(2,1)} async-done(((bf16[688,512]{1,0:T(8,128)(2,1)}), bf16[11008,512]{1,0:T(8,128)(2,1)}) %all-gather.3.cloned.1.call-update) | async-done | bytes 11272208 | tf_op jit(solution)/shard_map/all_gather | solution.py:135
  127.1 6.3 %shard_map.38 = bf16[336,688]{1,0:T(8,128)(2,1)} custom-call(bf16[4,2,2,688,512]{4,3,2,1,0:T(8,128)(2,1)} %bitcast.68, bf16[4,2,2,688,512]{4,3,2,1,0:T(8,128)(2,1)} %bitcast.69, bf16[8,688,512]{2,1,0:T(8,128)(2,1)} %bitcast_dynamic-update-slice_fusion.7.columns_ref), custom_call_target="tpu_custom_call" | custom-call | flops 1893728256 | bytes 12582912 | tf_op jit(solution)/shard_map/pallas_call | solution.py:83
  133.4 2.6 %collective-permute-start.16 = (bf16[21,16,688]{2,1,0:T(8,128)(2,1)}, bf16[21,16,688]{2,1,0:T(8,128)(2,1)S(1)}, u32[]{:S(2)}, u32[]{:S(2)}) collective-permute-start(bf16[21,16,688]{2,1,0:T(8,128)(2,1)} %bitcast.79), channel_id=1, source_target_pairs={{0,128},{16,144},{32,160},{48,176},{64,192},{80,208},{96,224},{112... | collective-permute-start | bytes 1387016 | tf_op jit(solution)/shard_map/ppermute | solution.py:150
  136.0 6.4 %shard_map.40 = bf16[352,688]{1,0:T(8,128)(2,1)} custom-call(bf16[4,2,2,688,512]{4,3,2,1,0:T(8,128)(2,1)} %bitcast.70, bf16[4,2,2,688,512]{4,3,2,1,0:T(8,128)(2,1)} %bitcast.71, bf16[8,688,512]{2,1,0:T(8,128)(2,1)} %bitcast_dynamic-update-slice_fusion.7.columns_ref), custom_call_target="tpu_custom_call" | custom-call | flops 1983905792 | bytes 12582912 | tf_op jit(solution)/shard_map/pallas_call | solution.py:83
  142.8 6.5 %shard_map.37 = f32[336,688]{1,0:T(8,128)} custom-call(bf16[4,2,2,688,512]{4,3,2,1,0:T(8,128)(2,1)} %bitcast.72, bf16[4,2,2,688,512]{4,3,2,1,0:T(8,128)(2,1)} %bitcast.73, bf16[8,688,512]{2,1,0:T(8,128)(2,1)} %bitcast_dynamic-update-slice_fusion.7.columns_ref), custom_call_target="tpu_custom_call" | custom-call | flops 1893728256 | bytes 12582912 | tf_op jit(solution)/shard_map/pallas_call | solution.py:83
  149.3 6.6 %shard_map.39 = f32[352,688]{1,0:T(8,128)} custom-call(bf16[4,2,2,688,512]{4,3,2,1,0:T(8,128)(2,1)} %bitcast.74, bf16[4,2,2,688,512]{4,3,2,1,0:T(8,128)(2,1)} %bitcast.75, bf16[8,688,512]{2,1,0:T(8,128)(2,1)} %bitcast_dynamic-update-slice_fusion.7.columns_ref), custom_call_target="tpu_custom_call" | custom-call | flops 1983905792 | bytes 12582912 | tf_op jit(solution)/shard_map/pallas_call | solution.py:83
  157.3 2.6 %collective-permute-done.17 = bf16[22,16,688]{2,1,0:T(8,128)(2,1)S(1)} collective-permute-done((bf16[22,16,688]{2,1,0:T(8,128)(2,1)}, bf16[22,16,688]{2,1,0:T(8,128)(2,1)S(1)}, u32[]{:S(2)}, u32[]{:S(2)}) %collective-permute-start.17) | collective-permute-done | bytes 484384 | tf_op jit(solution)/shard_map/ppermute | solution.py:150
  (52 shorter events, 19.9 us)
Async XLA Ops:
  6.5 1.6 copy-start
  6.5 12.9 %copy-start.5 = (bf16[512,688]{0,1:T(8,128)(2,1)S(1)}, bf16[512,688]{0,1:T(8,128)(2,1)}, u32[]{:S(2)}) copy-start(bf16[512,688]{0,1:T(8,128)(2,1)} %param.5) | copy-start | bytes 2113540
  6.5 120.6 %all-gather.3.cloned.1.call-start = ((), (), s32[]{:S(2)}) async-start(), calls=%async_computation | async-start | bytes 11976704 | tf_op jit(solution)/shard_map/all_gather | solution.py:135
  8.1 11.3 %copy-start.4 = (bf16[688,2048]{1,0:T(8,128)(2,1)S(1)}, bf16[688,2048]{1,0:T(8,128)(2,1)}, u32[]{:S(2)}) copy-start(bf16[688,2048]{1,0:T(8,128)(2,1)} %param.4) | copy-start | bytes 8454148
  10.7 24.2 %collective-permute-start = (bf16[176,512]{1,0:T(8,128)(2,1)S(1)}, bf16[176,512]{1,0:T(8,128)(2,1)S(1)}, u32[]{:S(2)}, u32[]{:S(2)}) collective-permute-start(bf16[176,512]{1,0:T(8,128)(2,1)S(1)} %get-tuple-element.9), channel_id=1, source_target_pairs={{0,0},{1,5},{2,9},{3,13},{4,1},{5,12},{6,8},{7,4},{8,2},{9,7},{10,... | collective-permute-start | bytes 540680 | tf_op jit(solution)/shard_map/ppermute | solution.py:130
  14.7 28.4 %collective-permute-start.2 = (bf16[176,512]{1,0:T(8,128)(2,1)S(1)}, bf16[176,512]{1,0:T(8,128)(2,1)S(1)}, u32[]{:S(2)}, u32[]{:S(2)}) collective-permute-start(bf16[176,512]{1,0:T(8,128)(2,1)S(1)} %get-tuple-element.10), channel_id=1, source_target_pairs={{0,4},{1,9},{2,13},{3,1},{4,5},{5,0},{6,12},{7,8},{8,6},{9,11},{10... | collective-permute-start | bytes 540680 | tf_op jit(solution)/shard_map/ppermute | solution.py:130
  20.4 24.6 %collective-permute-start.4 = (bf16[176,512]{1,0:T(8,128)(2,1)S(1)}, bf16[176,512]{1,0:T(8,128)(2,1)S(1)}, u32[]{:S(2)}, u32[]{:S(2)}) collective-permute-start(bf16[176,512]{1,0:T(8,128)(2,1)S(1)} %slice.42), channel_id=1, source_target_pairs={{0,8},{1,13},{2,1},{3,5},{4,9},{5,4},{6,0},{7,12},{8,10},{9,15},{1... | collective-permute-start | bytes 540680 | tf_op jit(solution)/shard_map/ppermute | solution.py:130
  24.9 0.7 collective-permute-start.6
  25.6 23.2 %collective-permute-start.7 = (bf16[160,512]{1,0:T(8,128)(2,1)S(1)}, bf16[160,512]{1,0:T(8,128)(2,1)S(1)}, u32[]{:S(2)}, u32[]{:S(2)}) collective-permute-start(bf16[160,512]{1,0:T(8,128)(2,1)S(1)} %collective-permute-done.6), channel_id=1, source_target_pairs={{12,12},{14,14},{16,0},{18,2},{36,4},{38,6},{56,8},{58,10},{77,13}... | collective-permute-start | bytes 491528 | tf_op jit(solution)/shard_map/ppermute | solution.py:129
  35.0 13.8 %collective-permute-start.1 = (bf16[176,512]{1,0:T(8,128)(2,1)S(1)}, bf16[176,512]{1,0:T(8,128)(2,1)S(1)}, u32[]{:S(2)}, u32[]{:S(2)}) collective-permute-start(bf16[176,512]{1,0:T(8,128)(2,1)S(1)} %collective-permute-done), channel_id=1, source_target_pairs={{0,0},{2,2},{20,4},{22,6},{40,8},{42,10},{60,12},{62,14},{65,1},{6... | collective-permute-start | bytes 540680 | tf_op jit(solution)/shard_map/ppermute | solution.py:129
  43.1 13.7 %collective-permute-start.3 = (bf16[176,512]{1,0:T(8,128)(2,1)S(1)}, bf16[176,512]{1,0:T(8,128)(2,1)S(1)}, u32[]{:S(2)}, u32[]{:S(2)}) collective-permute-start(bf16[176,512]{1,0:T(8,128)(2,1)S(1)} %collective-permute-done.2), channel_id=1, source_target_pairs={{4,4},{6,6},{24,8},{26,10},{44,12},{46,14},{48,0},{50,2},{69,5},{7... | collective-permute-start | bytes 540680 | tf_op jit(solution)/shard_map/ppermute | solution.py:129
  45.0 12.6 %collective-permute-start.5 = (bf16[176,512]{1,0:T(8,128)(2,1)S(1)}, bf16[176,512]{1,0:T(8,128)(2,1)S(1)}, u32[]{:S(2)}, u32[]{:S(2)}) collective-permute-start(bf16[176,512]{1,0:T(8,128)(2,1)S(1)} %collective-permute-done.4), channel_id=1, source_target_pairs={{8,8},{10,10},{28,12},{30,14},{32,0},{34,2},{52,4},{54,6},{73,9},{... | collective-permute-start | bytes 540680 | tf_op jit(solution)/shard_map/ppermute | solution.py:129
  58.6 19.1 %collective-permute-start.8 = (bf16[688,512]{1,0:T(8,128)(2,1)S(1)}, bf16[688,512]{1,0:T(8,128)(2,1)S(1)}, u32[]{:S(2)}, u32[]{:S(2)}) collective-permute-start(bf16[688,512]{1,0:T(8,128)(2,1)S(1)} %fusion.6), channel_id=1, source_target_pairs={{0,16},{16,32},{32,48},{48,64},{64,80},{80,96},{96,112},{112,0},{1... | collective-permute-start | bytes 2113544 | tf_op jit(solution)/shard_map/ppermute | solution.py:140
  60.1 17.8 %collective-permute-start.9 = (bf16[688,512]{1,0:T(8,128)(2,1)S(1)}, bf16[688,512]{1,0:T(8,128)(2,1)S(1)}, u32[]{:S(2)}, u32[]{:S(2)}) collective-permute-start(bf16[688,512]{1,0:T(8,128)(2,1)S(1)} %fusion.6), channel_id=1, source_target_pairs={{0,112},{16,0},{32,16},{48,32},{64,48},{80,64},{96,80},{112,96},{1... | collective-permute-start | bytes 2113544 | tf_op jit(solution)/shard_map/ppermute | solution.py:140
  77.6 18.2 %collective-permute-start.10 = (bf16[688,512]{1,0:T(8,128)(2,1)S(1)}, bf16[688,512]{1,0:T(8,128)(2,1)S(1)}, u32[]{:S(2)}, u32[]{:S(2)}) collective-permute-start(bf16[688,512]{1,0:T(8,128)(2,1)S(1)} %collective-permute-done.8), channel_id=1, source_target_pairs={{0,16},{16,32},{32,48},{48,64},{64,80},{80,96},{96,112},{112,0},{1... | collective-permute-start | bytes 2113544 | tf_op jit(solution)/shard_map/ppermute | solution.py:140
  77.9 18.0 %collective-permute-start.11 = (bf16[688,512]{1,0:T(8,128)(2,1)S(1)}, bf16[688,512]{1,0:T(8,128)(2,1)S(1)}, u32[]{:S(2)}, u32[]{:S(2)}) collective-permute-start(bf16[688,512]{1,0:T(8,128)(2,1)S(1)} %collective-permute-done.9), channel_id=1, source_target_pairs={{0,112},{16,0},{32,16},{48,32},{64,48},{80,64},{96,80},{112,96},{1... | collective-permute-start | bytes 2113544 | tf_op jit(solution)/shard_map/ppermute | solution.py:140
  95.8 17.3 %collective-permute-start.12 = (bf16[688,512]{1,0:T(8,128)(2,1)S(1)}, bf16[688,512]{1,0:T(8,128)(2,1)S(1)}, u32[]{:S(2)}, u32[]{:S(2)}) collective-permute-start(bf16[688,512]{1,0:T(8,128)(2,1)S(1)} %collective-permute-done.10), channel_id=1, source_target_pairs={{0,16},{16,32},{32,48},{48,64},{64,80},{80,96},{96,112},{112,0},{1... | collective-permute-start | bytes 2113544 | tf_op jit(solution)/shard_map/ppermute | solution.py:140
  95.8 17.4 %collective-permute-start.13 = (bf16[688,512]{1,0:T(8,128)(2,1)S(1)}, bf16[688,512]{1,0:T(8,128)(2,1)S(1)}, u32[]{:S(2)}, u32[]{:S(2)}) collective-permute-start(bf16[688,512]{1,0:T(8,128)(2,1)S(1)} %collective-permute-done.11), channel_id=1, source_target_pairs={{0,112},{16,0},{32,16},{48,32},{64,48},{80,64},{96,80},{112,96},{1... | collective-permute-start | bytes 2113544 | tf_op jit(solution)/shard_map/ppermute | solution.py:140
  113.1 9.0 %collective-permute-start.14 = (bf16[352,512]{1,0:T(8,128)(2,1)S(1)}, bf16[352,512]{1,0:T(8,128)(2,1)S(1)}, u32[]{:S(2)}, u32[]{:S(2)}) collective-permute-start(bf16[352,512]{1,0:T(8,128)(2,1)S(1)} %slice.44), channel_id=1, source_target_pairs={{0,16},{16,32},{32,48},{48,64},{64,80},{80,96},{96,112},{112,0},{1... | collective-permute-start | bytes 1081352 | tf_op jit(solution)/shard_map/ppermute | solution.py:142
  113.2 9.7 %collective-permute-start.15 = (bf16[336,512]{1,0:T(8,128)(2,1)S(1)}, bf16[336,512]{1,0:T(8,128)(2,1)S(1)}, u32[]{:S(2)}, u32[]{:S(2)}) collective-permute-start(bf16[336,512]{1,0:T(8,128)(2,1)S(1)} %slice.45), channel_id=1, source_target_pairs={{0,112},{16,0},{32,16},{48,32},{64,48},{80,64},{96,80},{112,96},{1... | collective-permute-start | bytes 1032200 | tf_op jit(solution)/shard_map/ppermute | solution.py:143
  133.4 22.5 %collective-permute-start.16 = (bf16[21,16,688]{2,1,0:T(8,128)(2,1)}, bf16[21,16,688]{2,1,0:T(8,128)(2,1)S(1)}, u32[]{:S(2)}, u32[]{:S(2)}) collective-permute-start(bf16[21,16,688]{2,1,0:T(8,128)(2,1)} %bitcast.79), channel_id=1, source_target_pairs={{0,128},{16,144},{32,160},{48,176},{64,192},{80,208},{96,224},{112... | collective-permute-start | bytes 1387016 | tf_op jit(solution)/shard_map/ppermute | solution.py:150
  142.5 17.4 %collective-permute-start.17 = (bf16[22,16,688]{2,1,0:T(8,128)(2,1)}, bf16[22,16,688]{2,1,0:T(8,128)(2,1)S(1)}, u32[]{:S(2)}, u32[]{:S(2)}) collective-permute-start(bf16[22,16,688]{2,1,0:T(8,128)(2,1)} %bitcast.77), channel_id=1, source_target_pairs={{0,128},{16,144},{32,160},{48,176},{64,192},{80,208},{96,224},{112... | collective-permute-start | bytes 1453064 | tf_op jit(solution)/shard_map/ppermute | solution.py:150
  155.9 3.9 %copy-start.1 = (f32[352,688]{1,0:T(8,128)S(1)}, f32[352,688]{1,0:T(8,128)}, u32[]{:S(2)}) copy-start(f32[352,688]{1,0:T(8,128)} %shard_map.39) | copy-start | bytes 2906116
  157.3 2.6 %copy-start.3 = (f32[688,688]{1,0:T(8,128)}, f32[688,688]{1,0:T(8,128)S(1)}, u32[]{:S(2)}) copy-start(f32[688,688]{1,0:T(8,128)S(1)} %fusion.36) | copy-start | bytes 5680132
  (1 other events, 1.2 us)
Sparse Core Ops, SparseCore 0:
  58.7 68.3 all-gather.2
